TPU v7x, 32 devices: a whole 2x2x4 slice. The times are simulated.
32 devices in a mesh: ctx: 8 (over z, x), fsdp: 4 (over y, core).
Axes of the slice: x: 2, y: 2, z: 4, core: 2. Of those that a mesh axis runs over, the one named last changes fastest.
Arguments:
- queries: bfloat16 [1024, 2048], P('ctx', 'fsdp'), may hold values from -120 to 120
- keys: bfloat16 [1024, 256], P('ctx'), may hold values from -5 to 5
- values: bfloat16 [1024, 256], P('ctx'), may hold values from -5 to 5
- out_grad: bfloat16 [1024, 2048], P('ctx', 'fsdp'), may hold values from -5 to 5
- hidden: bfloat16 [1024, 8192], P('ctx', 'fsdp'), may hold values from -40 to 40
- key_weight: bfloat16 [8192, 256], P('fsdp'), may hold values from -10 to 10
- value_weight: bfloat16 [8192, 256], P('fsdp'), may hold values from -10 to 10
- stretch_owner: int32 [8], replicated, may hold values from 0 to 7, as said below
- positions: int32 [1024], P('ctx'), may hold values from 0 to 511, as said below
Outputs:
- query_grad: bfloat16 [1024, 2048], P('ctx', 'fsdp')
- key_weight_grad: float32 [8192, 256], P('fsdp')
- value_weight_grad: float32 [8192, 256], P('fsdp')
Inputs may be any that keep to these rules, and one draw needn't show every extreme that they name: A permutation; index b of ctx holds sequence stretch stretch_owner[b] in its first 64 rows and stretch 2 * 8 - 1 - stretch_owner[b] in the others. `positions`: documents are contiguous in sequence order; a row's position counts from its document's first token, and the sequence's first token has position 0.
All inputs are finite; a program needn't handle non-finite values.
Results may differ from a plain program's by a relative error of at most 0.015.
Values may be sent and summed in bfloat16 or wider, within the bound.
No kernel may reach another device: no remote copies, remote signals or barrier semaphores. Data moves between devices by JAX's collectives and lax.ppermute only.
A program may use at most 64 MiB of HBM per device.

v0:
```python
import math

import jax
import jax.numpy as jnp
from jax import lax
from jax.sharding import PartitionSpec as P

DH = 128
HPG = 8
KVG = 2


CLIP_RATE = 0.02
EPSILON = 1e-06
NEGATIVE = -1e30


def rows_by_head(block, heads, width):
    count = block.shape[0]
    return block.reshape(count, heads, width).transpose(1, 0, 2).reshape(heads * count, width)


def local(
    queries, keys, values, out_grad, hidden, key_weight, value_weight, stretch_owner, positions
):
    tok_dev = queries.shape[0]
    heads = queries.shape[1] // DH
    ctx_count = lax.axis_size("ctx")
    total = tok_dev * ctx_count
    half = tok_dev // 2
    ctx_index = lax.axis_index("ctx")
    group = lax.axis_index("fsdp") * heads // HPG
    scale = 1.0 / math.sqrt(DH)
    block = min(512, total)
    blocks = total // block
    query_count = heads * tok_dev
    own_keys = lax.dynamic_slice_in_dim(keys, group * DH, DH, 1)
    own_values = lax.dynamic_slice_in_dim(values, group * DH, DH, 1)
    all_keys, all_values = (
        lax.all_gather(own_keys, "ctx", axis=0, tiled=True),
        lax.all_gather(own_values, "ctx", axis=0, tiled=True),
    )
    offsets = jnp.arange(half, dtype=jnp.int32)
    stretches = jnp.stack([stretch_owner, 2 * ctx_count - 1 - stretch_owner], axis=1)
    key_place = (stretches[:, :, None] * half + offsets[None, None, :]).reshape(total)
    mine = lax.dynamic_slice_in_dim(stretches, ctx_index, 1, 0)[0]
    local_place = (mine[:, None] * half + offsets[None, :]).reshape(tok_dev)
    query_place = jnp.tile(local_place, heads)
    query_floor = jnp.tile(local_place - positions, heads)
    query_rows = rows_by_head(queries, heads, DH)
    grad_rows = rows_by_head(out_grad, heads, DH)
    contract_last = (((1,), (1,)), ((), ()))
    contract_first = (((0,), (0,)), ((), ()))

    def scores_at(start, width):
        key_block = lax.dynamic_slice_in_dim(all_keys, start, width, 0)
        place = lax.dynamic_slice_in_dim(key_place, start, width, 0)
        raw = (
            lax.dot_general(
                query_rows, key_block, contract_last, preferred_element_type=jnp.float32
            )
            * scale
        )
        seen = (place[None, :] <= query_place[:, None]) & (place[None, :] >= query_floor[:, None])
        return (jnp.where(seen, raw, NEGATIVE), seen, key_block)

    def stats_step(step, carry):
        top, mass = carry
        masked, seen, key_block = scores_at(step * block, block)
        new_top = jnp.maximum(top, jnp.max(masked, axis=1))
        weights = jnp.where(seen, jnp.exp(masked - new_top[:, None]), 0.0)
        mass = mass * jnp.exp(top - new_top) + jnp.sum(weights, axis=1)
        return (new_top, mass)

    start_top = jnp.full((query_count,), NEGATIVE, jnp.float32)
    start_mass = jnp.zeros((query_count,), jnp.float32)
    top, mass = lax.fori_loop(0, blocks, stats_step, (start_top, start_mass))
    lse = top + jnp.log(mass)

    def probs_at(start, width):
        masked, seen, key_block = scores_at(start, width)
        probs = jnp.where(seen, jnp.exp(masked - lse[:, None]), 0.0)
        value_block = lax.dynamic_slice_in_dim(all_values, start, width, 0)
        dprobs = lax.dot_general(
            grad_rows, value_block, contract_last, preferred_element_type=jnp.float32
        )
        return (probs, dprobs, key_block)

    def delta_step(step, acc):
        probs, dprobs, key_block = probs_at(step * block, block)
        return acc + jnp.sum(probs * dprobs, axis=1)

    delta = lax.fori_loop(0, blocks, delta_step, jnp.zeros((query_count,), jnp.float32))

    def slopes_at(start, width):
        probs, dprobs, key_block = probs_at(start, width)
        slopes = (probs * (dprobs - delta[:, None]) * scale).astype(jnp.bfloat16)
        return (probs.astype(jnp.bfloat16), slopes, key_block)

    def key_terms(probs_b, slopes):
        key_part = lax.dot_general(
            slopes, query_rows, contract_first, preferred_element_type=jnp.float32
        )
        value_part = lax.dot_general(
            probs_b, grad_rows, contract_first, preferred_element_type=jnp.float32
        )
        return jnp.concatenate([key_part, value_part], axis=1)

    start_query = jnp.zeros((query_count, DH), jnp.float32)

    def query_step(step, query_acc):
        probs_b, slopes, key_block = slopes_at(step * block, block)
        return query_acc + jnp.dot(slopes, key_block, preferred_element_type=jnp.float32)

    query_acc = lax.fori_loop(0, blocks, query_step, start_query)
    width = math.gcd(tok_dev * lax.axis_size("ctx"), block)

    def inner(step, acc):
        offset = step * width
        probs_b, slopes, key_block = slopes_at(offset, width)
        return lax.dynamic_update_slice_in_dim(acc, key_terms(probs_b, slopes), offset, 0)

    own_grads = lax.psum_scatter(
        lax.fori_loop(
            0,
            tok_dev * lax.axis_size("ctx") // width,
            inner,
            jnp.zeros((tok_dev * lax.axis_size("ctx"), 2 * DH), jnp.float32),
        ),
        "ctx",
        scatter_dimension=0,
        tiled=True,
    )
    query_grad = (
        query_acc.reshape(heads, tok_dev, DH)
        .transpose(1, 0, 2)
        .reshape(tok_dev, heads * DH)
        .astype(jnp.bfloat16)
    )
    members = lax.all_gather(own_grads.astype(jnp.bfloat16), "fsdp", axis=0, tiled=True).astype(
        own_grads.dtype
    )
    per_group = members.reshape(KVG, -1, tok_dev, 2 * DH).sum(axis=1)
    key_grads = (
        per_group[:, :, :DH].transpose(1, 0, 2).reshape(tok_dev, KVG * DH).astype(jnp.bfloat16)
    )
    value_grads = (
        per_group[:, :, DH:].transpose(1, 0, 2).reshape(tok_dev, KVG * DH).astype(jnp.bfloat16)
    )
    both_grads = jnp.concatenate([key_grads, value_grads], axis=1)
    columns = KVG * DH
    raw = lax.psum(
        lax.dot_general(hidden, both_grads, contract_first, preferred_element_type=jnp.float32),
        "ctx",
    )
    key_f = key_weight.astype(jnp.float32)
    value_f = value_weight.astype(jnp.float32)
    grad_sq, key_sq, value_sq = lax.psum(
        (
            jnp.sum(raw * raw, axis=0),
            jnp.sum(key_f * key_f, axis=0),
            jnp.sum(value_f * value_f, axis=0),
        ),
        "fsdp",
    )
    weight_norm = jnp.sqrt(jnp.concatenate([key_sq, value_sq]) + EPSILON)
    grad_norm = jnp.sqrt(grad_sq + EPSILON)
    clipped = raw * jnp.minimum(1.0, CLIP_RATE * total * weight_norm / grad_norm)[None, :]
    return (query_grad, clipped[:, :columns], clipped[:, columns:])


def solution(mesh):
    return jax.shard_map(
        local,
        mesh=mesh,
        in_specs=(
            P("ctx", "fsdp"),
            P("ctx", None),
            P("ctx", None),
            P("ctx", "fsdp"),
            P("ctx", "fsdp"),
            P("fsdp", None),
            P("fsdp", None),
            P(),
            P("ctx"),
        ),
        out_specs=(P("ctx", "fsdp"), P("fsdp", None), P("fsdp", None)),
        check_vma=False,
    )
```

profile of v0, /device:TPU:0, one launch (start us, length us, event | category | flops | bytes accessed | tf_op | source)
XLA Modules:
  0.0 340.1 jit_solution(14859050243077654224)
XLA Ops:
  8.9 0.8 constant_dynamic-slice_fusion.1
  9.6 32.5 %all_gather.9 = bf16[1024,128]{1,0:T(8,128)(2,1)S(1)} all-gather(bf16[128,128]{1,0:T(8,128)(2,1)S(1)} %constant_dynamic-slice_fusion.1), channel_id=1, replica_groups=mesh['ctx'=8,'fsdp'=4] {'ctx'}, dimensions={0}, use_global_device_ids=true | all-gather | bytes 294912 | tf_op jit(solution)/shard_map/all_gather | solution.py:40
  42.2 0.9 copy_bitcast_fusion.2
  44.1 1.7 while.59
  45.8 30.7 %all_gather.10 = bf16[1024,128]{1,0:T(8,128)(2,1)S(1)} all-gather(bf16[128,128]{1,0:T(8,128)(2,1)S(1)} %constant_dynamic-slice_fusion), channel_id=1, replica_groups=mesh['ctx'=8,'fsdp'=4] {'ctx'}, dimensions={0}, use_global_device_ids=true | all-gather | bytes 294912 | tf_op jit(solution)/shard_map/all_gather | solution.py:41
  76.6 1.8 while.60
  78.4 1.1 broadcast_in_dim.106
  79.5 4.4 %while.58 = (s32[]{:T(128)}, f32[1024,256]{0,1:T(8,128)}, s32[1024]{0:T(1024)S(1)}, bf16[1024,128]{1,0:T(8,128)(2,1)S(1)}, bf16[512,128]{1,0:T(8,128)(2,1)S(1)},...) while((s32[]{:T(128)}, f32[1024,256]{0,1:T(8,128)}, ...), condition=%wide.region_10.11_spmd.clone, body=%wide.region_9.10_spmd.clone.sunk | while | flops 271712256 | bytes 5524691 | solution.py:124
  80.9 0.8 maximum_dynamic-update-slice_fusion.2
  83.1 0.8 maximum_dynamic-update-slice_fusion.2
  84.1 64.9 %reduce-scatter.2.cloned.1.call-done = f32[128,256]{0,1:T(8,128)} async-done(((f32[1024,256]{0,1:T(8,128)}), f32[128,256]{0,1:T(8,128)}) %reduce-scatter.2.cloned.1.call-update) | async-done | bytes 131088 | tf_op jit(solution)/shard_map/reduce_scatter | solution.py:123
  148.9 0.9 convert_element_type.61
  149.8 5.8 %all_gather.11 = bf16[512,256]{0,1:T(8,128)(2,1)S(1)} all-gather(bf16[128,256]{0,1:T(8,128)(2,1)S(1)} %convert_element_type.61), channel_id=1, replica_groups=mesh['ctx'=8,'fsdp'=4] {'fsdp'}, dimensions={0}, use_global_device_ids=true | all-gather | bytes 327680 | tf_op jit(solution)/shard_map/all_gather | solution.py:140
  155.7 0.8 reduce
  156.7 2.7 convolution_bitcast_fusion.1
  159.4 2.4 while.61
  162.6 2.2 multiply_reduce_fusion.1
  164.9 150.1 %all-reduce.3.cloned.1.call-done = f32[2048,512]{0,1:T(8,128)} async-done(((f32[2048,512]{0,1:T(8,128)}), f32[2048,512]{0,1:T(8,128)}) %all-reduce.3.cloned.1.call-update) | async-done | bytes 4194320 | tf_op jit(solution)/shard_map/psum | solution.py:152
  314.9 2.5 multiply_reduce_fusion
  317.5 6.8 %all-reduce = (f32[256]{0:T(256)S(1)}, f32[256]{0:T(256)S(1)}, f32[512]{0:T(512)S(1)}) all-reduce(f32[256]{0:T(256)S(1)} %get-tuple-element.934, f32[256]{0:T(256)S(1)} %get-tuple-element.935, f32[512]{0:T(512)S(1)} %multiply_reduce_fusion), channel_id=1, replica_groups=mesh['ctx'=8,'fsdp'=4] {'fsdp'}, use_global_device_ids=true, to_apply=%region_17.18 | all-reduce | flops 1024 | bytes 8192 | tf_op jit(solution)/shard_map/psum | solution.py:158
  324.3 2.5 broadcast_multiply_fusion
  326.8 1.7 fusion.83
  328.6 2.9 copy.38
  331.4 1.8 copy.39
  (76 shorter events, 12.2 us)
Async XLA Ops:
  7.2 149.5 %copy-start = (bf16[128,2048]{1,0:T(8,128)(2,1)S(1)}, bf16[128,2048]{1,0:T(8,128)(2,1)}, u32[]{:S(2)}) copy-start(bf16[128,2048]{1,0:T(8,128)(2,1)} %param.21) | copy-start | bytes 1572868
  7.2 141.8 %reduce-scatter.2.cloned.1.call-start = ((), (), s32[]{:S(2)}) async-start(), calls=%async_computation.1 | async-start | bytes 1179648 | tf_op jit(solution)/shard_map/reduce_scatter | solution.py:123
  44.1 1.7 copy-start.2
  44.1 32.5 %copy-start.1 = (bf16[128,512]{1,0:T(8,128)(2,1)S(1)}, bf16[128,512]{1,0:T(8,128)(2,1)}, u32[]{:S(2)}) copy-start(bf16[128,512]{1,0:T(8,128)(2,1)} %param.20) | copy-start | bytes 393220
  84.0 230.9 %all-reduce.3.cloned.1.call-start = ((), (), s32[]{:S(2)}) async-start(), calls=%async_computation.2 | async-start | bytes 8388608 | tf_op jit(solution)/shard_map/psum | solution.py:152
Sparse Core Ops, SparseCore 0:
  84.1 64.7 reduce-scatter.1
  159.5 155.3 all-reduce.2
where the time goes:
time: 341 us; the launch traced here: 340 us
  waiting for transfers between devices  215 us (63%)
  blocking collectives  75.9 us (22%)
  between operations  14.2 us (4%)
  other arithmetic  13.8 us (4%)
  local copies, waits for them, and re-layouts  11.1 us (3%)
  matrix products  9.7 us (3%)
    psum x1, waiting for transfers between devices, local(): lax.psum(lax.dot_general(hidden, both_grads, contract_first, preferred_el...  150 us
    reduce_scatter x1, waiting for transfers between devices, local(): lax.psum_scatter(lax.fori_loop(0, tok_dev * lax.axis_size('ctx') // width...  64.9 us
    all_gather x1, blocking collectives, local(): lax.all_gather(own_keys, 'ctx', axis=0, tiled=True)  32.5 us
    all_gather x1, blocking collectives, local(): lax.all_gather(own_values, 'ctx', axis=0, tiled=True)  30.7 us
    psum x1, blocking collectives, local(): lax.psum((jnp.sum(raw * raw, axis=0), jnp.sum(key_f * key_f, axis=0), jnp...  6.84 us
  transfers between devices with their start and end apart: 2, of which 2 were waited for; matrix products, arithmetic and copies ran while one was open for 2% of the time, Pallas kernels for 0%

commit v1 on v0

--- a/solution.py
+++ b/solution.py
@@ -1,8 +1,11 @@
+import functools
 import math
 
 import jax
 import jax.numpy as jnp
 from jax import lax
+from jax.experimental import pallas as pl
+from jax.experimental.pallas import tpu as pltpu
 from jax.sharding import PartitionSpec as P
 
 DH = 128
@@ -13,6 +16,12 @@
 CLIP_RATE = 0.02
 EPSILON = 1e-06
 NEGATIVE = -1e30
+GATHER_LIMIT = 8 * 2**20
+
+CONTRACT_LAST = (((1,), (1,)), ((), ()))
+CONTRACT_FIRST = (((0,), (0,)), ((), ()))
+VMEM = pl.BlockSpec(memory_space=pltpu.VMEM)
+SMEM = pl.BlockSpec(memory_space=pltpu.SMEM)
 
 
 def rows_by_head(block, heads, width):
@@ -20,7 +29,7 @@
     return block.reshape(count, heads, width).transpose(1, 0, 2).reshape(heads * count, width)
 
 
-def local(
+def local_large(
     queries, keys, values, out_grad, hidden, key_weight, value_weight, stretch_owner, positions
 ):
     tok_dev = queries.shape[0]
@@ -49,15 +58,13 @@
     query_floor = jnp.tile(local_place - positions, heads)
     query_rows = rows_by_head(queries, heads, DH)
     grad_rows = rows_by_head(out_grad, heads, DH)
-    contract_last = (((1,), (1,)), ((), ()))
-    contract_first = (((0,), (0,)), ((), ()))
 
     def scores_at(start, width):
         key_block = lax.dynamic_slice_in_dim(all_keys, start, width, 0)
         place = lax.dynamic_slice_in_dim(key_place, start, width, 0)
         raw = (
             lax.dot_general(
-                query_rows, key_block, contract_last, preferred_element_type=jnp.float32
+                query_rows, key_block, CONTRACT_LAST, preferred_element_type=jnp.float32
             )
             * scale
         )
@@ -82,7 +89,7 @@
         probs = jnp.where(seen, jnp.exp(masked - lse[:, None]), 0.0)
         value_block = lax.dynamic_slice_in_dim(all_values, start, width, 0)
         dprobs = lax.dot_general(
-            grad_rows, value_block, contract_last, preferred_element_type=jnp.float32
+            grad_rows, value_block, CONTRACT_LAST, preferred_element_type=jnp.float32
         )
         return (probs, dprobs, key_block)
 
@@ -99,10 +106,10 @@
 
     def key_terms(probs_b, slopes):
         key_part = lax.dot_general(
-            slopes, query_rows, contract_first, preferred_element_type=jnp.float32
+            slopes, query_rows, CONTRACT_FIRST, preferred_element_type=jnp.float32
         )
         value_part = lax.dot_general(
-            probs_b, grad_rows, contract_first, preferred_element_type=jnp.float32
+            probs_b, grad_rows, CONTRACT_FIRST, preferred_element_type=jnp.float32
         )
         return jnp.concatenate([key_part, value_part], axis=1)
 
@@ -150,7 +157,7 @@
     both_grads = jnp.concatenate([key_grads, value_grads], axis=1)
     columns = KVG * DH
     raw = lax.psum(
-        lax.dot_general(hidden, both_grads, contract_first, preferred_element_type=jnp.float32),
+        lax.dot_general(hidden, both_grads, CONTRACT_FIRST, preferred_element_type=jnp.float32),
         "ctx",
     )
     key_f = key_weight.astype(jnp.float32)
@@ -169,21 +176,396 @@
     return (query_grad, clipped[:, :columns], clipped[:, columns:])
 
 
+SIDES = 2
+MEMBERS = 2
+DIGIT = 64
+
+
+def pack_kernel(ids, keys, values, queries, out_grad, positions, kv_out, qd_out):
+    half = kv_out.shape[0]
+    tok_dev = queries.shape[0]
+    rows = pl.ds(pl.multiple_of(ids[3] * half, half), half)
+    columns = pl.ds(pl.multiple_of(ids[2] * DH, DH), DH)
+    kv_out[:, :DH] = keys[rows, columns]
+    kv_out[:, DH:] = values[rows, columns]
+    qd_out[:tok_dev] = queries[...]
+    qd_out[tok_dev : 2 * tok_dev] = out_grad[...]
+    place = positions[...]
+    high = place // DIGIT
+    low = place - high * DIGIT
+    pad = jnp.zeros((qd_out.shape[0] - 2 * tok_dev - 2, tok_dev), jnp.float32)
+    digits = jnp.concatenate([high.astype(jnp.float32), low.astype(jnp.float32), pad], axis=0)
+    qd_out[2 * tok_dev :, :tok_dev] = digits.astype(jnp.bfloat16)
+    rest = qd_out.shape[1] - tok_dev
+    if rest > 0:
+        qd_out[2 * tok_dev :, tok_dev:] = jnp.zeros((qd_out.shape[0] - 2 * tok_dev, rest), jnp.bfloat16)
+
+
+def turn_kernel(hidden, out):
+    out[...] = hidden[...].T
+
+
+def seen_pairs(ids, owner, planes, half, qd):
+    last = 2 * planes * SIDES - 1
+    tok_dev = 2 * half
+    key_rows = []
+    row = lax.broadcasted_iota(jnp.int32, (half, tok_dev), 0)
+    for j in range(planes):
+        stretch = owner[(ids[0] ^ j) * SIDES + ids[1]]
+        stretch = jnp.where(ids[3] == 0, stretch, last - stretch)
+        key_rows.append(row + stretch * half)
+    key_place = jnp.concatenate(key_rows, axis=0)
+    lane = lax.broadcasted_iota(jnp.int32, (1, tok_dev), 1)
+    seen = []
+    for side in range(SIDES):
+        stretch = owner[ids[0] * SIDES + (ids[1] ^ side)]
+        place = jnp.where(lane < half, lane + stretch * half, lane - half + (last - stretch) * half)
+        digits = qd[side * MEMBERS][2 * tok_dev :, :tok_dev].astype(jnp.float32)
+        back = (digits[0:1] * DIGIT + digits[1:2]).astype(jnp.int32)
+        seen.append((key_place <= place) & (key_place >= place - back))
+    return seen
+
+
+def scaled_scores(k, q, scale):
+    return lax.dot_general(k, q, CONTRACT_LAST, preferred_element_type=jnp.float32) * scale
+
+
+def stats_kernel(planes, ids, owner, *refs):
+    kv_refs, qd, stats = refs[:planes], refs[planes : planes + SIDES * MEMBERS], refs[-1]
+    half = kv_refs[0].shape[0]
+    tok_dev = 2 * half
+    heads = qd[0].shape[1] // DH
+    scale = 1.0 / math.sqrt(DH)
+    kv = jnp.concatenate([ref[...] for ref in kv_refs], axis=0)
+    k, v = kv[:, :DH], kv[:, DH:]
+    seen = seen_pairs(ids, owner, planes, half, qd)
+    tiles = SIDES * MEMBERS * heads
+    for source in range(SIDES * MEMBERS):
+        for head in range(heads):
+            q = qd[source][:tok_dev, head * DH : (head + 1) * DH]
+            d = qd[source][tok_dev : 2 * tok_dev, head * DH : (head + 1) * DH]
+            mask = seen[source // MEMBERS]
+            scores = jnp.where(mask, scaled_scores(k, q, scale), NEGATIVE)
+            dprobs = lax.dot_general(v, d, CONTRACT_LAST, preferred_element_type=jnp.float32)
+            top = jnp.max(scores, axis=0, keepdims=True)
+            weights = jnp.where(mask, jnp.exp(scores - top), 0.0)
+            tile = source * heads + head
+            stats[tile : tile + 1] = top
+            stats[tiles + tile : tiles + tile + 1] = jnp.sum(weights, axis=0, keepdims=True)
+            stats[2 * tiles + tile : 2 * tiles + tile + 1] = jnp.sum(
+                weights * dprobs, axis=0, keepdims=True
+            )
+
+
+def grads_kernel(planes, ids, owner, *refs):
+    sources = SIDES * MEMBERS
+    kv_refs, refs = refs[:planes], refs[planes:]
+    qd, refs = refs[:sources], refs[sources:]
+    stats, refs = refs[:sources], refs[sources:]
+    kv_out, q_out = refs[:planes], refs[planes:]
+    half = kv_refs[0].shape[0]
+    tok_dev = 2 * half
+    heads = qd[0].shape[1] // DH
+    scale = 1.0 / math.sqrt(DH)
+    kv = jnp.concatenate([ref[...] for ref in kv_refs], axis=0)
+    k, v = kv[:, :DH], kv[:, DH:]
+    seen = seen_pairs(ids, owner, planes, half, qd)
+    tiles = sources * heads
+    key_acc = jnp.zeros((planes * half, DH), jnp.float32)
+    value_acc = jnp.zeros((planes * half, DH), jnp.float32)
+    for source in range(sources):
+        q_rows, d_rows, slope_tiles, prob_tiles = [], [], [], []
+        mask = seen[source // MEMBERS]
+        first = source * heads
+        parts = [
+            [
+                stats[other][kind * tiles + (source ^ other) * heads :][:heads]
+                for other in range(sources)
+            ]
+            for kind in range(3)
+        ]
+        top = functools.reduce(jnp.maximum, parts[0])
+        shares = [jnp.exp(part - top) for part in parts[0]]
+        mass = sum(share * part for share, part in zip(shares, parts[1], strict=True))
+        lse = top + jnp.log(mass)
+        delta = sum(share * part for share, part in zip(shares, parts[2], strict=True)) / mass
+        for head in range(heads):
+            q = qd[source][:tok_dev, head * DH : (head + 1) * DH]
+            d = qd[source][tok_dev : 2 * tok_dev, head * DH : (head + 1) * DH]
+            scores = scaled_scores(k, q, scale)
+            dprobs = lax.dot_general(v, d, CONTRACT_LAST, preferred_element_type=jnp.float32)
+            probs = jnp.where(mask, jnp.exp(scores - lse[head : head + 1]), 0.0)
+            slopes = (probs * (dprobs - delta[head : head + 1]) * scale).astype(jnp.bfloat16)
+            q_rows.append(q)
+            d_rows.append(d)
+            slope_tiles.append(slopes)
+            prob_tiles.append(probs.astype(jnp.bfloat16))
+            q_part = lax.dot_general(slopes, k, CONTRACT_FIRST, preferred_element_type=jnp.float32)
+            q_out[source][:, head * DH : (head + 1) * DH] = q_part.astype(q_out[source].dtype)
+        key_acc += jnp.dot(
+            jnp.concatenate(slope_tiles, axis=1),
+            jnp.concatenate(q_rows, axis=0),
+            preferred_element_type=jnp.float32,
+        )
+        value_acc += jnp.dot(
+            jnp.concatenate(prob_tiles, axis=1),
+            jnp.concatenate(d_rows, axis=0),
+            preferred_element_type=jnp.float32,
+        )
+    for j in range(planes):
+        kv_out[j][:, :DH] = key_acc[j * half : (j + 1) * half].astype(kv_out[j].dtype)
+        kv_out[j][:, DH:] = value_acc[j * half : (j + 1) * half].astype(kv_out[j].dtype)
+
+
+def sum_kernel(*refs):
+    total = refs[0][...].astype(jnp.float32)
+    for ref in refs[1:-1]:
+        total += ref[...].astype(jnp.float32)
+    refs[-1][...] = total.astype(refs[-1].dtype)
+
+
+def square_kernel(key_weight, value_weight, out):
+    width = key_weight.shape[1]
+    step = 256
+
+    def body(i, acc):
+        rows = pl.ds(pl.multiple_of(i * step, step), step)
+        k = key_weight[rows].astype(jnp.float32)
+        v = value_weight[rows].astype(jnp.float32)
+        return (
+            acc[0] + jnp.sum((k * k).reshape(-1, 8, width), axis=0),
+            acc[1] + jnp.sum((v * v).reshape(-1, 8, width), axis=0),
+        )
+
+    zero = jnp.zeros((8, width), jnp.float32)
+    k, v = lax.fori_loop(0, key_weight.shape[0] // step, body, (zero, zero))
+    out[:, :width] = jnp.broadcast_to(jnp.sum(k, axis=0, keepdims=True), (8, width))
+    out[:, width:] = jnp.broadcast_to(jnp.sum(v, axis=0, keepdims=True), (8, width))
+
+
+def project_kernel(planes, ids, squares, *refs):
+    count = planes * SIDES
+    turned, refs = refs[: count + 1], refs[count + 1 :]
+    pieces, refs = refs[:8], refs[8:]
+    raw, sums, all_turned, grads, acc = refs
+    step = pl.program_id(0)
+    steps = pl.num_programs(0)
+    tok_dev = turned[0].shape[1]
+    half = tok_dev // 2
+    mine = jnp.where(ids[1] == 0, ids[0], count - 1 - ids[0])
+
+    @pl.when(step == 0)
+    def _():
+        for index, piece in enumerate(pieces):
+            side = ids[1] ^ (index & 1)
+            group = ids[2] ^ ((index >> 1) & 1)
+            member = ids[3] ^ ((index >> 2) & 1)
+            for j in range(planes):
+                block = (ids[0] ^ j) * SIDES + side
+                rows = pl.ds(pl.multiple_of(block * tok_dev + member * half, half), half)
+                for kind in range(2):
+                    columns = pl.ds(pl.multiple_of((kind * KVG + group) * DH, DH), DH)
+                    grads[rows, columns] = piece[
+                        j * half : (j + 1) * half, kind * DH : (kind + 1) * DH
+                    ]
+        acc[...] = jnp.zeros_like(acc)
+
+    for r in range(count):
+        spot = mine + r
+        spot = jnp.where(spot >= count, spot - count, spot)
+        block = jnp.where(spot < planes, spot * SIDES, (count - 1 - spot) * SIDES + 1)
+        columns = pl.ds(pl.multiple_of(block * tok_dev, tok_dev), tok_dev)
+        if r == count // 2:
+            tile = jnp.where(step < steps // 2, turned[r][...], turned[count][...])
+        else:
+            tile = turned[r][...]
+        all_turned[:, columns] = tile
+    out = jnp.dot(all_turned[...], grads[...], preferred_element_type=jnp.float32)
+    raw[...] = out
+    acc[...] += jnp.sum((out * out).reshape(-1, 8, out.shape[1]), axis=0)
+
+    @pl.when(step == steps - 1)
+    def _():
+        total = jnp.sum(acc[...], axis=0, keepdims=True)
+        row = lax.broadcasted_iota(jnp.int32, sums.shape, 0)
+        sums[...] = jnp.where(row == 0, total, squares[...])
+
+
+def scale_kernel(factor, sums, sums_1, sums_2, sums_3, raw, key_out, value_out):
+    total = (sums[...] + sums_1[...]) + (sums_2[...] + sums_3[...])
+    grad_norm = jnp.sqrt(total[0:1] + EPSILON)
+    weight_norm = jnp.sqrt(total[1:2] + EPSILON)
+    clip = jnp.minimum(1.0, factor * weight_norm / grad_norm)
+    width = key_out.shape[1]
+    key_out[...] = raw[:, :width] * clip[:, :width]
+    value_out[...] = raw[:, width:] * clip[:, width:]
+
+
+def local_small(
+    queries, keys, values, out_grad, hidden, key_weight, value_weight, stretch_owner, positions
+):
+    tok_dev, width = queries.shape
+    half = tok_dev // 2
+    count = lax.axis_size("ctx")
+    planes = count // SIDES
+    groups = lax.axis_size("fsdp") // MEMBERS
+    total = tok_dev * count
+    ctx, fsdp = lax.axis_index("ctx"), lax.axis_index("fsdp")
+    ids = jnp.stack([ctx // SIDES, ctx % SIDES, fsdp // MEMBERS, fsdp % MEMBERS]).astype(jnp.int32)
+    bf16, f32 = jnp.bfloat16, jnp.float32
+    shape = jax.ShapeDtypeStruct
+
+    def call(kernel, ins, outs, **more):
+        return pl.pallas_call(
+            kernel,
+            out_shape=outs,
+            in_specs=ins,
+            out_specs=jax.tree.map(lambda _: VMEM, outs),
+            compiler_params=pltpu.CompilerParams(vmem_limit_bytes=32 * 2**20),
+            **more,
+        )
+
+    def move(x, plane=0, side=0, group=0, member=0):
+        pairs = []
+        fs = groups * MEMBERS
+        for i in range(count):
+            for j in range(fs):
+                p, s = i // SIDES ^ plane, i % SIDES ^ side
+                g, m = j // MEMBERS ^ group, j % MEMBERS ^ member
+                pairs.append((i * fs + j, (p * SIDES + s) * fs + g * MEMBERS + m))
+        return lax.ppermute(x, ("ctx", "fsdp"), pairs)
+
+    def around(x, step):
+        ring = [p * SIDES for p in range(planes)] + [p * SIDES + 1 for p in reversed(range(planes))]
+        pairs = [(ring[i], ring[(i + step) % count]) for i in range(count)]
+        return lax.ppermute(x, "ctx", pairs)
+
+    kv, qd = call(
+        pack_kernel,
+        [SMEM] + [VMEM] * 5,
+        (shape((half, 2 * DH), bf16), shape((2 * tok_dev + 16, width), bf16)),
+    )(ids, keys, values, queries, out_grad, positions.reshape(1, tok_dev))
+    qd_side = move(qd, side=1)
+    kv_all = [kv] + [move(kv, plane=j) for j in range(1, planes)]
+    qd_member = move(qd, member=1)
+    qd_both = move(qd_side, member=1)
+    qd_all = [qd, qd_member, qd_side, qd_both]
+
+    turned = call(turn_kernel, [VMEM], shape(hidden.shape[::-1], bf16))(hidden)
+    up = down = turned
+    blocks = {0: turned}
+    for step in range(1, count // 2):
+        up, down = around(up, 1), around(down, -1)
+        blocks[count - step], blocks[step] = up, down
+    middle = turned.shape[0] // 2
+    blocks[count // 2] = around(up[:middle], 1)
+    blocks[count] = around(down[middle:], -1)
+
+    squares = call(square_kernel, [VMEM] * 2, shape((8, 2 * key_weight.shape[1]), f32))(
+        key_weight, value_weight
+    )
+
+    tiles = SIDES * MEMBERS * width // DH
+    stats = call(
+        functools.partial(stats_kernel, planes),
+        [SMEM] * 2 + [VMEM] * (planes + 4),
+        shape((3 * tiles, tok_dev), f32),
+    )(ids, stretch_owner, *kv_all, *qd_all)
+    stats_all = [stats, move(stats, member=1), move(stats, side=1), move(stats, side=1, member=1)]
+    outs = call(
+        functools.partial(grads_kernel, planes),
+        [SMEM] * 2 + [VMEM] * (planes + 8),
+        tuple(shape((half, 2 * DH), bf16 if j else f32) for j in range(planes))
+        + tuple(shape((tok_dev, width), bf16 if j else f32) for j in range(4)),
+    )(ids, stretch_owner, *kv_all, *qd_all, *stats_all)
+    kv_parts, q_parts = outs[:planes], outs[planes:]
+    piece = call(sum_kernel, [VMEM] * planes, shape((half, 2 * DH), bf16))(
+        kv_parts[0], *[move(kv_parts[j], plane=j) for j in range(1, planes)]
+    )
+    piece_all = jnp.concatenate([piece] + [move(piece, plane=j) for j in range(1, planes)], axis=0)
+    near = [
+        piece_all,
+        move(piece_all, side=1),
+        move(piece_all, group=1),
+        move(piece_all, side=1, group=1),
+    ]
+    pieces = near + [move(part, member=1) for part in near]
+
+    query_grad = call(sum_kernel, [VMEM] * 4, shape((tok_dev, width), bf16))(
+        q_parts[0],
+        move(q_parts[1], member=1),
+        move(q_parts[2], side=1),
+        move(q_parts[3], side=1, member=1),
+    )
+
+    columns = 2 * KVG * DH
+    steps = 8
+    tile = turned.shape[0] // steps
+    block = pl.BlockSpec((tile, tok_dev), lambda i: (i, 0))
+    low = pl.BlockSpec((tile, tok_dev), lambda i: (jnp.minimum(i, steps // 2 - 1), 0))
+    high = pl.BlockSpec((tile, tok_dev), lambda i: (jnp.maximum(i - steps // 2, 0), 0))
+    turned_specs = [low if r == count // 2 else block for r in range(count)] + [high]
+    whole = lambda *dims: pl.BlockSpec(dims, lambda i: (0,) * len(dims))
+    raw, sums = pl.pallas_call(
+        functools.partial(project_kernel, planes),
+        grid=(steps,),
+        out_shape=(shape((turned.shape[0], columns), f32), shape((8, columns), f32)),
+        in_specs=[SMEM, whole(8, columns)]
+        + turned_specs
+        + [whole(planes * half, 2 * DH)] * len(pieces),
+        out_specs=(pl.BlockSpec((tile, columns), lambda i: (i, 0)), whole(8, columns)),
+        scratch_shapes=[
+            pltpu.VMEM((tile, total), bf16),
+            pltpu.VMEM((total, columns), bf16),
+            pltpu.VMEM((8, columns), f32),
+        ],
+        compiler_params=pltpu.CompilerParams(vmem_limit_bytes=32 * 2**20),
+    )(ids, squares, *[blocks[r] for r in range(count + 1)], *pieces)
+    sums_all = [sums, move(sums, member=1), move(sums, group=1), move(sums, group=1, member=1)]
+    out_block = pl.BlockSpec((tile, columns // 2), lambda i: (i, 0))
+    key_grad, value_grad = pl.pallas_call(
+        functools.partial(scale_kernel, CLIP_RATE * total),
+        grid=(steps,),
+        out_shape=(shape((turned.shape[0], columns // 2), f32),) * 2,
+        in_specs=[whole(8, columns)] * 4 + [pl.BlockSpec((tile, columns), lambda i: (i, 0))],
+        out_specs=(out_block, out_block),
+        compiler_params=pltpu.CompilerParams(vmem_limit_bytes=32 * 2**20),
+    )(*sums_all, raw)
+    return (query_grad, key_grad, value_grad)
+
+
 def solution(mesh):
-    return jax.shard_map(
-        local,
-        mesh=mesh,
-        in_specs=(
-            P("ctx", "fsdp"),
-            P("ctx", None),
-            P("ctx", None),
-            P("ctx", "fsdp"),
-            P("ctx", "fsdp"),
-            P("fsdp", None),
-            P("fsdp", None),
-            P(),
-            P("ctx"),
-        ),
-        out_specs=(P("ctx", "fsdp"), P("fsdp", None), P("fsdp", None)),
-        check_vma=False,
-    )
+    ctx_count, fsdp_count = mesh.shape["ctx"], mesh.shape["fsdp"]
+
+    def program(queries, keys, values, out_grad, hidden, *rest):
+        tok_dev = queries.shape[0] // ctx_count
+        heads = queries.shape[1] // fsdp_count // DH
+        gathered = hidden.size // fsdp_count * hidden.dtype.itemsize
+        planes = ctx_count // SIDES
+        small = (
+            gathered <= GATHER_LIMIT
+            and planes * SIDES == ctx_count
+            and planes & (planes - 1) == 0
+            and heads * MEMBERS == HPG
+            and fsdp_count == KVG * MEMBERS
+            and tok_dev == DH
+        )
+        return jax.shard_map(
+            local_small if small else local_large,
+            mesh=mesh,
+            in_specs=(
+                P("ctx", "fsdp"),
+                P("ctx", None),
+                P("ctx", None),
+                P("ctx", "fsdp"),
+                P("ctx", "fsdp"),
+                P("fsdp", None),
+                P("fsdp", None),
+                P(),
+                P("ctx"),
+            ),
+            out_specs=(P("ctx", "fsdp"), P("fsdp", None), P("fsdp", None)),
+            check_vma=False,
+        )(queries, keys, values, out_grad, hidden, *rest)
+
+    return program

time: 341 us -> 118 us (0.35)
  waiting for transfers between devices: 215 us -> 63.4 us
  blocking collectives: 75.9 us -> 0 us
  starting transfers between devices: 0.08 us -> 30.3 us
  Pallas kernels: 0 us -> 17.6 us
  other arithmetic: 13.8 us -> 0.09 us
  between operations: 14.2 us -> 0.81 us
  matrix products: 9.7 us -> 0 us
  local copies, waits for them, and re-layouts: 11.1 us -> 5.88 us
    psum x1 -> x0, waiting for transfers between devices: 150 us -> none  [local(): lax.psum(lax.dot_general(hidden, both_grads, contract_first, preferred_el...]
    all_gather x3 -> x0, blocking collectives: 69.1 us -> none  [the longest x1 32.5 us: local(): lax.all_gather(own_keys, 'ctx', axis=0, tiled=True)]
    reduce_scatter x1 -> x0, waiting for transfers between devices: 64.9 us -> none  [local(): lax.psum_scatter(lax.fori_loop(0, tok_dev * lax.axis_size('ctx') // width...]
    ppermute x0 -> x36, waiting for transfers between devices: none -> 63.4 us  [the longest x28 42.2 us: move(): return lax.ppermute(x, ('ctx', 'fsdp'), pairs)]
    ppermute x0 -> x36, starting transfers between devices: none -> 30.3 us  [the longest x28 23 us: move(): return lax.ppermute(x, ('ctx', 'fsdp'), pairs)]
    pallas_call x0 -> x9, Pallas kernels: none -> 17.6 us  [the longest x1 5.75 us: local_small(): pl.pallas_call(functools.partial(project_kernel, planes), grid=(steps,),...]
    dot_general x17 -> x0, matrix products: 9.7 us -> none  [the longest x8 3.46 us: scores_at(): lax.dot_general(query_rows, key_block, contract_last, preferred_element_t...]
    psum x1 -> x0, blocking collectives: 6.84 us -> none  [local(): lax.psum((jnp.sum(raw * raw, axis=0), jnp.sum(key_f * key_f, axis=0), jnp...]
  transfers between devices with their start and end apart: 2 -> 36, of which waited for: 2 -> 20; matrix products, arithmetic and copies ran while one was open for 2% -> 0% of each run, Pallas kernels for 0% -> 12%
where the time goes in v1:
time: 118 us
  waiting for transfers between devices  63.4 us (54%)
  starting transfers between devices  30.3 us (26%)
  Pallas kernels  17.6 us (15%)
  local copies, waits for them, and re-layouts  5.88 us (5%)
    ppermute x28, waiting for transfers between devices, move(): return lax.ppermute(x, ('ctx', 'fsdp'), pairs)  42.2 us
    ppermute x28, starting transfers between devices, move(): return lax.ppermute(x, ('ctx', 'fsdp'), pairs)  23 us
    ppermute x8, waiting for transfers between devices, around(): return lax.ppermute(x, 'ctx', pairs)  21.2 us
    ppermute x8, starting transfers between devices, around(): return lax.ppermute(x, 'ctx', pairs)  7.23 us
    unnamed x18, local copies, waits for them, and re-layouts  5.84 us
    pallas_call x1, Pallas kernels, local_small(): pl.pallas_call(functools.partial(project_kernel, planes), grid=(steps,),...  5.75 us
    pallas_call x1, Pallas kernels, local_small(): call(functools.partial(grads_kernel, planes), [SMEM] * 2 + [VMEM] * (plan...  4.91 us
    pallas_call x1, Pallas kernels, local_small(): pl.pallas_call(functools.partial(scale_kernel, CLIP_RATE * total), grid=(...  3.49 us
  transfers between devices with their start and end apart: 36, of which 20 were waited for; matrix products, arithmetic and copies ran while one was open for 0% of the time, Pallas kernels for 12%

profile of v1, /device:TPU:0, one launch (start us, length us, event | category | flops | bytes accessed | tf_op | source)
XLA Modules:
  0.0 118.0 jit_solution(10321849683789935366)
XLA Ops:
  1.9 3.1 %collective-permute-start.15 = (bf16[2048,128]{1,0:T(8,128)(2,1)S(1)}, bf16[2048,128]{1,0:T(8,128)(2,1)S(1)}, u32[]{:S(2)}, u32[]{:S(2)}) collective-permute-start(bf16[2048,128]{1,0:T(8,128)(2,1)S(1)} %shard_map.117.refs_0_), channel_id=1, source_target_pairs={{0,8},{8,16},{16,24},{24,28},{28,20},{20,12},{12,4},{4,0},{1,9},{9... | collective-permute-start | bytes 1572872 | tf_op jit(solution)/shard_map/ppermute | solution.py:441
  4.9 11.8 %collective-permute-done.15.refs_7_ = bf16[2048,128]{1,0:T(8,128)(2,1)S(1)} collective-permute-done((bf16[2048,128]{1,0:T(8,128)(2,1)S(1)}, bf16[2048,128]{1,0:T(8,128)(2,1)S(1)}, u32[]{:S(2)}, u32[]{:S(2)}) %collective-permute-start.15) | collective-permute-done | bytes 524320 | tf_op jit(solution)/shard_map/ppermute | solution.py:441
  16.8 1.8 %collective-permute-start.16 = (bf16[2048,128]{1,0:T(8,128)(2,1)S(1)}, bf16[2048,128]{1,0:T(8,128)(2,1)S(1)}, u32[]{:S(2)}, u32[]{:S(2)}) collective-permute-start(bf16[2048,128]{1,0:T(8,128)(2,1)S(1)} %collective-permute-done.15.refs_7_), channel_id=1, source_target_pairs={{0,8},{8,16},{16,24},{24,28},{28,20},{20,12},{12,4},{4,0},{1,9},{9... | collective-permute-start | bytes 1572872 | tf_op jit(solution)/shard_map/ppermute | solution.py:441
  23.6 1.8 %collective-permute-start.4 = (bf16[272,512]{1,0:T(8,128)(2,1)S(1)}, bf16[272,512]{1,0:T(8,128)(2,1)S(1)}, u32[]{:S(2)}, u32[]{:S(2)}) collective-permute-start(bf16[272,512]{1,0:T(8,128)(2,1)S(1)} %get-tuple-element.18.refs_4_), channel_id=1, source_target_pairs={{0,4},{1,5},{2,6},{3,7},{4,0},{5,1},{6,2},{7,3},{8,12},{9,13},{10,... | collective-permute-start | bytes 835592 | tf_op jit(solution)/shard_map/ppermute | solution.py:436
  25.4 6.2 %collective-permute-done.16.refs_6_ = bf16[2048,128]{1,0:T(8,128)(2,1)S(1)} collective-permute-done((bf16[2048,128]{1,0:T(8,128)(2,1)S(1)}, bf16[2048,128]{1,0:T(8,128)(2,1)S(1)}, u32[]{:S(2)}, u32[]{:S(2)}) %collective-permute-start.16) | collective-permute-done | bytes 524320 | tf_op jit(solution)/shard_map/ppermute | solution.py:441
  31.6 6.0 %collective-permute-done.4.refs_6_ = bf16[272,512]{1,0:T(8,128)(2,1)S(1)} collective-permute-done((bf16[272,512]{1,0:T(8,128)(2,1)S(1)}, bf16[272,512]{1,0:T(8,128)(2,1)S(1)}, u32[]{:S(2)}, u32[]{:S(2)}) %collective-permute-start.4) | collective-permute-done | bytes 278560 | tf_op jit(solution)/shard_map/ppermute | solution.py:436
  37.6 3.1 %collective-permute-start.2 = (bf16[64,256]{1,0:T(8,128)(2,1)S(1)}, bf16[64,256]{1,0:T(8,128)(2,1)S(1)}, u32[]{:S(2)}, u32[]{:S(2)}) collective-permute-start(bf16[64,256]{1,0:T(8,128)(2,1)S(1)} %get-tuple-element.17.refs_0_), channel_id=1, source_target_pairs={{0,24},{1,25},{2,26},{3,27},{4,28},{5,29},{6,30},{7,31},{8,16},{9,... | collective-permute-start | bytes 98312 | tf_op jit(solution)/shard_map/ppermute | solution.py:436
  40.7 13.2 %collective-permute-done.2.refs_3_ = bf16[64,256]{1,0:T(8,128)(2,1)S(1)} collective-permute-done((bf16[64,256]{1,0:T(8,128)(2,1)S(1)}, bf16[64,256]{1,0:T(8,128)(2,1)S(1)}, u32[]{:S(2)}, u32[]{:S(2)}) %collective-permute-start.2) | collective-permute-done | bytes 32800 | tf_op jit(solution)/shard_map/ppermute | solution.py:436
  53.9 4.8 %collective-permute-done.1.refs_2_ = bf16[64,256]{1,0:T(8,128)(2,1)S(1)} collective-permute-done((bf16[64,256]{1,0:T(8,128)(2,1)S(1)}, bf16[64,256]{1,0:T(8,128)(2,1)S(1)}, u32[]{:S(2)}, u32[]{:S(2)}) %collective-permute-start.1) | collective-permute-done | bytes 32800 | tf_op jit(solution)/shard_map/ppermute | solution.py:436
  58.7 3.9 %collective-permute-done.refs_1_ = bf16[64,256]{1,0:T(8,128)(2,1)S(1)} collective-permute-done((bf16[64,256]{1,0:T(8,128)(2,1)S(1)}, bf16[64,256]{1,0:T(8,128)(2,1)S(1)}, u32[]{:S(2)}, u32[]{:S(2)}) %collective-permute-start) | collective-permute-done | bytes 32800 | tf_op jit(solution)/shard_map/ppermute | solution.py:436
  63.3 1.7 %shard_map.113.refs_8_ = f32[48,128]{1,0:T(8,128)S(1)} custom-call(s32[4]{0:T(128)S(1)} %pad_add_fusion.ids, s32[8]{0:T(128)S(1)} %copy-done.7, bf16[64,256]{1,0:T(8,128)(2,1)S(1)} %get-tuple-element.17.refs_0_, bf16[64,256]{1,0:T(8,128)(2,1)S(1)} %collective-permute-done.refs_1_, bf16[64,256]{1,0:T(8,128)(2,1)S(1)} %collective-permute-done.1.refs_2_, ...), custom_call_target="tpu_custom_call" | custom-call | tf_op jit(solution)/shard_map/pallas_call | solution.py:469
  65.2 1.8 %collective-permute-start.6 = (f32[48,128]{1,0:T(8,128)S(1)}, f32[48,128]{1,0:T(8,128)S(1)}, u32[]{:S(2)}, u32[]{:S(2)}) collective-permute-start(f32[48,128]{1,0:T(8,128)S(1)} %shard_map.113.refs_8_), channel_id=1, source_target_pairs={{0,1},{1,0},{2,3},{3,2},{4,5},{5,4},{6,7},{7,6},{8,9},{9,8},{10,11... | collective-permute-start | bytes 73736 | tf_op jit(solution)/shard_map/ppermute | solution.py:436
  69.0 4.9 %shard_map.114 = (f32[64,256]{1,0:T(8,128)S(1)}, bf16[64,256]{1,0:T(8,128)(2,1)S(1)}, bf16[64,256]{1,0:T(8,128)(2,1)S(1)}, bf16[64,256]{1,0:T(8,128)(2,1)S(1)}, ...) custom-call(s32[4]{0:T(128)S(1)} %pad_add_fusion.ids, ...), custom_call_target="tpu_custom_call" | custom-call | tf_op jit(solution)/shard_map/pallas_call | solution.py:475
  74.1 4.3 %collective-permute-start.22 = (bf16[64,256]{1,0:T(8,128)(2,1)S(1)}, bf16[64,256]{1,0:T(8,128)(2,1)S(1)}, u32[]{:S(2)}, u32[]{:S(2)}) collective-permute-start(bf16[64,256]{1,0:T(8,128)(2,1)S(1)} %get-tuple-element.26), channel_id=1, source_target_pairs={{0,24},{1,25},{2,26},{3,27},{4,28},{5,29},{6,30},{7,31},{8,16},{9,... | collective-permute-start | bytes 98312 | tf_op jit(solution)/shard_map/ppermute | solution.py:436
  79.2 1.4 %collective-permute-done.22.refs_3_ = bf16[64,256]{1,0:T(8,128)(2,1)S(1)} collective-permute-done((bf16[64,256]{1,0:T(8,128)(2,1)S(1)}, bf16[64,256]{1,0:T(8,128)(2,1)S(1)}, u32[]{:S(2)}, u32[]{:S(2)}) %collective-permute-start.22) | collective-permute-done | bytes 32800 | tf_op jit(solution)/shard_map/ppermute | solution.py:436
  80.6 3.5 %collective-permute-start.25 = (bf16[64,256]{1,0:T(8,128)(2,1)S(1)}, bf16[64,256]{1,0:T(8,128)(2,1)S(1)}, u32[]{:S(2)}, u32[]{:S(2)}) collective-permute-start(bf16[64,256]{1,0:T(8,128)(2,1)S(1)} %shard_map.118), channel_id=1, source_target_pairs={{0,24},{1,25},{2,26},{3,27},{4,28},{5,29},{6,30},{7,31},{8,16},{9,... | collective-permute-start | bytes 98312 | tf_op jit(solution)/shard_map/ppermute | solution.py:436
  86.4 2.6 %collective-permute-done.24 = bf16[64,256]{1,0:T(8,128)(2,1)S(1)} collective-permute-done((bf16[64,256]{1,0:T(8,128)(2,1)S(1)}, bf16[64,256]{1,0:T(8,128)(2,1)S(1)}, u32[]{:S(2)}, u32[]{:S(2)}) %collective-permute-start.24) | collective-permute-done | bytes 32800 | tf_op jit(solution)/shard_map/ppermute | solution.py:436
  90.8 1.8 %collective-permute-start.26 = (bf16[256,256]{1,0:T(8,128)(2,1)S(1)}, bf16[256,256]{1,0:T(8,128)(2,1)S(1)}, u32[]{:S(2)}, u32[]{:S(2)}) collective-permute-start(bf16[256,256]{1,0:T(8,128)(2,1)S(1)} %pad_maximum_fusion.refs_9_), channel_id=1, source_target_pairs={{0,4},{1,5},{2,6},{3,7},{4,0},{5,1},{6,2},{7,3},{8,12},{9,13},{10,... | collective-permute-start | bytes 393224 | tf_op jit(solution)/shard_map/ppermute | solution.py:436
  92.8 2.1 %collective-permute-start.19 = (bf16[1024,128]{1,0:T(8,128)(2,1)S(1)}, bf16[1024,128]{1,0:T(8,128)(2,1)S(1)}, u32[]{:S(2)}, u32[]{:S(2)}) collective-permute-start(bf16[1024,128]{1,0:T(8,128)(2,1)S(1)} %slice.9), channel_id=1, source_target_pairs={{0,4},{8,0},{16,8},{24,16},{28,24},{20,28},{12,20},{4,12},{1,5},{9... | collective-permute-start | bytes 786440 | tf_op jit(solution)/shard_map/ppermute | solution.py:441
  94.8 1.6 %collective-permute-done.28.refs_12_ = bf16[256,256]{1,0:T(8,128)(2,1)S(1)} collective-permute-done((bf16[256,256]{1,0:T(8,128)(2,1)S(1)}, bf16[256,256]{1,0:T(8,128)(2,1)S(1)}, u32[]{:S(2)}, u32[]{:S(2)}) %collective-permute-start.28) | collective-permute-done | bytes 131104 | tf_op jit(solution)/shard_map/ppermute | solution.py:436
  96.4 2.3 %collective-permute-done.27.refs_11_ = bf16[256,256]{1,0:T(8,128)(2,1)S(1)} collective-permute-done((bf16[256,256]{1,0:T(8,128)(2,1)S(1)}, bf16[256,256]{1,0:T(8,128)(2,1)S(1)}, u32[]{:S(2)}, u32[]{:S(2)}) %collective-permute-start.27) | collective-permute-done | bytes 131104 | tf_op jit(solution)/shard_map/ppermute | solution.py:436
  101.7 3.1 %collective-permute-done.18.refs_4_ = bf16[1024,128]{1,0:T(8,128)(2,1)S(1)} collective-permute-done((bf16[1024,128]{1,0:T(8,128)(2,1)S(1)}, bf16[1024,128]{1,0:T(8,128)(2,1)S(1)}, u32[]{:S(2)}, u32[]{:S(2)}) %collective-permute-start.18) | collective-permute-done | bytes 262176 | tf_op jit(solution)/shard_map/ppermute | solution.py:441
  104.9 5.8 %shard_map.119 = (f32[2048,512]{1,0:T(8,128)S(1)}, f32[8,512]{1,0:T(8,128)S(1)}) custom-call(s32[4]{0:T(128)S(1)} %pad_add_fusion.ids, f32[8,512]{1,0:T(8,128)S(1)} %shard_map.116.squares, bf16[2048,128]{1,0:T(8,128)(2,1)S(1)} %shard_map.117.refs_0_, bf16[2048,128]{1,0:T(8,128)(2,1)S(1)} %collective-permute-done.12.refs_1_, ...), custom_call_target="tpu_custom_call" | custom-call | tf_op jit(solution)/shard_map/pallas_call | solution.py:509
  114.5 3.5 %shard_map.120 = (f32[2048,256]{1,0:T(8,128)}, f32[2048,256]{1,0:T(8,128)}) custom-call(f32[8,512]{1,0:T(8,128)S(1)} %get-tuple-element.27.sums, f32[8,512]{1,0:T(8,128)S(1)} %collective-permute-done.33.sums_1, f32[8,512]{1,0:T(8,128)S(1)} %collective-permute-done.34.sums_2, f32[8,512]{1,0:T(8,128)S(1)} %collective-permute-done.35.sums_3, ...), custom_call_target="tpu_custom_call" | custom-call | tf_op jit(solution)/shard_map/pallas_call | solution.py:526
  (79 shorter events, 21.2 us)
Async XLA Ops:
  1.9 14.9 %collective-permute-start.15 = (bf16[2048,128]{1,0:T(8,128)(2,1)S(1)}, bf16[2048,128]{1,0:T(8,128)(2,1)S(1)}, u32[]{:S(2)}, u32[]{:S(2)}) collective-permute-start(bf16[2048,128]{1,0:T(8,128)(2,1)S(1)} %shard_map.117.refs_0_), channel_id=1, source_target_pairs={{0,8},{8,16},{16,24},{24,28},{28,20},{20,12},{12,4},{4,0},{1,9},{9... | collective-permute-start | bytes 1572872 | tf_op jit(solution)/shard_map/ppermute | solution.py:441
  4.9 13.7 %collective-permute-start.12 = (bf16[2048,128]{1,0:T(8,128)(2,1)S(1)}, bf16[2048,128]{1,0:T(8,128)(2,1)S(1)}, u32[]{:S(2)}, u32[]{:S(2)}) collective-permute-start(bf16[2048,128]{1,0:T(8,128)(2,1)S(1)} %shard_map.117.refs_0_), channel_id=1, source_target_pairs={{0,4},{8,0},{16,8},{24,16},{28,24},{20,28},{12,20},{4,12},{1,5},{9... | collective-permute-start | bytes 1572872 | tf_op jit(solution)/shard_map/ppermute | solution.py:441
  16.8 14.9 %collective-permute-start.16 = (bf16[2048,128]{1,0:T(8,128)(2,1)S(1)}, bf16[2048,128]{1,0:T(8,128)(2,1)S(1)}, u32[]{:S(2)}, u32[]{:S(2)}) collective-permute-start(bf16[2048,128]{1,0:T(8,128)(2,1)S(1)} %collective-permute-done.15.refs_7_), channel_id=1, source_target_pairs={{0,8},{8,16},{16,24},{24,28},{28,20},{20,12},{12,4},{4,0},{1,9},{9... | collective-permute-start | bytes 1572872 | tf_op jit(solution)/shard_map/ppermute | solution.py:441
  18.6 19.0 %collective-permute-start.13 = (bf16[2048,128]{1,0:T(8,128)(2,1)S(1)}, bf16[2048,128]{1,0:T(8,128)(2,1)S(1)}, u32[]{:S(2)}, u32[]{:S(2)}) collective-permute-start(bf16[2048,128]{1,0:T(8,128)(2,1)S(1)} %collective-permute-done.12.refs_1_), channel_id=1, source_target_pairs={{0,4},{8,0},{16,8},{24,16},{28,24},{20,28},{12,20},{4,12},{1,5},{9... | collective-permute-start | bytes 1572872 | tf_op jit(solution)/shard_map/ppermute | solution.py:441
  23.6 14.0 %collective-permute-start.4 = (bf16[272,512]{1,0:T(8,128)(2,1)S(1)}, bf16[272,512]{1,0:T(8,128)(2,1)S(1)}, u32[]{:S(2)}, u32[]{:S(2)}) collective-permute-start(bf16[272,512]{1,0:T(8,128)(2,1)S(1)} %get-tuple-element.18.refs_4_), channel_id=1, source_target_pairs={{0,4},{1,5},{2,6},{3,7},{4,0},{5,1},{6,2},{7,3},{8,12},{9,13},{10,... | collective-permute-start | bytes 835592 | tf_op jit(solution)/shard_map/ppermute | solution.py:436
  31.6 59.2 %collective-permute-start.17 = (bf16[2048,128]{1,0:T(8,128)(2,1)S(1)}, bf16[2048,128]{1,0:T(8,128)(2,1)S(1)}, u32[]{:S(2)}, u32[]{:S(2)}) collective-permute-start(bf16[2048,128]{1,0:T(8,128)(2,1)S(1)} %collective-permute-done.16.refs_6_), channel_id=1, source_target_pairs={{0,8},{8,16},{16,24},{24,28},{28,20},{20,12},{12,4},{4,0},{1,9},{9... | collective-permute-start | bytes 1572872 | tf_op jit(solution)/shard_map/ppermute | solution.py:441
  31.6 31.0 %collective-permute-start.3 = (bf16[272,512]{1,0:T(8,128)(2,1)S(1)}, bf16[272,512]{1,0:T(8,128)(2,1)S(1)}, u32[]{:S(2)}, u32[]{:S(2)}) collective-permute-start(bf16[272,512]{1,0:T(8,128)(2,1)S(1)} %get-tuple-element.18.refs_4_), channel_id=1, source_target_pairs={{0,1},{1,0},{2,3},{3,2},{4,5},{5,4},{6,7},{7,6},{8,9},{9,8},{10,11... | collective-permute-start | bytes 835592 | tf_op jit(solution)/shard_map/ppermute | solution.py:436
  37.6 25.0 %collective-permute-start.5 = (bf16[272,512]{1,0:T(8,128)(2,1)S(1)}, bf16[272,512]{1,0:T(8,128)(2,1)S(1)}, u32[]{:S(2)}, u32[]{:S(2)}) collective-permute-start(bf16[272,512]{1,0:T(8,128)(2,1)S(1)} %collective-permute-done.4.refs_6_), channel_id=1, source_target_pairs={{0,1},{1,0},{2,3},{3,2},{4,5},{5,4},{6,7},{7,6},{8,9},{9,8},{10,11... | collective-permute-start | bytes 835592 | tf_op jit(solution)/shard_map/ppermute | solution.py:436
  37.6 55.0 %collective-permute-start.14 = (bf16[2048,128]{1,0:T(8,128)(2,1)S(1)}, bf16[2048,128]{1,0:T(8,128)(2,1)S(1)}, u32[]{:S(2)}, u32[]{:S(2)}) collective-permute-start(bf16[2048,128]{1,0:T(8,128)(2,1)S(1)} %collective-permute-done.13.refs_2_), channel_id=1, source_target_pairs={{0,4},{8,0},{16,8},{24,16},{28,24},{20,28},{12,20},{4,12},{1,5},{9... | collective-permute-start | bytes 1572872 | tf_op jit(solution)/shard_map/ppermute | solution.py:441
  37.6 16.3 %collective-permute-start.2 = (bf16[64,256]{1,0:T(8,128)(2,1)S(1)}, bf16[64,256]{1,0:T(8,128)(2,1)S(1)}, u32[]{:S(2)}, u32[]{:S(2)}) collective-permute-start(bf16[64,256]{1,0:T(8,128)(2,1)S(1)} %get-tuple-element.17.refs_0_), channel_id=1, source_target_pairs={{0,24},{1,25},{2,26},{3,27},{4,28},{5,29},{6,30},{7,31},{8,16},{9,... | collective-permute-start | bytes 98312 | tf_op jit(solution)/shard_map/ppermute | solution.py:436
  53.9 4.8 %collective-permute-start.1 = (bf16[64,256]{1,0:T(8,128)(2,1)S(1)}, bf16[64,256]{1,0:T(8,128)(2,1)S(1)}, u32[]{:S(2)}, u32[]{:S(2)}) collective-permute-start(bf16[64,256]{1,0:T(8,128)(2,1)S(1)} %get-tuple-element.17.refs_0_), channel_id=1, source_target_pairs={{0,16},{1,17},{2,18},{3,19},{4,20},{5,21},{6,22},{7,23},{8,24},{9,... | collective-permute-start | bytes 98312 | tf_op jit(solution)/shard_map/ppermute | solution.py:436
  74.0 5.2 %collective-permute-start.21 = (bf16[64,256]{1,0:T(8,128)(2,1)S(1)}, bf16[64,256]{1,0:T(8,128)(2,1)S(1)}, u32[]{:S(2)}, u32[]{:S(2)}) collective-permute-start(bf16[64,256]{1,0:T(8,128)(2,1)S(1)} %get-tuple-element.25), channel_id=1, source_target_pairs={{0,16},{1,17},{2,18},{3,19},{4,20},{5,21},{6,22},{7,23},{8,24},{9,... | collective-permute-start | bytes 98312 | tf_op jit(solution)/shard_map/ppermute | solution.py:436
  74.1 6.5 %collective-permute-start.22 = (bf16[64,256]{1,0:T(8,128)(2,1)S(1)}, bf16[64,256]{1,0:T(8,128)(2,1)S(1)}, u32[]{:S(2)}, u32[]{:S(2)}) collective-permute-start(bf16[64,256]{1,0:T(8,128)(2,1)S(1)} %get-tuple-element.26), channel_id=1, source_target_pairs={{0,24},{1,25},{2,26},{3,27},{4,28},{5,29},{6,30},{7,31},{8,16},{9,... | collective-permute-start | bytes 98312 | tf_op jit(solution)/shard_map/ppermute | solution.py:436
  80.6 5.8 %collective-permute-start.25 = (bf16[64,256]{1,0:T(8,128)(2,1)S(1)}, bf16[64,256]{1,0:T(8,128)(2,1)S(1)}, u32[]{:S(2)}, u32[]{:S(2)}) collective-permute-start(bf16[64,256]{1,0:T(8,128)(2,1)S(1)} %shard_map.118), channel_id=1, source_target_pairs={{0,24},{1,25},{2,26},{3,27},{4,28},{5,29},{6,30},{7,31},{8,16},{9,... | collective-permute-start | bytes 98312 | tf_op jit(solution)/shard_map/ppermute | solution.py:436
  84.2 4.8 %collective-permute-start.24 = (bf16[64,256]{1,0:T(8,128)(2,1)S(1)}, bf16[64,256]{1,0:T(8,128)(2,1)S(1)}, u32[]{:S(2)}, u32[]{:S(2)}) collective-permute-start(bf16[64,256]{1,0:T(8,128)(2,1)S(1)} %shard_map.118), channel_id=1, source_target_pairs={{0,16},{1,17},{2,18},{3,19},{4,20},{5,21},{6,22},{7,23},{8,24},{9,... | collective-permute-start | bytes 98312 | tf_op jit(solution)/shard_map/ppermute | solution.py:436
  84.2 4.8 %collective-permute-start.23 = (bf16[64,256]{1,0:T(8,128)(2,1)S(1)}, bf16[64,256]{1,0:T(8,128)(2,1)S(1)}, u32[]{:S(2)}, u32[]{:S(2)}) collective-permute-start(bf16[64,256]{1,0:T(8,128)(2,1)S(1)} %shard_map.118), channel_id=1, source_target_pairs={{0,8},{1,9},{2,10},{3,11},{4,12},{5,13},{6,14},{7,15},{8,0},{9,1},... | collective-permute-start | bytes 98312 | tf_op jit(solution)/shard_map/ppermute | solution.py:436
  89.1 7.3 %collective-permute-start.28 = (bf16[256,256]{1,0:T(8,128)(2,1)S(1)}, bf16[256,256]{1,0:T(8,128)(2,1)S(1)}, u32[]{:S(2)}, u32[]{:S(2)}) collective-permute-start(bf16[256,256]{1,0:T(8,128)(2,1)S(1)} %pad_maximum_fusion.refs_9_), channel_id=1, source_target_pairs={{0,6},{1,7},{2,4},{3,5},{4,2},{5,3},{6,0},{7,1},{8,14},{9,15},{10,... | collective-permute-start | bytes 393224 | tf_op jit(solution)/shard_map/ppermute | solution.py:436
  90.3 8.4 %collective-permute-start.27 = (bf16[256,256]{1,0:T(8,128)(2,1)S(1)}, bf16[256,256]{1,0:T(8,128)(2,1)S(1)}, u32[]{:S(2)}, u32[]{:S(2)}) collective-permute-start(bf16[256,256]{1,0:T(8,128)(2,1)S(1)} %pad_maximum_fusion.refs_9_), channel_id=1, source_target_pairs={{0,2},{1,3},{2,0},{3,1},{4,6},{5,7},{6,4},{7,5},{8,10},{9,11},{10,... | collective-permute-start | bytes 393224 | tf_op jit(solution)/shard_map/ppermute | solution.py:436
  90.8 8.4 %collective-permute-start.26 = (bf16[256,256]{1,0:T(8,128)(2,1)S(1)}, bf16[256,256]{1,0:T(8,128)(2,1)S(1)}, u32[]{:S(2)}, u32[]{:S(2)}) collective-permute-start(bf16[256,256]{1,0:T(8,128)(2,1)S(1)} %pad_maximum_fusion.refs_9_), channel_id=1, source_target_pairs={{0,4},{1,5},{2,6},{3,7},{4,0},{5,1},{6,2},{7,3},{8,12},{9,13},{10,... | collective-permute-start | bytes 393224 | tf_op jit(solution)/shard_map/ppermute | solution.py:436
  92.7 12.2 %collective-permute-start.18 = (bf16[1024,128]{1,0:T(8,128)(2,1)S(1)}, bf16[1024,128]{1,0:T(8,128)(2,1)S(1)}, u32[]{:S(2)}, u32[]{:S(2)}) collective-permute-start(bf16[1024,128]{1,0:T(8,128)(2,1)S(1)} %slice.8), channel_id=1, source_target_pairs={{0,8},{8,16},{16,24},{24,28},{28,20},{20,12},{12,4},{4,0},{1,9},{9... | collective-permute-start | bytes 786440 | tf_op jit(solution)/shard_map/ppermute | solution.py:441
  92.8 12.1 %collective-permute-start.19 = (bf16[1024,128]{1,0:T(8,128)(2,1)S(1)}, bf16[1024,128]{1,0:T(8,128)(2,1)S(1)}, u32[]{:S(2)}, u32[]{:S(2)}) collective-permute-start(bf16[1024,128]{1,0:T(8,128)(2,1)S(1)} %slice.9), channel_id=1, source_target_pairs={{0,4},{8,0},{16,8},{24,16},{28,24},{20,28},{12,20},{4,12},{1,5},{9... | collective-permute-start | bytes 786440 | tf_op jit(solution)/shard_map/ppermute | solution.py:441
  99.2 12.3 %collective-permute-start.9 = (bf16[128,512]{1,0:T(8,128)(2,1)S(1)}, bf16[128,512]{1,0:T(8,128)(2,1)S(1)}, u32[]{:S(2)}, u32[]{:S(2)}) collective-permute-start(bf16[128,512]{1,0:T(8,128)(2,1)S(1)} %get-tuple-element.20), channel_id=1, source_target_pairs={{0,1},{1,0},{2,3},{3,2},{4,5},{5,4},{6,7},{7,6},{8,9},{9,8},{10,11... | collective-permute-start | bytes 393224 | tf_op jit(solution)/shard_map/ppermute | solution.py:436
  100.0 12.5 %collective-permute-start.10 = (bf16[128,512]{1,0:T(8,128)(2,1)S(1)}, bf16[128,512]{1,0:T(8,128)(2,1)S(1)}, u32[]{:S(2)}, u32[]{:S(2)}) collective-permute-start(bf16[128,512]{1,0:T(8,128)(2,1)S(1)} %get-tuple-element.21), channel_id=1, source_target_pairs={{0,4},{1,5},{2,6},{3,7},{4,0},{5,1},{6,2},{7,3},{8,12},{9,13},{10,... | collective-permute-start | bytes 393224 | tf_op jit(solution)/shard_map/ppermute | solution.py:436
  100.6 12.0 %collective-permute-start.11 = (bf16[128,512]{1,0:T(8,128)(2,1)S(1)}, bf16[128,512]{1,0:T(8,128)(2,1)S(1)}, u32[]{:S(2)}, u32[]{:S(2)}) collective-permute-start(bf16[128,512]{1,0:T(8,128)(2,1)S(1)} %get-tuple-element.22), channel_id=1, source_target_pairs={{0,5},{1,4},{2,7},{3,6},{4,1},{5,0},{6,3},{7,2},{8,13},{9,12},{10,... | collective-permute-start | bytes 393224 | tf_op jit(solution)/shard_map/ppermute | solution.py:436
  (21 other events, 200.4 us)

commit v2 on v1

--- a/solution.py
+++ b/solution.py
@@ -22,6 +22,7 @@
 CONTRACT_FIRST = (((0,), (0,)), ((), ()))
 VMEM = pl.BlockSpec(memory_space=pltpu.VMEM)
 SMEM = pl.BlockSpec(memory_space=pltpu.SMEM)
+ANY = pl.BlockSpec(memory_space=pl.ANY)
 
 
 def rows_by_head(block, heads, width):
@@ -181,28 +182,56 @@
 DIGIT = 64
 
 
-def pack_kernel(ids, keys, values, queries, out_grad, positions, kv_out, qd_out):
+def pack_kernel(
+    ids, keys, values, queries, out_grad, positions, hidden, kv_out, qd_out, turned, place, held, sems
+):
     half = kv_out.shape[0]
     tok_dev = queries.shape[0]
     rows = pl.ds(pl.multiple_of(ids[3] * half, half), half)
     columns = pl.ds(pl.multiple_of(ids[2] * DH, DH), DH)
-    kv_out[:, :DH] = keys[rows, columns]
-    kv_out[:, DH:] = values[rows, columns]
-    qd_out[:tok_dev] = queries[...]
-    qd_out[tok_dev : 2 * tok_dev] = out_grad[...]
-    place = positions[...]
-    high = place // DIGIT
-    low = place - high * DIGIT
+    copies = [
+        pltpu.make_async_copy(source, target, sems.at[i])
+        for i, (source, target) in enumerate(
+            (
+                (hidden, held),
+                (positions, place),
+                (keys.at[rows, columns], kv_out.at[:, :DH]),
+                (values.at[rows, columns], kv_out.at[:, DH:]),
+                (queries, qd_out.at[:tok_dev]),
+                (out_grad, qd_out.at[tok_dev : 2 * tok_dev]),
+            )
+        )
+    ]
+    for copy in copies:
+        copy.start()
+    rest = qd_out.shape[1] - tok_dev
+    if rest > 0:
+        qd_out[2 * tok_dev :, tok_dev:] = jnp.zeros((qd_out.shape[0] - 2 * tok_dev, rest), jnp.bfloat16)
+    copies[0].wait()
+    turned[...] = held[...].T
+    copies[1].wait()
+    high = place[...] // DIGIT
+    low = place[...] - high * DIGIT
     pad = jnp.zeros((qd_out.shape[0] - 2 * tok_dev - 2, tok_dev), jnp.float32)
     digits = jnp.concatenate([high.astype(jnp.float32), low.astype(jnp.float32), pad], axis=0)
     qd_out[2 * tok_dev :, :tok_dev] = digits.astype(jnp.bfloat16)
-    rest = qd_out.shape[1] - tok_dev
-    if rest > 0:
-        qd_out[2 * tok_dev :, tok_dev:] = jnp.zeros((qd_out.shape[0] - 2 * tok_dev, rest), jnp.bfloat16)
-
-
-def turn_kernel(hidden, out):
-    out[...] = hidden[...].T
+    for copy in copies[2:]:
+        copy.wait()
+
+
+def nothing_kernel(*refs):
+    pass
+
+
+def after(x, *events):
+    return pl.pallas_call(
+        nothing_kernel,
+        out_shape=jax.ShapeDtypeStruct(x.shape, x.dtype),
+        in_specs=[ANY] * (1 + len(events)),
+        out_specs=ANY,
+        input_output_aliases={0: 0},
+        compiler_params=pltpu.CompilerParams(vmem_limit_bytes=2**20),
+    )(x, *events)
 
 
 def seen_pairs(ids, owner, planes, half, qd):
@@ -262,7 +291,7 @@
     kv_refs, refs = refs[:planes], refs[planes:]
     qd, refs = refs[:sources], refs[sources:]
     stats, refs = refs[:sources], refs[sources:]
-    kv_out, q_out = refs[:planes], refs[planes:]
+    kv_out, slopes_out = refs[:planes], refs[planes]
     half = kv_refs[0].shape[0]
     tok_dev = 2 * half
     heads = qd[0].shape[1] // DH
@@ -300,10 +329,10 @@
             d_rows.append(d)
             slope_tiles.append(slopes)
             prob_tiles.append(probs.astype(jnp.bfloat16))
-            q_part = lax.dot_general(slopes, k, CONTRACT_FIRST, preferred_element_type=jnp.float32)
-            q_out[source][:, head * DH : (head + 1) * DH] = q_part.astype(q_out[source].dtype)
+        slope_tile = jnp.concatenate(slope_tiles, axis=1)
+        slopes_out[source] = slope_tile
         key_acc += jnp.dot(
-            jnp.concatenate(slope_tiles, axis=1),
+            slope_tile,
             jnp.concatenate(q_rows, axis=0),
             preferred_element_type=jnp.float32,
         )
@@ -315,6 +344,23 @@
     for j in range(planes):
         kv_out[j][:, :DH] = key_acc[j * half : (j + 1) * half].astype(kv_out[j].dtype)
         kv_out[j][:, DH:] = value_acc[j * half : (j + 1) * half].astype(kv_out[j].dtype)
+
+
+def query_kernel(planes, *refs):
+    kv_refs, slopes, q_out = refs[:planes], refs[planes], refs[planes + 2 :]
+    k = jnp.concatenate([ref[:, :DH] for ref in kv_refs], axis=0)
+    for source, out in enumerate(q_out):
+        tok_dev, width = out.shape
+        for head in range(width // DH):
+            tile = slopes[source, :, head * tok_dev : (head + 1) * tok_dev]
+            part = lax.dot_general(tile, k, CONTRACT_FIRST, preferred_element_type=jnp.float32)
+            out[:, head * DH : (head + 1) * DH] = part.astype(out.dtype)
+
+
+def join_kernel(*refs):
+    rows = refs[0].shape[0]
+    for i, ref in enumerate(refs[:-1]):
+        refs[-1][i * rows : (i + 1) * rows] = ref[...]
 
 
 def sum_kernel(*refs):
@@ -326,79 +372,76 @@
 
 def square_kernel(key_weight, value_weight, out):
     width = key_weight.shape[1]
-    step = 256
-
-    def body(i, acc):
-        rows = pl.ds(pl.multiple_of(i * step, step), step)
-        k = key_weight[rows].astype(jnp.float32)
-        v = value_weight[rows].astype(jnp.float32)
-        return (
-            acc[0] + jnp.sum((k * k).reshape(-1, 8, width), axis=0),
-            acc[1] + jnp.sum((v * v).reshape(-1, 8, width), axis=0),
-        )
-
-    zero = jnp.zeros((8, width), jnp.float32)
-    k, v = lax.fori_loop(0, key_weight.shape[0] // step, body, (zero, zero))
-    out[:, :width] = jnp.broadcast_to(jnp.sum(k, axis=0, keepdims=True), (8, width))
-    out[:, width:] = jnp.broadcast_to(jnp.sum(v, axis=0, keepdims=True), (8, width))
-
-
-def project_kernel(planes, ids, squares, *refs):
+
+    @pl.when(pl.program_id(0) == 0)
+    def _():
+        out[...] = jnp.zeros_like(out)
+
+    k = key_weight[...].astype(jnp.float32)
+    v = value_weight[...].astype(jnp.float32)
+    out[:, :width] += jnp.sum((k * k).reshape(-1, 8, width), axis=0)
+    out[:, width:] += jnp.sum((v * v).reshape(-1, 8, width), axis=0)
+
+
+def project_kernel(planes, steps, ids, squares, turned, *refs):
     count = planes * SIDES
-    turned, refs = refs[: count + 1], refs[count + 1 :]
-    pieces, refs = refs[:8], refs[8:]
-    raw, sums, all_turned, grads, acc = refs
-    step = pl.program_id(0)
-    steps = pl.num_programs(0)
-    tok_dev = turned[0].shape[1]
+    pieces, (raw, sums, grads, held, sems) = refs[:8], refs[8:]
+    tok_dev = turned.shape[2]
     half = tok_dev // 2
-    mine = jnp.where(ids[1] == 0, ids[0], count - 1 - ids[0])
-
-    @pl.when(step == 0)
-    def _():
-        for index, piece in enumerate(pieces):
-            side = ids[1] ^ (index & 1)
-            group = ids[2] ^ ((index >> 1) & 1)
-            member = ids[3] ^ ((index >> 2) & 1)
-            for j in range(planes):
-                block = (ids[0] ^ j) * SIDES + side
-                rows = pl.ds(pl.multiple_of(block * tok_dev + member * half, half), half)
-                for kind in range(2):
-                    columns = pl.ds(pl.multiple_of((kind * KVG + group) * DH, DH), DH)
-                    grads[rows, columns] = piece[
-                        j * half : (j + 1) * half, kind * DH : (kind + 1) * DH
-                    ]
-        acc[...] = jnp.zeros_like(acc)
-
-    for r in range(count):
-        spot = mine + r
-        spot = jnp.where(spot >= count, spot - count, spot)
-        block = jnp.where(spot < planes, spot * SIDES, (count - 1 - spot) * SIDES + 1)
-        columns = pl.ds(pl.multiple_of(block * tok_dev, tok_dev), tok_dev)
-        if r == count // 2:
-            tile = jnp.where(step < steps // 2, turned[r][...], turned[count][...])
-        else:
-            tile = turned[r][...]
-        all_turned[:, columns] = tile
-    out = jnp.dot(all_turned[...], grads[...], preferred_element_type=jnp.float32)
-    raw[...] = out
-    acc[...] += jnp.sum((out * out).reshape(-1, 8, out.shape[1]), axis=0)
-
-    @pl.when(step == steps - 1)
-    def _():
-        total = jnp.sum(acc[...], axis=0, keepdims=True)
-        row = lax.broadcasted_iota(jnp.int32, sums.shape, 0)
-        sums[...] = jnp.where(row == 0, total, squares[...])
-
-
-def scale_kernel(factor, sums, sums_1, sums_2, sums_3, raw, key_out, value_out):
+    tile = raw.shape[0] // steps
+    copies = [
+        pltpu.make_async_copy(turned.at[:, rows], held.at[:, rows], sems.at[i])
+        for i, rows in enumerate(pl.ds(i * tile, tile) for i in range(steps))
+    ]
+    for copy in copies:
+        copy.start()
+    for index, piece in enumerate(pieces):
+        side = ids[1] ^ (index & 1)
+        group = ids[2] ^ ((index >> 1) & 1)
+        member = ids[3] ^ ((index >> 2) & 1)
+        for j in range(planes):
+            plane = ids[0] ^ j
+            spot = jnp.where(side == 0, plane, count - 1 - plane)
+            rows = pl.ds(pl.multiple_of(spot * tok_dev + member * half, half), half)
+            for kind in range(2):
+                columns = pl.ds(pl.multiple_of((kind * KVG + group) * DH, DH), DH)
+                grads[rows, columns] = piece[
+                    j * half : (j + 1) * half, kind * DH : (kind + 1) * DH
+                ]
+    width = raw.shape[1]
+    acc = jnp.zeros((8, width), jnp.float32)
+    for i in range(steps):
+        copies[i].wait()
+        rows = slice(i * tile, (i + 1) * tile)
+        block = jnp.concatenate([held[spot, rows] for spot in range(count)], axis=1)
+        out = jnp.dot(block, grads[...], preferred_element_type=jnp.float32)
+        raw[rows] = out
+        acc += jnp.sum((out * out).reshape(-1, 8, width), axis=0)
+    total = jnp.sum(acc, axis=0, keepdims=True)
+    weights = jnp.sum(squares[...], axis=0, keepdims=True)
+    row = lax.broadcasted_iota(jnp.int32, sums.shape, 0)
+    sums[...] = jnp.where(row == 0, total, weights)
+
+
+def scale_kernel(factor, steps, sums, sums_1, sums_2, sums_3, raw, *refs):
+    outs, helds, sems = refs[:2], refs[2:4], refs[4]
     total = (sums[...] + sums_1[...]) + (sums_2[...] + sums_3[...])
     grad_norm = jnp.sqrt(total[0:1] + EPSILON)
     weight_norm = jnp.sqrt(total[1:2] + EPSILON)
     clip = jnp.minimum(1.0, factor * weight_norm / grad_norm)
-    width = key_out.shape[1]
-    key_out[...] = raw[:, :width] * clip[:, :width]
-    value_out[...] = raw[:, width:] * clip[:, width:]
+    width = outs[0].shape[1]
+    tile = raw.shape[0] // steps
+    copies = []
+    for i in range(steps):
+        rows = pl.ds(i * tile, tile)
+        for kind, (out, held) in enumerate(zip(outs, helds, strict=True)):
+            columns = slice(kind * width, (kind + 1) * width)
+            held[rows] = raw[rows, columns] * clip[:, columns]
+            copy = pltpu.make_async_copy(held.at[rows], out.at[rows], sems.at[2 * i + kind])
+            copy.start()
+            copies.append(copy)
+    for copy in copies:
+        copy.wait()
 
 
 def local_small(
@@ -415,13 +458,13 @@
     bf16, f32 = jnp.bfloat16, jnp.float32
     shape = jax.ShapeDtypeStruct
 
-    def call(kernel, ins, outs, **more):
+    def call(kernel, ins, outs, mib=8, **more):
         return pl.pallas_call(
             kernel,
             out_shape=outs,
             in_specs=ins,
             out_specs=jax.tree.map(lambda _: VMEM, outs),
-            compiler_params=pltpu.CompilerParams(vmem_limit_bytes=32 * 2**20),
+            compiler_params=pltpu.CompilerParams(vmem_limit_bytes=mib * 2**20),
             **more,
         )
 
@@ -435,35 +478,47 @@
                 pairs.append((i * fs + j, (p * SIDES + s) * fs + g * MEMBERS + m))
         return lax.ppermute(x, ("ctx", "fsdp"), pairs)
 
-    def around(x, step):
-        ring = [p * SIDES for p in range(planes)] + [p * SIDES + 1 for p in reversed(range(planes))]
-        pairs = [(ring[i], ring[(i + step) % count]) for i in range(count)]
-        return lax.ppermute(x, "ctx", pairs)
-
-    kv, qd = call(
+    far = [
+        pltpu.with_memory_space_constraint(x, pltpu.HBM)
+        for x in (keys, values, queries, out_grad, positions.reshape(1, tok_dev), hidden)
+    ]
+    kv, qd, turned = call(
         pack_kernel,
-        [SMEM] + [VMEM] * 5,
-        (shape((half, 2 * DH), bf16), shape((2 * tok_dev + 16, width), bf16)),
-    )(ids, keys, values, queries, out_grad, positions.reshape(1, tok_dev))
+        [SMEM] + [ANY] * 6,
+        (
+            shape((half, 2 * DH), bf16),
+            shape((2 * tok_dev + 16, width), bf16),
+            shape(hidden.shape[::-1], bf16),
+        ),
+        scratch_shapes=[
+            pltpu.VMEM((1, tok_dev), jnp.int32),
+            pltpu.VMEM(hidden.shape, bf16),
+            pltpu.SemaphoreType.DMA((6,)),
+        ],
+    )(ids, *far)
     qd_side = move(qd, side=1)
     kv_all = [kv] + [move(kv, plane=j) for j in range(1, planes)]
     qd_member = move(qd, member=1)
+    qd_side = after(qd_side, qd_member, *kv_all)
     qd_both = move(qd_side, member=1)
     qd_all = [qd, qd_member, qd_side, qd_both]
 
-    turned = call(turn_kernel, [VMEM], shape(hidden.shape[::-1], bf16))(hidden)
-    up = down = turned
-    blocks = {0: turned}
-    for step in range(1, count // 2):
-        up, down = around(up, 1), around(down, -1)
-        blocks[count - step], blocks[step] = up, down
-    middle = turned.shape[0] // 2
-    blocks[count // 2] = around(up[:middle], 1)
-    blocks[count] = around(down[middle:], -1)
-
-    squares = call(square_kernel, [VMEM] * 2, shape((8, 2 * key_weight.shape[1]), f32))(
-        key_weight, value_weight
-    )
+    ring = [p * SIDES for p in range(planes)] + [p * SIDES + 1 for p in reversed(range(planes))]
+    turned = lax.all_gather(turned, "ctx", axis_index_groups=[ring])
+    rows = turned.shape[1]
+
+    columns = 2 * KVG * DH
+    steps = 8
+    tile = rows // steps
+    weight = pl.BlockSpec((tile, columns // 2), lambda i: (i, 0))
+    squares = pl.pallas_call(
+        square_kernel,
+        grid=(steps,),
+        out_shape=shape((8, columns), f32),
+        in_specs=[weight] * 2,
+        out_specs=pl.BlockSpec((8, columns), lambda i: (0, 0)),
+        compiler_params=pltpu.CompilerParams(vmem_limit_bytes=8 * 2**20),
+    )(key_weight, value_weight)
 
     tiles = SIDES * MEMBERS * width // DH
     stats = call(
@@ -476,13 +531,15 @@
         functools.partial(grads_kernel, planes),
         [SMEM] * 2 + [VMEM] * (planes + 8),
         tuple(shape((half, 2 * DH), bf16 if j else f32) for j in range(planes))
-        + tuple(shape((tok_dev, width), bf16 if j else f32) for j in range(4)),
+        + (shape((4, planes * half, tok_dev * width // DH), bf16),),
     )(ids, stretch_owner, *kv_all, *qd_all, *stats_all)
-    kv_parts, q_parts = outs[:planes], outs[planes:]
+    kv_parts, slopes = outs[:planes], outs[planes]
     piece = call(sum_kernel, [VMEM] * planes, shape((half, 2 * DH), bf16))(
         kv_parts[0], *[move(kv_parts[j], plane=j) for j in range(1, planes)]
     )
-    piece_all = jnp.concatenate([piece] + [move(piece, plane=j) for j in range(1, planes)], axis=0)
+    piece_all = call(join_kernel, [VMEM] * planes, shape((planes * half, 2 * DH), bf16))(
+        piece, *[move(piece, plane=j) for j in range(1, planes)]
+    )
     near = [
         piece_all,
         move(piece_all, side=1),
@@ -491,6 +548,11 @@
     ]
     pieces = near + [move(part, member=1) for part in near]
 
+    q_parts = call(
+        functools.partial(query_kernel, planes),
+        [VMEM] * (planes + 1) + [ANY],
+        tuple(shape((tok_dev, width), bf16 if j else f32) for j in range(4)),
+    )(*kv_all, slopes, pieces[-1])
     query_grad = call(sum_kernel, [VMEM] * 4, shape((tok_dev, width), bf16))(
         q_parts[0],
         move(q_parts[1], member=1),
@@ -498,39 +560,29 @@
         move(q_parts[3], side=1, member=1),
     )
 
-    columns = 2 * KVG * DH
+    steps = 4
+    raw, sums = call(
+        functools.partial(project_kernel, planes, steps),
+        [SMEM, VMEM, ANY] + [VMEM] * len(pieces),
+        (pltpu.VMEM((rows, columns), f32), shape((8, columns), f32)),
+        mib=24,
+        scratch_shapes=[
+            pltpu.VMEM((total, columns), bf16),
+            pltpu.VMEM(turned.shape, bf16),
+            pltpu.SemaphoreType.DMA((steps,)),
+        ],
+    )(ids, squares, pltpu.with_memory_space_constraint(turned, pltpu.HBM), *pieces)
+    sums_all = [sums, move(sums, member=1), move(sums, group=1), move(sums, group=1, member=1)]
     steps = 8
-    tile = turned.shape[0] // steps
-    block = pl.BlockSpec((tile, tok_dev), lambda i: (i, 0))
-    low = pl.BlockSpec((tile, tok_dev), lambda i: (jnp.minimum(i, steps // 2 - 1), 0))
-    high = pl.BlockSpec((tile, tok_dev), lambda i: (jnp.maximum(i - steps // 2, 0), 0))
-    turned_specs = [low if r == count // 2 else block for r in range(count)] + [high]
-    whole = lambda *dims: pl.BlockSpec(dims, lambda i: (0,) * len(dims))
-    raw, sums = pl.pallas_call(
-        functools.partial(project_kernel, planes),
-        grid=(steps,),
-        out_shape=(shape((turned.shape[0], columns), f32), shape((8, columns), f32)),
-        in_specs=[SMEM, whole(8, columns)]
-        + turned_specs
-        + [whole(planes * half, 2 * DH)] * len(pieces),
-        out_specs=(pl.BlockSpec((tile, columns), lambda i: (i, 0)), whole(8, columns)),
-        scratch_shapes=[
-            pltpu.VMEM((tile, total), bf16),
-            pltpu.VMEM((total, columns), bf16),
-            pltpu.VMEM((8, columns), f32),
-        ],
-        compiler_params=pltpu.CompilerParams(vmem_limit_bytes=32 * 2**20),
-    )(ids, squares, *[blocks[r] for r in range(count + 1)], *pieces)
-    sums_all = [sums, move(sums, member=1), move(sums, group=1), move(sums, group=1, member=1)]
-    out_block = pl.BlockSpec((tile, columns // 2), lambda i: (i, 0))
     key_grad, value_grad = pl.pallas_call(
-        functools.partial(scale_kernel, CLIP_RATE * total),
-        grid=(steps,),
-        out_shape=(shape((turned.shape[0], columns // 2), f32),) * 2,
-        in_specs=[whole(8, columns)] * 4 + [pl.BlockSpec((tile, columns), lambda i: (i, 0))],
-        out_specs=(out_block, out_block),
-        compiler_params=pltpu.CompilerParams(vmem_limit_bytes=32 * 2**20),
-    )(*sums_all, raw)
+        functools.partial(scale_kernel, CLIP_RATE * total, steps),
+        out_shape=(shape((rows, columns // 2), f32),) * 2,
+        in_specs=[VMEM] * 5,
+        out_specs=(ANY, ANY),
+        scratch_shapes=[pltpu.VMEM((rows, columns // 2), f32)] * 2
+        + [pltpu.SemaphoreType.DMA((2 * steps,))],
+        compiler_params=pltpu.CompilerParams(vmem_limit_bytes=24 * 2**20),
+    )(*sums_all, pltpu.with_memory_space_constraint(raw, pltpu.VMEM))
     return (query_grad, key_grad, value_grad)
 
 

time: 118 us -> 89.9 us (0.76)
  waiting for transfers between devices: 63.4 us -> 31.1 us
  between operations: 0.81 us -> 14.2 us
  local copies, waits for them, and re-layouts: 5.88 us -> 0.66 us
  starting transfers between devices: 30.3 us -> 26.7 us
    ppermute x8 -> x0, waiting for transfers between devices: 21.2 us -> none  [around(): return lax.ppermute(x, 'ctx', pairs)]
    ppermute x28, waiting for transfers between devices: 42.2 us -> 31.1 us  [move(): return lax.ppermute(x, ('ctx', 'fsdp'), pairs)]
    ppermute x8 -> x0, starting transfers between devices: 7.23 us -> none  [around(): return lax.ppermute(x, 'ctx', pairs)]
    unnamed x18 -> x6, local copies, waits for them, and re-layouts: 5.84 us -> 0.66 us
    ppermute x28, starting transfers between devices: 23 us -> 26.7 us  [move(): return lax.ppermute(x, ('ctx', 'fsdp'), pairs)]
    pallas_call x1, Pallas kernels: 4.91 us -> 2.3 us  [local_small(): call(functools.partial(grads_kernel, planes), [SMEM] * 2 + [VMEM] * (plan...]
    pallas_call x5 -> x7, Pallas kernels: 10.2 us -> 11.1 us  [the longest x1 4.86 us: local_small(): call(functools.partial(project_kernel, planes, steps), [SMEM, VMEM, ANY]...]
  transfers between devices with their start and end apart: 36 -> 29, of which waited for: 20 -> 14; matrix products, arithmetic and copies ran while one was open for 0% -> 0% of each run, Pallas kernels for 12% -> 13%
where the time goes in v2:
time: 89.9 us; the launch traced here: 89.7 us
  waiting for transfers between devices  31.1 us (35%)
  starting transfers between devices  26.7 us (30%)
  Pallas kernels  16.9 us (19%)
  between operations  14.2 us (16%)
    ppermute x28, waiting for transfers between devices, move(): return lax.ppermute(x, ('ctx', 'fsdp'), pairs)  31.1 us
    ppermute x28, starting transfers between devices, move(): return lax.ppermute(x, ('ctx', 'fsdp'), pairs)  26.7 us
    pallas_call x1, Pallas kernels, local_small(): call(functools.partial(project_kernel, planes, steps), [SMEM, VMEM, ANY]...  4.86 us
    pallas_call x1, Pallas kernels, local_small(): call(pack_kernel, [SMEM] + [ANY] * 6, (shape((half, 2 * DH), bf16), shape...  2.64 us
    pallas_call x1, Pallas kernels, local_small(): call(functools.partial(grads_kernel, planes), [SMEM] * 2 + [VMEM] * (plan...  2.3 us
    pallas_call x1, Pallas kernels, local_small(): pl.pallas_call(functools.partial(scale_kernel, CLIP_RATE * total, steps),...  2.17 us
  transfers between devices with their start and end apart: 29, of which 14 were waited for; matrix products, arithmetic and copies ran while one was open for 0% of the time, Pallas kernels for 13%

profile of v2, /device:TPU:0, one launch (start us, length us, event | category | flops | bytes accessed | tf_op | source)
XLA Modules:
  0.0 89.7 jit_solution(12599011254822182166)
XLA Ops:
  7.3 2.6 %shard_map.112 = (bf16[64,256]{1,0:T(8,128)(2,1)S(1)}, bf16[272,512]{1,0:T(8,128)(2,1)S(1)}, bf16[2048,128]{1,0:T(8,128)(2,1)}) custom-call(s32[4]{0:T(128)S(1)} %pad_add_fusion.ids, bf16[128,256]{1,0:T(8,128)(2,1)} %keys.1, bf16[128,256]{1,0:T(8,128)(2,1)} %values.1, bf16[128,512]{1,0:T(8,128)(2,1)} %queries.1, bf16[128,512]{1,0:T(8,128)(2,1)} %out_grad.1, ...), custom_call_target="tpu_custom_call" | custom-call | tf_op jit(solution)/shard_map/pallas_call | solution.py:485
  10.5 2.6 %collective-permute-start.4 = (bf16[272,512]{1,0:T(8,128)(2,1)S(1)}, bf16[272,512]{1,0:T(8,128)(2,1)S(1)}, u32[]{:S(2)}, u32[]{:S(2)}) collective-permute-start(bf16[272,512]{1,0:T(8,128)(2,1)S(1)} %get-tuple-element.20.refs_4_), channel_id=1, source_target_pairs={{0,4},{1,5},{2,6},{3,7},{4,0},{5,1},{6,2},{7,3},{8,12},{9,13},{10,... | collective-permute-start | bytes 835592 | tf_op jit(solution)/shard_map/ppermute | solution.py:479
  13.1 1.6 %collective-permute-start = (bf16[64,256]{1,0:T(8,128)(2,1)S(1)}, bf16[64,256]{1,0:T(8,128)(2,1)S(1)}, u32[]{:S(2)}, u32[]{:S(2)}) collective-permute-start(bf16[64,256]{1,0:T(8,128)(2,1)S(1)} %get-tuple-element.19.refs_2_.refs_0_), channel_id=1, source_target_pairs={{0,8},{1,9},{2,10},{3,11},{4,12},{5,13},{6,14},{7,15},{8,0},{9,1},... | collective-permute-start | bytes 98312 | tf_op jit(solution)/shard_map/ppermute | solution.py:479
  14.7 2.6 %collective-permute-start.1 = (bf16[64,256]{1,0:T(8,128)(2,1)S(1)}, bf16[64,256]{1,0:T(8,128)(2,1)S(1)}, u32[]{:S(2)}, u32[]{:S(2)}) collective-permute-start(bf16[64,256]{1,0:T(8,128)(2,1)S(1)} %get-tuple-element.19.refs_2_.refs_0_), channel_id=1, source_target_pairs={{0,16},{1,17},{2,18},{3,19},{4,20},{5,21},{6,22},{7,23},{8,24},{9,... | collective-permute-start | bytes 98312 | tf_op jit(solution)/shard_map/ppermute | solution.py:479
  17.5 2.6 %collective-permute-done.1.refs_4_.refs_2_ = bf16[64,256]{1,0:T(8,128)(2,1)S(1)} collective-permute-done((bf16[64,256]{1,0:T(8,128)(2,1)S(1)}, bf16[64,256]{1,0:T(8,128)(2,1)S(1)}, u32[]{:S(2)}, u32[]{:S(2)}) %collective-permute-start.1) | collective-permute-done | bytes 32800 | tf_op jit(solution)/shard_map/ppermute | solution.py:479
  20.1 3.5 %collective-permute-done.2.refs_5_.refs_3_ = bf16[64,256]{1,0:T(8,128)(2,1)S(1)} collective-permute-done((bf16[64,256]{1,0:T(8,128)(2,1)S(1)}, bf16[64,256]{1,0:T(8,128)(2,1)S(1)}, u32[]{:S(2)}, u32[]{:S(2)}) %collective-permute-start.2) | collective-permute-done | bytes 32800 | tf_op jit(solution)/shard_map/ppermute | solution.py:479
  23.6 1.5 %collective-permute-done.5.refs_7_ = bf16[272,512]{1,0:T(8,128)(2,1)S(1)} collective-permute-done((bf16[272,512]{1,0:T(8,128)(2,1)S(1)}, bf16[272,512]{1,0:T(8,128)(2,1)S(1)}, u32[]{:S(2)}, u32[]{:S(2)}) %collective-permute-start.5) | collective-permute-done | bytes 278560 | tf_op jit(solution)/shard_map/ppermute | solution.py:479
  25.8 1.7 %shard_map.114.refs_8_ = f32[48,128]{1,0:T(8,128)S(1)} custom-call(s32[4]{0:T(128)S(1)} %pad_add_fusion.ids, s32[8]{0:T(128)S(1)} %copy-done.2, bf16[64,256]{1,0:T(8,128)(2,1)S(1)} %get-tuple-element.19.refs_2_.refs_0_, bf16[64,256]{1,0:T(8,128)(2,1)S(1)} %collective-permute-done.refs_3_.refs_1_, bf16[64,256]{1,0:T(8,128)(2,1)S(1)} %collective-permute-done.1.refs_4_.refs_2_, ...), custom_call_target="tpu_custom_call" | custom-call | tf_op jit(solution)/shard_map/pallas_call | solution.py:524
  27.8 1.6 %collective-permute-start.8 = (f32[48,128]{1,0:T(8,128)S(1)}, f32[48,128]{1,0:T(8,128)S(1)}, u32[]{:S(2)}, u32[]{:S(2)}) collective-permute-start(f32[48,128]{1,0:T(8,128)S(1)} %shard_map.114.refs_8_), channel_id=1, source_target_pairs={{0,5},{1,4},{2,7},{3,6},{4,1},{5,0},{6,3},{7,2},{8,13},{9,12},{10,... | collective-permute-start | bytes 73736 | tf_op jit(solution)/shard_map/ppermute | solution.py:479
  29.5 2.9 %collective-permute-done.7.refs_10_ = f32[48,128]{1,0:T(8,128)S(1)} collective-permute-done((f32[48,128]{1,0:T(8,128)S(1)}, f32[48,128]{1,0:T(8,128)S(1)}, u32[]{:S(2)}, u32[]{:S(2)}) %collective-permute-start.7) | collective-permute-done | bytes 24608 | tf_op jit(solution)/shard_map/ppermute | solution.py:479
  32.6 2.3 %shard_map.115 = (f32[64,256]{1,0:T(8,128)S(1)}, bf16[64,256]{1,0:T(8,128)(2,1)S(1)}, bf16[64,256]{1,0:T(8,128)(2,1)S(1)}, bf16[64,256]{1,0:T(8,128)(2,1)S(1)}, bf16[4,256,512]{2,1,0:T(8,128)(2,1)S(1)}) custom-call(s32[4]{0:T(128)S(1)} %pad_add_fusion.ids, s32[8]{0:T(128)S(1)} %copy-done.2, bf16[64,256]{1,0:T(8,128)(2,1)S(1)} %get-tuple-element.19.refs_2_.refs_0_, ...), custom_call_target="tpu_custom_call" | custom-call | tf_op jit(solution)/shard_map/pallas_call | solution.py:530
  35.0 3.1 %collective-permute-start.10 = (bf16[64,256]{1,0:T(8,128)(2,1)S(1)}, bf16[64,256]{1,0:T(8,128)(2,1)S(1)}, u32[]{:S(2)}, u32[]{:S(2)}) collective-permute-start(bf16[64,256]{1,0:T(8,128)(2,1)S(1)} %get-tuple-element.24), channel_id=1, source_target_pairs={{0,16},{1,17},{2,18},{3,19},{4,20},{5,21},{6,22},{7,23},{8,24},{9,... | collective-permute-start | bytes 98312 | tf_op jit(solution)/shard_map/ppermute | solution.py:479
  38.1 1.3 %collective-permute-start.11 = (bf16[64,256]{1,0:T(8,128)(2,1)S(1)}, bf16[64,256]{1,0:T(8,128)(2,1)S(1)}, u32[]{:S(2)}, u32[]{:S(2)}) collective-permute-start(bf16[64,256]{1,0:T(8,128)(2,1)S(1)} %get-tuple-element.25), channel_id=1, source_target_pairs={{0,24},{1,25},{2,26},{3,27},{4,28},{5,29},{6,30},{7,31},{8,16},{9,... | collective-permute-start | bytes 98312 | tf_op jit(solution)/shard_map/ppermute | solution.py:479
  41.3 3.1 %collective-permute-done.11.refs_3_ = bf16[64,256]{1,0:T(8,128)(2,1)S(1)} collective-permute-done((bf16[64,256]{1,0:T(8,128)(2,1)S(1)}, bf16[64,256]{1,0:T(8,128)(2,1)S(1)}, u32[]{:S(2)}, u32[]{:S(2)}) %collective-permute-start.11) | collective-permute-done | bytes 32800 | tf_op jit(solution)/shard_map/ppermute | solution.py:479
  44.6 2.0 %collective-permute-start.13 = (bf16[64,256]{1,0:T(8,128)(2,1)S(1)}, bf16[64,256]{1,0:T(8,128)(2,1)S(1)}, u32[]{:S(2)}, u32[]{:S(2)}) collective-permute-start(bf16[64,256]{1,0:T(8,128)(2,1)S(1)} %shard_map.116.refs_0_), channel_id=1, source_target_pairs={{0,16},{1,17},{2,18},{3,19},{4,20},{5,21},{6,22},{7,23},{8,24},{9,... | collective-permute-start | bytes 98312 | tf_op jit(solution)/shard_map/ppermute | solution.py:479
  46.6 2.3 %collective-permute-start.14 = (bf16[64,256]{1,0:T(8,128)(2,1)S(1)}, bf16[64,256]{1,0:T(8,128)(2,1)S(1)}, u32[]{:S(2)}, u32[]{:S(2)}) collective-permute-start(bf16[64,256]{1,0:T(8,128)(2,1)S(1)} %shard_map.116.refs_0_), channel_id=1, source_target_pairs={{0,24},{1,25},{2,26},{3,27},{4,28},{5,29},{6,30},{7,31},{8,16},{9,... | collective-permute-start | bytes 98312 | tf_op jit(solution)/shard_map/ppermute | solution.py:479
  49.1 1.3 %collective-permute-done.13.refs_2_ = bf16[64,256]{1,0:T(8,128)(2,1)S(1)} collective-permute-done((bf16[64,256]{1,0:T(8,128)(2,1)S(1)}, bf16[64,256]{1,0:T(8,128)(2,1)S(1)}, u32[]{:S(2)}, u32[]{:S(2)}) %collective-permute-start.13) | collective-permute-done | bytes 32800 | tf_op jit(solution)/shard_map/ppermute | solution.py:479
  50.4 2.5 %collective-permute-done.14.refs_3_ = bf16[64,256]{1,0:T(8,128)(2,1)S(1)} collective-permute-done((bf16[64,256]{1,0:T(8,128)(2,1)S(1)}, bf16[64,256]{1,0:T(8,128)(2,1)S(1)}, u32[]{:S(2)}, u32[]{:S(2)}) %collective-permute-start.14) | collective-permute-done | bytes 32800 | tf_op jit(solution)/shard_map/ppermute | solution.py:479
  53.0 2.2 %collective-permute-start.15 = (bf16[256,256]{1,0:T(8,128)(2,1)S(1)}, bf16[256,256]{1,0:T(8,128)(2,1)S(1)}, u32[]{:S(2)}, u32[]{:S(2)}) collective-permute-start(bf16[256,256]{1,0:T(8,128)(2,1)S(1)} %shard_map.117.refs_0_), channel_id=1, source_target_pairs={{0,6},{1,7},{2,4},{3,5},{4,2},{5,3},{6,0},{7,1},{8,14},{9,15},{10,... | collective-permute-start | bytes 393224 | tf_op jit(solution)/shard_map/ppermute | solution.py:479
  56.5 6.5 %collective-permute-done.15.refs_3_ = bf16[256,256]{1,0:T(8,128)(2,1)S(1)} collective-permute-done((bf16[256,256]{1,0:T(8,128)(2,1)S(1)}, bf16[256,256]{1,0:T(8,128)(2,1)S(1)}, u32[]{:S(2)}, u32[]{:S(2)}) %collective-permute-start.15) | collective-permute-done | bytes 131104 | tf_op jit(solution)/shard_map/ppermute | solution.py:479
  63.6 4.1 %collective-permute-done.20.refs_1_ = bf16[256,256]{1,0:T(8,128)(2,1)S(1)} collective-permute-done((bf16[256,256]{1,0:T(8,128)(2,1)S(1)}, bf16[256,256]{1,0:T(8,128)(2,1)S(1)}, u32[]{:S(2)}, u32[]{:S(2)}) %collective-permute-start.20) | collective-permute-done | bytes 131104 | tf_op jit(solution)/shard_map/ppermute | solution.py:479
  71.6 4.9 %shard_map.121 = (f32[2048,512]{1,0:T(8,128)S(1)}, f32[8,512]{1,0:T(8,128)S(1)}) custom-call(s32[4]{0:T(128)S(1)} %pad_add_fusion.ids, f32[8,512]{1,0:T(8,128)S(1)} %shard_map.120.squares, bf16[8,2048,128]{2,1,0:T(8,128)(2,1)} %bitcast.6, bf16[256,256]{1,0:T(8,128)(2,1)S(1)} %shard_map.117.refs_0_, bf16[256,256]{1,0:T(8,128)(2,1)S(1)} %collective-permute-done.20.refs_1_, ...), custom_call_target="tpu_custom_call" | custom-call | tf_op jit(solution)/shard_map/pallas_call | solution.py:564
  78.4 1.7 %shard_map.119 = bf16[128,512]{1,0:T(8,128)(2,1)} custom-call(f32[128,512]{1,0:T(8,128)S(1)} %get-tuple-element.26.refs_0_, bf16[128,512]{1,0:T(8,128)(2,1)} %collective-permute-done.17.refs_1_, bf16[128,512]{1,0:T(8,128)(2,1)} %collective-permute-done.18.refs_2_, bf16[128,512]{1,0:T(8,128)(2,1)} %collective-permute-done.19.refs_3_), custom_call_target="tpu_custom_call" | custom-call | tf_op jit(solution)/shard_map/pallas_call | solution.py:556
  80.7 2.2 %shard_map.122 = (f32[2048,256]{1,0:T(8,128)}, f32[2048,256]{1,0:T(8,128)}) custom-call(f32[8,512]{1,0:T(8,128)S(1)} %get-tuple-element.31.sums, f32[8,512]{1,0:T(8,128)S(1)} %collective-permute-done.25.sums_1, f32[8,512]{1,0:T(8,128)S(1)} %collective-permute-done.26.sums_2, f32[8,512]{1,0:T(8,128)S(1)} %collective-permute-done.27.sums_3, ...), custom_call_target="tpu_custom_call" | custom-call | tf_op jit(solution)/shard_map/pallas_call | solution.py:577
  (53 shorter events, 12.7 us)
Async XLA Ops:
  7.2 64.4 %all-gather.3.cloned.1.call-start = ((), (), s32[]{:S(2)}) async-start(), calls=%async_computation | async-start | bytes 4718592 | tf_op jit(solution)/shard_map/all_gather | solution.py:507
  10.0 13.5 %collective-permute-start.3 = (bf16[272,512]{1,0:T(8,128)(2,1)S(1)}, bf16[272,512]{1,0:T(8,128)(2,1)S(1)}, u32[]{:S(2)}, u32[]{:S(2)}) collective-permute-start(bf16[272,512]{1,0:T(8,128)(2,1)S(1)} %get-tuple-element.20.refs_4_), channel_id=1, source_target_pairs={{0,1},{1,0},{2,3},{3,2},{4,5},{5,4},{6,7},{7,6},{8,9},{9,8},{10,11... | collective-permute-start | bytes 835592 | tf_op jit(solution)/shard_map/ppermute | solution.py:479
  10.5 13.0 %collective-permute-start.4 = (bf16[272,512]{1,0:T(8,128)(2,1)S(1)}, bf16[272,512]{1,0:T(8,128)(2,1)S(1)}, u32[]{:S(2)}, u32[]{:S(2)}) collective-permute-start(bf16[272,512]{1,0:T(8,128)(2,1)S(1)} %get-tuple-element.20.refs_4_), channel_id=1, source_target_pairs={{0,4},{1,5},{2,6},{3,7},{4,0},{5,1},{6,2},{7,3},{8,12},{9,13},{10,... | collective-permute-start | bytes 835592 | tf_op jit(solution)/shard_map/ppermute | solution.py:479
  13.1 4.4 %collective-permute-start = (bf16[64,256]{1,0:T(8,128)(2,1)S(1)}, bf16[64,256]{1,0:T(8,128)(2,1)S(1)}, u32[]{:S(2)}, u32[]{:S(2)}) collective-permute-start(bf16[64,256]{1,0:T(8,128)(2,1)S(1)} %get-tuple-element.19.refs_2_.refs_0_), channel_id=1, source_target_pairs={{0,8},{1,9},{2,10},{3,11},{4,12},{5,13},{6,14},{7,15},{8,0},{9,1},... | collective-permute-start | bytes 98312 | tf_op jit(solution)/shard_map/ppermute | solution.py:479
  14.7 5.4 %collective-permute-start.1 = (bf16[64,256]{1,0:T(8,128)(2,1)S(1)}, bf16[64,256]{1,0:T(8,128)(2,1)S(1)}, u32[]{:S(2)}, u32[]{:S(2)}) collective-permute-start(bf16[64,256]{1,0:T(8,128)(2,1)S(1)} %get-tuple-element.19.refs_2_.refs_0_), channel_id=1, source_target_pairs={{0,16},{1,17},{2,18},{3,19},{4,20},{5,21},{6,22},{7,23},{8,24},{9,... | collective-permute-start | bytes 98312 | tf_op jit(solution)/shard_map/ppermute | solution.py:479
  17.3 6.3 %collective-permute-start.2 = (bf16[64,256]{1,0:T(8,128)(2,1)S(1)}, bf16[64,256]{1,0:T(8,128)(2,1)S(1)}, u32[]{:S(2)}, u32[]{:S(2)}) collective-permute-start(bf16[64,256]{1,0:T(8,128)(2,1)S(1)} %get-tuple-element.19.refs_2_.refs_0_), channel_id=1, source_target_pairs={{0,24},{1,25},{2,26},{3,27},{4,28},{5,29},{6,30},{7,31},{8,16},{9,... | collective-permute-start | bytes 98312 | tf_op jit(solution)/shard_map/ppermute | solution.py:479
  27.8 4.6 %collective-permute-start.7 = (f32[48,128]{1,0:T(8,128)S(1)}, f32[48,128]{1,0:T(8,128)S(1)}, u32[]{:S(2)}, u32[]{:S(2)}) collective-permute-start(f32[48,128]{1,0:T(8,128)S(1)} %shard_map.114.refs_8_), channel_id=1, source_target_pairs={{0,4},{1,5},{2,6},{3,7},{4,0},{5,1},{6,2},{7,3},{8,12},{9,13},{10,... | collective-permute-start | bytes 73736 | tf_op jit(solution)/shard_map/ppermute | solution.py:479
  27.8 4.8 %collective-permute-start.8 = (f32[48,128]{1,0:T(8,128)S(1)}, f32[48,128]{1,0:T(8,128)S(1)}, u32[]{:S(2)}, u32[]{:S(2)}) collective-permute-start(f32[48,128]{1,0:T(8,128)S(1)} %shard_map.114.refs_8_), channel_id=1, source_target_pairs={{0,5},{1,4},{2,7},{3,6},{4,1},{5,0},{6,3},{7,2},{8,13},{9,12},{10,... | collective-permute-start | bytes 73736 | tf_op jit(solution)/shard_map/ppermute | solution.py:479
  34.9 5.4 %collective-permute-start.9 = (bf16[64,256]{1,0:T(8,128)(2,1)S(1)}, bf16[64,256]{1,0:T(8,128)(2,1)S(1)}, u32[]{:S(2)}, u32[]{:S(2)}) collective-permute-start(bf16[64,256]{1,0:T(8,128)(2,1)S(1)} %get-tuple-element.23), channel_id=1, source_target_pairs={{0,8},{1,9},{2,10},{3,11},{4,12},{5,13},{6,14},{7,15},{8,0},{9,1},... | collective-permute-start | bytes 98312 | tf_op jit(solution)/shard_map/ppermute | solution.py:479
  35.0 6.4 %collective-permute-start.10 = (bf16[64,256]{1,0:T(8,128)(2,1)S(1)}, bf16[64,256]{1,0:T(8,128)(2,1)S(1)}, u32[]{:S(2)}, u32[]{:S(2)}) collective-permute-start(bf16[64,256]{1,0:T(8,128)(2,1)S(1)} %get-tuple-element.24), channel_id=1, source_target_pairs={{0,16},{1,17},{2,18},{3,19},{4,20},{5,21},{6,22},{7,23},{8,24},{9,... | collective-permute-start | bytes 98312 | tf_op jit(solution)/shard_map/ppermute | solution.py:479
  38.1 6.4 %collective-permute-start.11 = (bf16[64,256]{1,0:T(8,128)(2,1)S(1)}, bf16[64,256]{1,0:T(8,128)(2,1)S(1)}, u32[]{:S(2)}, u32[]{:S(2)}) collective-permute-start(bf16[64,256]{1,0:T(8,128)(2,1)S(1)} %get-tuple-element.25), channel_id=1, source_target_pairs={{0,24},{1,25},{2,26},{3,27},{4,28},{5,29},{6,30},{7,31},{8,16},{9,... | collective-permute-start | bytes 98312 | tf_op jit(solution)/shard_map/ppermute | solution.py:479
  44.5 4.7 %collective-permute-start.12 = (bf16[64,256]{1,0:T(8,128)(2,1)S(1)}, bf16[64,256]{1,0:T(8,128)(2,1)S(1)}, u32[]{:S(2)}, u32[]{:S(2)}) collective-permute-start(bf16[64,256]{1,0:T(8,128)(2,1)S(1)} %shard_map.116.refs_0_), channel_id=1, source_target_pairs={{0,8},{1,9},{2,10},{3,11},{4,12},{5,13},{6,14},{7,15},{8,0},{9,1},... | collective-permute-start | bytes 98312 | tf_op jit(solution)/shard_map/ppermute | solution.py:479
  44.6 5.9 %collective-permute-start.13 = (bf16[64,256]{1,0:T(8,128)(2,1)S(1)}, bf16[64,256]{1,0:T(8,128)(2,1)S(1)}, u32[]{:S(2)}, u32[]{:S(2)}) collective-permute-start(bf16[64,256]{1,0:T(8,128)(2,1)S(1)} %shard_map.116.refs_0_), channel_id=1, source_target_pairs={{0,16},{1,17},{2,18},{3,19},{4,20},{5,21},{6,22},{7,23},{8,24},{9,... | collective-permute-start | bytes 98312 | tf_op jit(solution)/shard_map/ppermute | solution.py:479
  46.6 6.4 %collective-permute-start.14 = (bf16[64,256]{1,0:T(8,128)(2,1)S(1)}, bf16[64,256]{1,0:T(8,128)(2,1)S(1)}, u32[]{:S(2)}, u32[]{:S(2)}) collective-permute-start(bf16[64,256]{1,0:T(8,128)(2,1)S(1)} %shard_map.116.refs_0_), channel_id=1, source_target_pairs={{0,24},{1,25},{2,26},{3,27},{4,28},{5,29},{6,30},{7,31},{8,16},{9,... | collective-permute-start | bytes 98312 | tf_op jit(solution)/shard_map/ppermute | solution.py:479
  53.0 10.1 %collective-permute-start.15 = (bf16[256,256]{1,0:T(8,128)(2,1)S(1)}, bf16[256,256]{1,0:T(8,128)(2,1)S(1)}, u32[]{:S(2)}, u32[]{:S(2)}) collective-permute-start(bf16[256,256]{1,0:T(8,128)(2,1)S(1)} %shard_map.117.refs_0_), channel_id=1, source_target_pairs={{0,6},{1,7},{2,4},{3,5},{4,2},{5,3},{6,0},{7,1},{8,14},{9,15},{10,... | collective-permute-start | bytes 393224 | tf_op jit(solution)/shard_map/ppermute | solution.py:479
  55.2 12.5 %collective-permute-start.20 = (bf16[256,256]{1,0:T(8,128)(2,1)S(1)}, bf16[256,256]{1,0:T(8,128)(2,1)S(1)}, u32[]{:S(2)}, u32[]{:S(2)}) collective-permute-start(bf16[256,256]{1,0:T(8,128)(2,1)S(1)} %shard_map.117.refs_0_), channel_id=1, source_target_pairs={{0,4},{1,5},{2,6},{3,7},{4,0},{5,1},{6,2},{7,3},{8,12},{9,13},{10,... | collective-permute-start | bytes 393224 | tf_op jit(solution)/shard_map/ppermute | solution.py:479
  56.1 11.6 %collective-permute-start.21 = (bf16[256,256]{1,0:T(8,128)(2,1)S(1)}, bf16[256,256]{1,0:T(8,128)(2,1)S(1)}, u32[]{:S(2)}, u32[]{:S(2)}) collective-permute-start(bf16[256,256]{1,0:T(8,128)(2,1)S(1)} %shard_map.117.refs_0_), channel_id=1, source_target_pairs={{0,2},{1,3},{2,0},{3,1},{4,6},{5,7},{6,4},{7,5},{8,10},{9,11},{10,... | collective-permute-start | bytes 393224 | tf_op jit(solution)/shard_map/ppermute | solution.py:479
  63.1 5.1 %collective-permute-start.16 = (bf16[256,256]{1,0:T(8,128)(2,1)S(1)}, bf16[256,256]{1,0:T(8,128)(2,1)S(1)}, u32[]{:S(2)}, u32[]{:S(2)}) collective-permute-start(bf16[256,256]{1,0:T(8,128)(2,1)S(1)} %collective-permute-done.15.refs_3_), channel_id=1, source_target_pairs={{0,1},{1,0},{2,3},{3,2},{4,5},{5,4},{6,7},{7,6},{8,9},{9,8},{10,11... | collective-permute-start | bytes 393224 | tf_op jit(solution)/shard_map/ppermute | solution.py:479
  63.1 7.4 %collective-permute-start.22 = (bf16[256,256]{1,0:T(8,128)(2,1)S(1)}, bf16[256,256]{1,0:T(8,128)(2,1)S(1)}, u32[]{:S(2)}, u32[]{:S(2)}) collective-permute-start(bf16[256,256]{1,0:T(8,128)(2,1)S(1)} %shard_map.117.refs_0_), channel_id=1, source_target_pairs={{0,1},{1,0},{2,3},{3,2},{4,5},{5,4},{6,7},{7,6},{8,9},{9,8},{10,11... | collective-permute-start | bytes 393224 | tf_op jit(solution)/shard_map/ppermute | solution.py:479
  67.7 3.8 %collective-permute-start.24 = (bf16[256,256]{1,0:T(8,128)(2,1)S(1)}, bf16[256,256]{1,0:T(8,128)(2,1)S(1)}, u32[]{:S(2)}, u32[]{:S(2)}) collective-permute-start(bf16[256,256]{1,0:T(8,128)(2,1)S(1)} %collective-permute-done.21.refs_2_), channel_id=1, source_target_pairs={{0,1},{1,0},{2,3},{3,2},{4,5},{5,4},{6,7},{7,6},{8,9},{9,8},{10,11... | collective-permute-start | bytes 393224 | tf_op jit(solution)/shard_map/ppermute | solution.py:479
  69.3 8.0 %collective-permute-start.17 = (bf16[128,512]{1,0:T(8,128)(2,1)}, bf16[128,512]{1,0:T(8,128)(2,1)}, u32[]{:S(2)}, u32[]{:S(2)}) collective-permute-start(bf16[128,512]{1,0:T(8,128)(2,1)} %get-tuple-element.27), channel_id=1, source_target_pairs={{0,1},{1,0},{2,3},{3,2},{4,5},{5,4},{6,7},{7,6},{8,9},{9,8},{10,11... | collective-permute-start | bytes 393224 | tf_op jit(solution)/shard_map/ppermute | solution.py:479
  69.3 9.0 %collective-permute-start.18 = (bf16[128,512]{1,0:T(8,128)(2,1)}, bf16[128,512]{1,0:T(8,128)(2,1)}, u32[]{:S(2)}, u32[]{:S(2)}) collective-permute-start(bf16[128,512]{1,0:T(8,128)(2,1)} %get-tuple-element.28), channel_id=1, source_target_pairs={{0,4},{1,5},{2,6},{3,7},{4,0},{5,1},{6,2},{7,3},{8,12},{9,13},{10,... | collective-permute-start | bytes 393224 | tf_op jit(solution)/shard_map/ppermute | solution.py:479
  70.5 7.9 %collective-permute-start.19 = (bf16[128,512]{1,0:T(8,128)(2,1)}, bf16[128,512]{1,0:T(8,128)(2,1)}, u32[]{:S(2)}, u32[]{:S(2)}) collective-permute-start(bf16[128,512]{1,0:T(8,128)(2,1)} %get-tuple-element.29), channel_id=1, source_target_pairs={{0,5},{1,4},{2,7},{3,6},{4,1},{5,0},{6,3},{7,2},{8,13},{9,12},{10,... | collective-permute-start | bytes 393224 | tf_op jit(solution)/shard_map/ppermute | solution.py:479
  76.8 3.9 %collective-permute-start.26 = (f32[8,512]{1,0:T(8,128)S(1)}, f32[8,512]{1,0:T(8,128)S(1)}, u32[]{:S(2)}, u32[]{:S(2)}) collective-permute-start(f32[8,512]{1,0:T(8,128)S(1)} %get-tuple-element.31.sums), channel_id=1, source_target_pairs={{0,2},{1,3},{2,0},{3,1},{4,6},{5,7},{6,4},{7,5},{8,10},{9,11},{10,... | collective-permute-start | bytes 49160 | tf_op jit(solution)/shard_map/ppermute | solution.py:479
  (8 other events, 143.1 us)
Sparse Core Ops, SparseCore 0:
  10.1 58.9 all-gather.2

commit v3 on v2

--- a/solution.py
+++ b/solution.py
@@ -183,7 +183,7 @@
 
 
 def pack_kernel(
-    ids, keys, values, queries, out_grad, positions, hidden, kv_out, qd_out, turned, place, held, sems
+    ids, keys, values, queries, out_grad, positions, kv_out, qd_out, place, sems
 ):
     half = kv_out.shape[0]
     tok_dev = queries.shape[0]
@@ -193,7 +193,6 @@
         pltpu.make_async_copy(source, target, sems.at[i])
         for i, (source, target) in enumerate(
             (
-                (hidden, held),
                 (positions, place),
                 (keys.at[rows, columns], kv_out.at[:, :DH]),
                 (values.at[rows, columns], kv_out.at[:, DH:]),
@@ -208,14 +207,12 @@
     if rest > 0:
         qd_out[2 * tok_dev :, tok_dev:] = jnp.zeros((qd_out.shape[0] - 2 * tok_dev, rest), jnp.bfloat16)
     copies[0].wait()
-    turned[...] = held[...].T
-    copies[1].wait()
     high = place[...] // DIGIT
     low = place[...] - high * DIGIT
     pad = jnp.zeros((qd_out.shape[0] - 2 * tok_dev - 2, tok_dev), jnp.float32)
     digits = jnp.concatenate([high.astype(jnp.float32), low.astype(jnp.float32), pad], axis=0)
     qd_out[2 * tok_dev :, :tok_dev] = digits.astype(jnp.bfloat16)
-    for copy in copies[2:]:
+    for copy in copies[1:]:
         copy.wait()
 
 
@@ -383,14 +380,14 @@
     out[:, width:] += jnp.sum((v * v).reshape(-1, 8, width), axis=0)
 
 
-def project_kernel(planes, steps, ids, squares, turned, *refs):
+def project_kernel(planes, steps, ids, squares, hidden, *refs):
     count = planes * SIDES
     pieces, (raw, sums, grads, held, sems) = refs[:8], refs[8:]
-    tok_dev = turned.shape[2]
+    tok_dev = hidden.shape[1]
     half = tok_dev // 2
     tile = raw.shape[0] // steps
     copies = [
-        pltpu.make_async_copy(turned.at[:, rows], held.at[:, rows], sems.at[i])
+        pltpu.make_async_copy(hidden.at[:, :, rows], held.at[:, :, rows], sems.at[i])
         for i, rows in enumerate(pl.ds(i * tile, tile) for i in range(steps))
     ]
     for copy in copies:
@@ -413,8 +410,10 @@
     for i in range(steps):
         copies[i].wait()
         rows = slice(i * tile, (i + 1) * tile)
-        block = jnp.concatenate([held[spot, rows] for spot in range(count)], axis=1)
-        out = jnp.dot(block, grads[...], preferred_element_type=jnp.float32)
+        block = held[:, :, rows].reshape(count * tok_dev, tile)
+        out = lax.dot_general(
+            block, grads[...], CONTRACT_FIRST, preferred_element_type=jnp.float32
+        )
         raw[rows] = out
         acc += jnp.sum((out * out).reshape(-1, 8, width), axis=0)
     total = jnp.sum(acc, axis=0, keepdims=True)
@@ -478,34 +477,9 @@
                 pairs.append((i * fs + j, (p * SIDES + s) * fs + g * MEMBERS + m))
         return lax.ppermute(x, ("ctx", "fsdp"), pairs)
 
-    far = [
-        pltpu.with_memory_space_constraint(x, pltpu.HBM)
-        for x in (keys, values, queries, out_grad, positions.reshape(1, tok_dev), hidden)
-    ]
-    kv, qd, turned = call(
-        pack_kernel,
-        [SMEM] + [ANY] * 6,
-        (
-            shape((half, 2 * DH), bf16),
-            shape((2 * tok_dev + 16, width), bf16),
-            shape(hidden.shape[::-1], bf16),
-        ),
-        scratch_shapes=[
-            pltpu.VMEM((1, tok_dev), jnp.int32),
-            pltpu.VMEM(hidden.shape, bf16),
-            pltpu.SemaphoreType.DMA((6,)),
-        ],
-    )(ids, *far)
-    qd_side = move(qd, side=1)
-    kv_all = [kv] + [move(kv, plane=j) for j in range(1, planes)]
-    qd_member = move(qd, member=1)
-    qd_side = after(qd_side, qd_member, *kv_all)
-    qd_both = move(qd_side, member=1)
-    qd_all = [qd, qd_member, qd_side, qd_both]
-
     ring = [p * SIDES for p in range(planes)] + [p * SIDES + 1 for p in reversed(range(planes))]
-    turned = lax.all_gather(turned, "ctx", axis_index_groups=[ring])
-    rows = turned.shape[1]
+    gathered = lax.all_gather(hidden, "ctx", axis_index_groups=[ring])
+    rows = hidden.shape[1]
 
     columns = 2 * KVG * DH
     steps = 8
@@ -519,6 +493,26 @@
         out_specs=pl.BlockSpec((8, columns), lambda i: (0, 0)),
         compiler_params=pltpu.CompilerParams(vmem_limit_bytes=8 * 2**20),
     )(key_weight, value_weight)
+
+    far = [
+        pltpu.with_memory_space_constraint(x, pltpu.HBM)
+        for x in (keys, values, queries, out_grad, positions.reshape(1, tok_dev))
+    ]
+    kv, qd = call(
+        pack_kernel,
+        [SMEM] + [ANY] * 5,
+        (shape((half, 2 * DH), bf16), shape((2 * tok_dev + 16, width), bf16)),
+        scratch_shapes=[
+            pltpu.VMEM((1, tok_dev), jnp.int32),
+            pltpu.SemaphoreType.DMA((5,)),
+        ],
+    )(ids, *far)
+    qd_side = move(qd, side=1)
+    kv_all = [kv] + [move(kv, plane=j) for j in range(1, planes)]
+    qd_member = move(qd, member=1)
+    qd_side = after(qd_side, qd_member, squares, *kv_all)
+    qd_both = move(qd_side, member=1)
+    qd_all = [qd, qd_member, qd_side, qd_both]
 
     tiles = SIDES * MEMBERS * width // DH
     stats = call(
@@ -540,19 +534,15 @@
     piece_all = call(join_kernel, [VMEM] * planes, shape((planes * half, 2 * DH), bf16))(
         piece, *[move(piece, plane=j) for j in range(1, planes)]
     )
-    near = [
-        piece_all,
-        move(piece_all, side=1),
-        move(piece_all, group=1),
-        move(piece_all, side=1, group=1),
-    ]
+    piece_side = move(piece_all, side=1)
+    near = [piece_all, piece_side, move(piece_all, group=1), move(piece_side, group=1)]
     pieces = near + [move(part, member=1) for part in near]
 
     q_parts = call(
         functools.partial(query_kernel, planes),
         [VMEM] * (planes + 1) + [ANY],
         tuple(shape((tok_dev, width), bf16 if j else f32) for j in range(4)),
-    )(*kv_all, slopes, pieces[-1])
+    )(*kv_all, slopes, near[2])
     query_grad = call(sum_kernel, [VMEM] * 4, shape((tok_dev, width), bf16))(
         q_parts[0],
         move(q_parts[1], member=1),
@@ -568,10 +558,10 @@
         mib=24,
         scratch_shapes=[
             pltpu.VMEM((total, columns), bf16),
-            pltpu.VMEM(turned.shape, bf16),
+            pltpu.VMEM(gathered.shape, bf16),
             pltpu.SemaphoreType.DMA((steps,)),
         ],
-    )(ids, squares, pltpu.with_memory_space_constraint(turned, pltpu.HBM), *pieces)
+    )(ids, squares, pltpu.with_memory_space_constraint(gathered, pltpu.HBM), *pieces)
     sums_all = [sums, move(sums, member=1), move(sums, group=1), move(sums, group=1, member=1)]
     steps = 8
     key_grad, value_grad = pl.pallas_call(

time: 89.9 us -> 85.5 us (0.951)
  waiting for transfers between devices: 31.1 us -> 25.8 us
  Pallas kernels: 16.9 us -> 14.3 us
  local copies, waits for them, and re-layouts: 0.66 us -> 3.1 us
  starting transfers between devices: 26.7 us -> 27.9 us
    ppermute x28, waiting for transfers between devices: 31.1 us -> 25.1 us  [move(): return lax.ppermute(x, ('ctx', 'fsdp'), pairs)]
    unnamed x6, local copies, waits for them, and re-layouts: 0.66 us -> 3.1 us
    ppermute x28, starting transfers between devices: 26.7 us -> 27.8 us  [move(): return lax.ppermute(x, ('ctx', 'fsdp'), pairs)]
    pallas_call x1, Pallas kernels: 2.64 us -> 1.6 us  [local_small(): call(pack_kernel, [SMEM] + [ANY] * 5, (shape((half, 2 * DH), bf16), shape...]
    pallas_call x1, Pallas kernels: 1.75 us -> 0.72 us  [local_small(): call(sum_kernel, [VMEM] * 4, shape((tok_dev, width), bf16))]
  transfers between devices with their start and end apart: 29 -> 29, of which waited for: 14 -> 14; matrix products, arithmetic and copies ran while one was open for 0% -> 0% of each run, Pallas kernels for 13% -> 14%
where the time goes in v3:
time: 85.5 us; the launch traced here: 85.3 us
  starting transfers between devices  27.9 us (33%)
  waiting for transfers between devices  25.8 us (30%)
  Pallas kernels  14.3 us (17%)
  between operations  14.2 us (17%)
  local copies, waits for them, and re-layouts  3.1 us (4%)
    ppermute x28, starting transfers between devices, move(): return lax.ppermute(x, ('ctx', 'fsdp'), pairs)  27.8 us
    ppermute x28, waiting for transfers between devices, move(): return lax.ppermute(x, ('ctx', 'fsdp'), pairs)  25.1 us
    pallas_call x1, Pallas kernels, local_small(): call(functools.partial(project_kernel, planes, steps), [SMEM, VMEM, ANY]...  5 us
    unnamed x6, local copies, waits for them, and re-layouts  3.1 us
    pallas_call x1, Pallas kernels, local_small(): call(functools.partial(grads_kernel, planes), [SMEM] * 2 + [VMEM] * (plan...  2.27 us
    pallas_call x1, Pallas kernels, local_small(): pl.pallas_call(functools.partial(scale_kernel, CLIP_RATE * total, steps),...  2.17 us
  transfers between devices with their start and end apart: 29, of which 14 were waited for; matrix products, arithmetic and copies ran while one was open for 0% of the time, Pallas kernels for 14%

profile of v3, /device:TPU:0, one launch (start us, length us, event | category | flops | bytes accessed | tf_op | source)
XLA Modules:
  0.0 85.3 jit_solution(10249868887099325790)
XLA Ops:
  8.0 1.6 %shard_map.112 = (bf16[64,256]{1,0:T(8,128)(2,1)S(1)}, bf16[272,512]{1,0:T(8,128)(2,1)S(1)}) custom-call(s32[4]{0:T(128)S(1)} %pad_add_fusion.ids, bf16[128,256]{1,0:T(8,128)(2,1)} %keys.1, bf16[128,256]{1,0:T(8,128)(2,1)} %values.1, bf16[128,512]{1,0:T(8,128)(2,1)} %queries.1, bf16[128,512]{1,0:T(8,128)(2,1)} %out_grad.1, s32[1,128]{1,0:T(1,128)} %bitcast.7), custom_call_target="tpu_custom_call" | custom-call | tf_op jit(solution)/shard_map/pallas_call | solution.py:501
  9.6 3.0 %collective-permute-start.4 = (bf16[272,512]{1,0:T(8,128)(2,1)S(1)}, bf16[272,512]{1,0:T(8,128)(2,1)S(1)}, u32[]{:S(2)}, u32[]{:S(2)}) collective-permute-start(bf16[272,512]{1,0:T(8,128)(2,1)S(1)} %get-tuple-element.19.refs_4_), channel_id=1, source_target_pairs={{0,4},{1,5},{2,6},{3,7},{4,0},{5,1},{6,2},{7,3},{8,12},{9,13},{10,... | collective-permute-start | bytes 835592 | tf_op jit(solution)/shard_map/ppermute | solution.py:478
  12.6 3.6 %collective-permute-start.2 = (bf16[64,256]{1,0:T(8,128)(2,1)S(1)}, bf16[64,256]{1,0:T(8,128)(2,1)S(1)}, u32[]{:S(2)}, u32[]{:S(2)}) collective-permute-start(bf16[64,256]{1,0:T(8,128)(2,1)S(1)} %get-tuple-element.18.refs_3_.refs_0_), channel_id=1, source_target_pairs={{0,24},{1,25},{2,26},{3,27},{4,28},{5,29},{6,30},{7,31},{8,16},{9,... | collective-permute-start | bytes 98312 | tf_op jit(solution)/shard_map/ppermute | solution.py:478
  19.8 1.3 %collective-permute-done.1.refs_5_.refs_2_ = bf16[64,256]{1,0:T(8,128)(2,1)S(1)} collective-permute-done((bf16[64,256]{1,0:T(8,128)(2,1)S(1)}, bf16[64,256]{1,0:T(8,128)(2,1)S(1)}, u32[]{:S(2)}, u32[]{:S(2)}) %collective-permute-start.1) | collective-permute-done | bytes 32800 | tf_op jit(solution)/shard_map/ppermute | solution.py:478
  21.2 1.5 %collective-permute-done.5.refs_7_ = bf16[272,512]{1,0:T(8,128)(2,1)S(1)} collective-permute-done((bf16[272,512]{1,0:T(8,128)(2,1)S(1)}, bf16[272,512]{1,0:T(8,128)(2,1)S(1)}, u32[]{:S(2)}, u32[]{:S(2)}) %collective-permute-start.5) | collective-permute-done | bytes 278560 | tf_op jit(solution)/shard_map/ppermute | solution.py:478
  23.4 1.7 %shard_map.115.refs_8_ = f32[48,128]{1,0:T(8,128)S(1)} custom-call(s32[4]{0:T(128)S(1)} %pad_add_fusion.ids, s32[8]{0:T(128)S(1)} %copy-done.2, bf16[64,256]{1,0:T(8,128)(2,1)S(1)} %get-tuple-element.18.refs_3_.refs_0_, bf16[64,256]{1,0:T(8,128)(2,1)S(1)} %collective-permute-done.refs_4_.refs_1_, bf16[64,256]{1,0:T(8,128)(2,1)S(1)} %collective-permute-done.1.refs_5_.refs_2_, ...), custom_call_target="tpu_custom_call" | custom-call | tf_op jit(solution)/shard_map/pallas_call | solution.py:518
  25.6 1.4 %collective-permute-start.7 = (f32[48,128]{1,0:T(8,128)S(1)}, f32[48,128]{1,0:T(8,128)S(1)}, u32[]{:S(2)}, u32[]{:S(2)}) collective-permute-start(f32[48,128]{1,0:T(8,128)S(1)} %shard_map.115.refs_8_), channel_id=1, source_target_pairs={{0,4},{1,5},{2,6},{3,7},{4,0},{5,1},{6,2},{7,3},{8,12},{9,13},{10,... | collective-permute-start | bytes 73736 | tf_op jit(solution)/shard_map/ppermute | solution.py:478
  27.0 2.0 %collective-permute-done.8.refs_11_ = f32[48,128]{1,0:T(8,128)S(1)} collective-permute-done((f32[48,128]{1,0:T(8,128)S(1)}, f32[48,128]{1,0:T(8,128)S(1)}, u32[]{:S(2)}, u32[]{:S(2)}) %collective-permute-start.8) | collective-permute-done | bytes 24608 | tf_op jit(solution)/shard_map/ppermute | solution.py:478
  29.0 1.4 %collective-permute-done.7.refs_10_ = f32[48,128]{1,0:T(8,128)S(1)} collective-permute-done((f32[48,128]{1,0:T(8,128)S(1)}, f32[48,128]{1,0:T(8,128)S(1)}, u32[]{:S(2)}, u32[]{:S(2)}) %collective-permute-start.7) | collective-permute-done | bytes 24608 | tf_op jit(solution)/shard_map/ppermute | solution.py:478
  30.4 2.3 %shard_map.116 = (f32[64,256]{1,0:T(8,128)S(1)}, bf16[64,256]{1,0:T(8,128)(2,1)S(1)}, bf16[64,256]{1,0:T(8,128)(2,1)S(1)}, bf16[64,256]{1,0:T(8,128)(2,1)S(1)}, bf16[4,256,512]{2,1,0:T(8,128)(2,1)S(1)}) custom-call(s32[4]{0:T(128)S(1)} %pad_add_fusion.ids, s32[8]{0:T(128)S(1)} %copy-done.2, bf16[64,256]{1,0:T(8,128)(2,1)S(1)} %get-tuple-element.18.refs_3_.refs_0_, ...), custom_call_target="tpu_custom_call" | custom-call | tf_op jit(solution)/shard_map/pallas_call | solution.py:524
  33.3 3.2 %collective-permute-start.10 = (bf16[64,256]{1,0:T(8,128)(2,1)S(1)}, bf16[64,256]{1,0:T(8,128)(2,1)S(1)}, u32[]{:S(2)}, u32[]{:S(2)}) collective-permute-start(bf16[64,256]{1,0:T(8,128)(2,1)S(1)} %get-tuple-element.23), channel_id=1, source_target_pairs={{0,16},{1,17},{2,18},{3,19},{4,20},{5,21},{6,22},{7,23},{8,24},{9,... | collective-permute-start | bytes 98312 | tf_op jit(solution)/shard_map/ppermute | solution.py:478
  37.6 2.4 %collective-permute-done.10.refs_2_ = bf16[64,256]{1,0:T(8,128)(2,1)S(1)} collective-permute-done((bf16[64,256]{1,0:T(8,128)(2,1)S(1)}, bf16[64,256]{1,0:T(8,128)(2,1)S(1)}, u32[]{:S(2)}, u32[]{:S(2)}) %collective-permute-start.10) | collective-permute-done | bytes 32800 | tf_op jit(solution)/shard_map/ppermute | solution.py:478
  40.0 2.9 %collective-permute-done.11.refs_3_ = bf16[64,256]{1,0:T(8,128)(2,1)S(1)} collective-permute-done((bf16[64,256]{1,0:T(8,128)(2,1)S(1)}, bf16[64,256]{1,0:T(8,128)(2,1)S(1)}, u32[]{:S(2)}, u32[]{:S(2)}) %collective-permute-start.11) | collective-permute-done | bytes 32800 | tf_op jit(solution)/shard_map/ppermute | solution.py:478
  44.2 3.2 %collective-permute-start.12 = (bf16[64,256]{1,0:T(8,128)(2,1)S(1)}, bf16[64,256]{1,0:T(8,128)(2,1)S(1)}, u32[]{:S(2)}, u32[]{:S(2)}) collective-permute-start(bf16[64,256]{1,0:T(8,128)(2,1)S(1)} %shard_map.117.refs_0_), channel_id=1, source_target_pairs={{0,8},{1,9},{2,10},{3,11},{4,12},{5,13},{6,14},{7,15},{8,0},{9,1},... | collective-permute-start | bytes 98312 | tf_op jit(solution)/shard_map/ppermute | solution.py:478
  47.4 2.0 %collective-permute-done.14.refs_3_ = bf16[64,256]{1,0:T(8,128)(2,1)S(1)} collective-permute-done((bf16[64,256]{1,0:T(8,128)(2,1)S(1)}, bf16[64,256]{1,0:T(8,128)(2,1)S(1)}, u32[]{:S(2)}, u32[]{:S(2)}) %collective-permute-start.14) | collective-permute-done | bytes 32800 | tf_op jit(solution)/shard_map/ppermute | solution.py:478
  51.7 1.6 %collective-permute-start.15 = (bf16[256,256]{1,0:T(8,128)(2,1)S(1)}, bf16[256,256]{1,0:T(8,128)(2,1)S(1)}, u32[]{:S(2)}, u32[]{:S(2)}) collective-permute-start(bf16[256,256]{1,0:T(8,128)(2,1)S(1)} %shard_map.118.refs_0_), channel_id=1, source_target_pairs={{0,2},{1,3},{2,0},{3,1},{4,6},{5,7},{6,4},{7,5},{8,10},{9,11},{10,... | collective-permute-start | bytes 393224 | tf_op jit(solution)/shard_map/ppermute | solution.py:478
  53.3 4.5 %collective-permute-done.19.refs_1_ = bf16[256,256]{1,0:T(8,128)(2,1)S(1)} collective-permute-done((bf16[256,256]{1,0:T(8,128)(2,1)S(1)}, bf16[256,256]{1,0:T(8,128)(2,1)S(1)}, u32[]{:S(2)}, u32[]{:S(2)}) %collective-permute-start.19) | collective-permute-done | bytes 131104 | tf_op jit(solution)/shard_map/ppermute | solution.py:478
  57.8 1.8 %collective-permute-start.20 = (bf16[256,256]{1,0:T(8,128)(2,1)S(1)}, bf16[256,256]{1,0:T(8,128)(2,1)S(1)}, u32[]{:S(2)}, u32[]{:S(2)}) collective-permute-start(bf16[256,256]{1,0:T(8,128)(2,1)S(1)} %collective-permute-done.19.refs_1_), channel_id=1, source_target_pairs={{0,2},{1,3},{2,0},{3,1},{4,6},{5,7},{6,4},{7,5},{8,10},{9,11},{10,... | collective-permute-start | bytes 393224 | tf_op jit(solution)/shard_map/ppermute | solution.py:478
  60.1 2.7 %collective-permute-done.20.refs_3_ = bf16[256,256]{1,0:T(8,128)(2,1)S(1)} collective-permute-done((bf16[256,256]{1,0:T(8,128)(2,1)S(1)}, bf16[256,256]{1,0:T(8,128)(2,1)S(1)}, u32[]{:S(2)}, u32[]{:S(2)}) %collective-permute-start.20) | collective-permute-done | bytes 131104 | tf_op jit(solution)/shard_map/ppermute | solution.py:478
  63.9 1.4 %collective-permute-start.17 = (bf16[128,512]{1,0:T(8,128)(2,1)S(1)}, bf16[128,512]{1,0:T(8,128)(2,1)S(1)}, u32[]{:S(2)}, u32[]{:S(2)}) collective-permute-start(bf16[128,512]{1,0:T(8,128)(2,1)S(1)} %get-tuple-element.27), channel_id=1, source_target_pairs={{0,4},{1,5},{2,6},{3,7},{4,0},{5,1},{6,2},{7,3},{8,12},{9,13},{10,... | collective-permute-start | bytes 393224 | tf_op jit(solution)/shard_map/ppermute | solution.py:478
  65.4 5.0 %shard_map.121 = (f32[2048,512]{1,0:T(8,128)S(1)}, f32[8,512]{1,0:T(8,128)S(1)}) custom-call(s32[4]{0:T(128)S(1)} %pad_add_fusion.ids, f32[8,512]{1,0:T(8,128)S(1)} %shard_map.113.refs_2_.squares, bf16[8,128,2048]{2,1,0:T(8,128)(2,1)} %bitcast.6, bf16[256,256]{1,0:T(8,128)(2,1)S(1)} %shard_map.118.refs_0_, ...), custom_call_target="tpu_custom_call" | custom-call | tf_op jit(solution)/shard_map/pallas_call | solution.py:554
  70.4 2.1 %collective-permute-start.27 = (f32[8,512]{1,0:T(8,128)S(1)}, f32[8,512]{1,0:T(8,128)S(1)}, u32[]{:S(2)}, u32[]{:S(2)}) collective-permute-start(f32[8,512]{1,0:T(8,128)S(1)} %get-tuple-element.29.sums), channel_id=1, source_target_pairs={{0,3},{1,2},{2,1},{3,0},{4,7},{5,6},{6,5},{7,4},{8,11},{9,10},{10,... | collective-permute-start | bytes 49160 | tf_op jit(solution)/shard_map/ppermute | solution.py:478
  73.9 2.3 %collective-permute-done.26.sums_2 = f32[8,512]{1,0:T(8,128)S(1)} collective-permute-done((f32[8,512]{1,0:T(8,128)S(1)}, f32[8,512]{1,0:T(8,128)S(1)}, u32[]{:S(2)}, u32[]{:S(2)}) %collective-permute-start.26) | collective-permute-done | bytes 16416 | tf_op jit(solution)/shard_map/ppermute | solution.py:478
  76.2 2.2 %shard_map.122 = (f32[2048,256]{1,0:T(8,128)}, f32[2048,256]{1,0:T(8,128)}) custom-call(f32[8,512]{1,0:T(8,128)S(1)} %get-tuple-element.29.sums, f32[8,512]{1,0:T(8,128)S(1)} %collective-permute-done.25.sums_1, f32[8,512]{1,0:T(8,128)S(1)} %collective-permute-done.26.sums_2, f32[8,512]{1,0:T(8,128)S(1)} %collective-permute-done.27.sums_3, ...), custom_call_target="tpu_custom_call" | custom-call | tf_op jit(solution)/shard_map/pallas_call | solution.py:567
  (53 shorter events, 13.9 us)
Async XLA Ops:
  7.2 58.2 %all-gather.3.cloned.1.call-start = ((), (), s32[]{:S(2)}) async-start(), calls=%async_computation | async-start | bytes 4718592 | tf_op jit(solution)/shard_map/all_gather | solution.py:481
  9.6 11.5 %collective-permute-start.4 = (bf16[272,512]{1,0:T(8,128)(2,1)S(1)}, bf16[272,512]{1,0:T(8,128)(2,1)S(1)}, u32[]{:S(2)}, u32[]{:S(2)}) collective-permute-start(bf16[272,512]{1,0:T(8,128)(2,1)S(1)} %get-tuple-element.19.refs_4_), channel_id=1, source_target_pairs={{0,4},{1,5},{2,6},{3,7},{4,0},{5,1},{6,2},{7,3},{8,12},{9,13},{10,... | collective-permute-start | bytes 835592 | tf_op jit(solution)/shard_map/ppermute | solution.py:478
  12.6 8.5 %collective-permute-start.3 = (bf16[272,512]{1,0:T(8,128)(2,1)S(1)}, bf16[272,512]{1,0:T(8,128)(2,1)S(1)}, u32[]{:S(2)}, u32[]{:S(2)}) collective-permute-start(bf16[272,512]{1,0:T(8,128)(2,1)S(1)} %get-tuple-element.19.refs_4_), channel_id=1, source_target_pairs={{0,1},{1,0},{2,3},{3,2},{4,5},{5,4},{6,7},{7,6},{8,9},{9,8},{10,11... | collective-permute-start | bytes 835592 | tf_op jit(solution)/shard_map/ppermute | solution.py:478
  12.6 7.1 %collective-permute-start.2 = (bf16[64,256]{1,0:T(8,128)(2,1)S(1)}, bf16[64,256]{1,0:T(8,128)(2,1)S(1)}, u32[]{:S(2)}, u32[]{:S(2)}) collective-permute-start(bf16[64,256]{1,0:T(8,128)(2,1)S(1)} %get-tuple-element.18.refs_3_.refs_0_), channel_id=1, source_target_pairs={{0,24},{1,25},{2,26},{3,27},{4,28},{5,29},{6,30},{7,31},{8,16},{9,... | collective-permute-start | bytes 98312 | tf_op jit(solution)/shard_map/ppermute | solution.py:478
  16.2 4.9 %collective-permute-start.1 = (bf16[64,256]{1,0:T(8,128)(2,1)S(1)}, bf16[64,256]{1,0:T(8,128)(2,1)S(1)}, u32[]{:S(2)}, u32[]{:S(2)}) collective-permute-start(bf16[64,256]{1,0:T(8,128)(2,1)S(1)} %get-tuple-element.18.refs_3_.refs_0_), channel_id=1, source_target_pairs={{0,16},{1,17},{2,18},{3,19},{4,20},{5,21},{6,22},{7,23},{8,24},{9,... | collective-permute-start | bytes 98312 | tf_op jit(solution)/shard_map/ppermute | solution.py:478
  16.2 4.9 %collective-permute-start = (bf16[64,256]{1,0:T(8,128)(2,1)S(1)}, bf16[64,256]{1,0:T(8,128)(2,1)S(1)}, u32[]{:S(2)}, u32[]{:S(2)}) collective-permute-start(bf16[64,256]{1,0:T(8,128)(2,1)S(1)} %get-tuple-element.18.refs_3_.refs_0_), channel_id=1, source_target_pairs={{0,8},{1,9},{2,10},{3,11},{4,12},{5,13},{6,14},{7,15},{8,0},{9,1},... | collective-permute-start | bytes 98312 | tf_op jit(solution)/shard_map/ppermute | solution.py:478
  25.1 4.0 %collective-permute-start.8 = (f32[48,128]{1,0:T(8,128)S(1)}, f32[48,128]{1,0:T(8,128)S(1)}, u32[]{:S(2)}, u32[]{:S(2)}) collective-permute-start(f32[48,128]{1,0:T(8,128)S(1)} %shard_map.115.refs_8_), channel_id=1, source_target_pairs={{0,5},{1,4},{2,7},{3,6},{4,1},{5,0},{6,3},{7,2},{8,13},{9,12},{10,... | collective-permute-start | bytes 73736 | tf_op jit(solution)/shard_map/ppermute | solution.py:478
  25.6 4.8 %collective-permute-start.7 = (f32[48,128]{1,0:T(8,128)S(1)}, f32[48,128]{1,0:T(8,128)S(1)}, u32[]{:S(2)}, u32[]{:S(2)}) collective-permute-start(f32[48,128]{1,0:T(8,128)S(1)} %shard_map.115.refs_8_), channel_id=1, source_target_pairs={{0,4},{1,5},{2,6},{3,7},{4,0},{5,1},{6,2},{7,3},{8,12},{9,13},{10,... | collective-permute-start | bytes 73736 | tf_op jit(solution)/shard_map/ppermute | solution.py:478
  32.7 4.9 %collective-permute-start.9 = (bf16[64,256]{1,0:T(8,128)(2,1)S(1)}, bf16[64,256]{1,0:T(8,128)(2,1)S(1)}, u32[]{:S(2)}, u32[]{:S(2)}) collective-permute-start(bf16[64,256]{1,0:T(8,128)(2,1)S(1)} %get-tuple-element.22), channel_id=1, source_target_pairs={{0,8},{1,9},{2,10},{3,11},{4,12},{5,13},{6,14},{7,15},{8,0},{9,1},... | collective-permute-start | bytes 98312 | tf_op jit(solution)/shard_map/ppermute | solution.py:478
  33.3 6.7 %collective-permute-start.10 = (bf16[64,256]{1,0:T(8,128)(2,1)S(1)}, bf16[64,256]{1,0:T(8,128)(2,1)S(1)}, u32[]{:S(2)}, u32[]{:S(2)}) collective-permute-start(bf16[64,256]{1,0:T(8,128)(2,1)S(1)} %get-tuple-element.23), channel_id=1, source_target_pairs={{0,16},{1,17},{2,18},{3,19},{4,20},{5,21},{6,22},{7,23},{8,24},{9,... | collective-permute-start | bytes 98312 | tf_op jit(solution)/shard_map/ppermute | solution.py:478
  36.5 6.4 %collective-permute-start.11 = (bf16[64,256]{1,0:T(8,128)(2,1)S(1)}, bf16[64,256]{1,0:T(8,128)(2,1)S(1)}, u32[]{:S(2)}, u32[]{:S(2)}) collective-permute-start(bf16[64,256]{1,0:T(8,128)(2,1)S(1)} %get-tuple-element.24), channel_id=1, source_target_pairs={{0,24},{1,25},{2,26},{3,27},{4,28},{5,29},{6,30},{7,31},{8,16},{9,... | collective-permute-start | bytes 98312 | tf_op jit(solution)/shard_map/ppermute | solution.py:478
  43.0 6.5 %collective-permute-start.14 = (bf16[64,256]{1,0:T(8,128)(2,1)S(1)}, bf16[64,256]{1,0:T(8,128)(2,1)S(1)}, u32[]{:S(2)}, u32[]{:S(2)}) collective-permute-start(bf16[64,256]{1,0:T(8,128)(2,1)S(1)} %shard_map.117.refs_0_), channel_id=1, source_target_pairs={{0,24},{1,25},{2,26},{3,27},{4,28},{5,29},{6,30},{7,31},{8,16},{9,... | collective-permute-start | bytes 98312 | tf_op jit(solution)/shard_map/ppermute | solution.py:478
  44.2 6.0 %collective-permute-start.13 = (bf16[64,256]{1,0:T(8,128)(2,1)S(1)}, bf16[64,256]{1,0:T(8,128)(2,1)S(1)}, u32[]{:S(2)}, u32[]{:S(2)}) collective-permute-start(bf16[64,256]{1,0:T(8,128)(2,1)S(1)} %shard_map.117.refs_0_), channel_id=1, source_target_pairs={{0,16},{1,17},{2,18},{3,19},{4,20},{5,21},{6,22},{7,23},{8,24},{9,... | collective-permute-start | bytes 98312 | tf_op jit(solution)/shard_map/ppermute | solution.py:478
  44.2 6.2 %collective-permute-start.12 = (bf16[64,256]{1,0:T(8,128)(2,1)S(1)}, bf16[64,256]{1,0:T(8,128)(2,1)S(1)}, u32[]{:S(2)}, u32[]{:S(2)}) collective-permute-start(bf16[64,256]{1,0:T(8,128)(2,1)S(1)} %shard_map.117.refs_0_), channel_id=1, source_target_pairs={{0,8},{1,9},{2,10},{3,11},{4,12},{5,13},{6,14},{7,15},{8,0},{9,1},... | collective-permute-start | bytes 98312 | tf_op jit(solution)/shard_map/ppermute | solution.py:478
  50.4 7.4 %collective-permute-start.19 = (bf16[256,256]{1,0:T(8,128)(2,1)S(1)}, bf16[256,256]{1,0:T(8,128)(2,1)S(1)}, u32[]{:S(2)}, u32[]{:S(2)}) collective-permute-start(bf16[256,256]{1,0:T(8,128)(2,1)S(1)} %shard_map.118.refs_0_), channel_id=1, source_target_pairs={{0,4},{1,5},{2,6},{3,7},{4,0},{5,1},{6,2},{7,3},{8,12},{9,13},{10,... | collective-permute-start | bytes 393224 | tf_op jit(solution)/shard_map/ppermute | solution.py:478
  51.7 8.5 %collective-permute-start.15 = (bf16[256,256]{1,0:T(8,128)(2,1)S(1)}, bf16[256,256]{1,0:T(8,128)(2,1)S(1)}, u32[]{:S(2)}, u32[]{:S(2)}) collective-permute-start(bf16[256,256]{1,0:T(8,128)(2,1)S(1)} %shard_map.118.refs_0_), channel_id=1, source_target_pairs={{0,2},{1,3},{2,0},{3,1},{4,6},{5,7},{6,4},{7,5},{8,10},{9,11},{10,... | collective-permute-start | bytes 393224 | tf_op jit(solution)/shard_map/ppermute | solution.py:478
  57.8 5.0 %collective-permute-start.20 = (bf16[256,256]{1,0:T(8,128)(2,1)S(1)}, bf16[256,256]{1,0:T(8,128)(2,1)S(1)}, u32[]{:S(2)}, u32[]{:S(2)}) collective-permute-start(bf16[256,256]{1,0:T(8,128)(2,1)S(1)} %collective-permute-done.19.refs_1_), channel_id=1, source_target_pairs={{0,2},{1,3},{2,0},{3,1},{4,6},{5,7},{6,4},{7,5},{8,10},{9,11},{10,... | collective-permute-start | bytes 393224 | tf_op jit(solution)/shard_map/ppermute | solution.py:478
  59.6 4.2 %collective-permute-start.21 = (bf16[256,256]{1,0:T(8,128)(2,1)S(1)}, bf16[256,256]{1,0:T(8,128)(2,1)S(1)}, u32[]{:S(2)}, u32[]{:S(2)}) collective-permute-start(bf16[256,256]{1,0:T(8,128)(2,1)S(1)} %shard_map.118.refs_0_), channel_id=1, source_target_pairs={{0,1},{1,0},{2,3},{3,2},{4,5},{5,4},{6,7},{7,6},{8,9},{9,8},{10,11... | collective-permute-start | bytes 393224 | tf_op jit(solution)/shard_map/ppermute | solution.py:478
  59.6 5.7 %collective-permute-start.22 = (bf16[256,256]{1,0:T(8,128)(2,1)S(1)}, bf16[256,256]{1,0:T(8,128)(2,1)S(1)}, u32[]{:S(2)}, u32[]{:S(2)}) collective-permute-start(bf16[256,256]{1,0:T(8,128)(2,1)S(1)} %collective-permute-done.19.refs_1_), channel_id=1, source_target_pairs={{0,1},{1,0},{2,3},{3,2},{4,5},{5,4},{6,7},{7,6},{8,9},{9,8},{10,11... | collective-permute-start | bytes 393224 | tf_op jit(solution)/shard_map/ppermute | solution.py:478
  60.1 5.2 %collective-permute-start.23 = (bf16[256,256]{1,0:T(8,128)(2,1)S(1)}, bf16[256,256]{1,0:T(8,128)(2,1)S(1)}, u32[]{:S(2)}, u32[]{:S(2)}) collective-permute-start(bf16[256,256]{1,0:T(8,128)(2,1)S(1)} %collective-permute-done.15.refs_5_.refs_2_), channel_id=1, source_target_pairs={{0,1},{1,0},{2,3},{3,2},{4,5},{5,4},{6,7},{7,6},{8,9},{9,8},{10,11... | collective-permute-start | bytes 393224 | tf_op jit(solution)/shard_map/ppermute | solution.py:478
  63.3 9.4 %collective-permute-start.16 = (bf16[128,512]{1,0:T(8,128)(2,1)S(1)}, bf16[128,512]{1,0:T(8,128)(2,1)S(1)}, u32[]{:S(2)}, u32[]{:S(2)}) collective-permute-start(bf16[128,512]{1,0:T(8,128)(2,1)S(1)} %get-tuple-element.26), channel_id=1, source_target_pairs={{0,1},{1,0},{2,3},{3,2},{4,5},{5,4},{6,7},{7,6},{8,9},{9,8},{10,11... | collective-permute-start | bytes 393224 | tf_op jit(solution)/shard_map/ppermute | solution.py:478
  63.9 8.9 %collective-permute-start.17 = (bf16[128,512]{1,0:T(8,128)(2,1)S(1)}, bf16[128,512]{1,0:T(8,128)(2,1)S(1)}, u32[]{:S(2)}, u32[]{:S(2)}) collective-permute-start(bf16[128,512]{1,0:T(8,128)(2,1)S(1)} %get-tuple-element.27), channel_id=1, source_target_pairs={{0,4},{1,5},{2,6},{3,7},{4,0},{5,1},{6,2},{7,3},{8,12},{9,13},{10,... | collective-permute-start | bytes 393224 | tf_op jit(solution)/shard_map/ppermute | solution.py:478
  65.3 7.4 %collective-permute-start.18 = (bf16[128,512]{1,0:T(8,128)(2,1)S(1)}, bf16[128,512]{1,0:T(8,128)(2,1)S(1)}, u32[]{:S(2)}, u32[]{:S(2)}) collective-permute-start(bf16[128,512]{1,0:T(8,128)(2,1)S(1)} %get-tuple-element.28), channel_id=1, source_target_pairs={{0,5},{1,4},{2,7},{3,6},{4,1},{5,0},{6,3},{7,2},{8,13},{9,12},{10,... | collective-permute-start | bytes 393224 | tf_op jit(solution)/shard_map/ppermute | solution.py:478
  72.5 3.7 %collective-permute-start.26 = (f32[8,512]{1,0:T(8,128)S(1)}, f32[8,512]{1,0:T(8,128)S(1)}, u32[]{:S(2)}, u32[]{:S(2)}) collective-permute-start(f32[8,512]{1,0:T(8,128)S(1)} %get-tuple-element.29.sums), channel_id=1, source_target_pairs={{0,2},{1,3},{2,0},{3,1},{4,6},{5,7},{6,4},{7,5},{8,10},{9,11},{10,... | collective-permute-start | bytes 49160 | tf_op jit(solution)/shard_map/ppermute | solution.py:478
  (8 other events, 17.8 us)
Sparse Core Ops, SparseCore 0:
  9.5 55.4 all-gather.2

commit v4 on v2

--- a/solution.py
+++ b/solution.py
@@ -183,22 +183,20 @@
 
 
 def pack_kernel(
-    ids, keys, values, queries, out_grad, positions, hidden, kv_out, qd_out, turned, place, held, sems
+    ids, keys, values, queries, out_grad, positions, hidden, kv_out, qd_out, held, place, sems
 ):
-    half = kv_out.shape[0]
     tok_dev = queries.shape[0]
-    rows = pl.ds(pl.multiple_of(ids[3] * half, half), half)
     columns = pl.ds(pl.multiple_of(ids[2] * DH, DH), DH)
     copies = [
         pltpu.make_async_copy(source, target, sems.at[i])
         for i, (source, target) in enumerate(
             (
-                (hidden, held),
                 (positions, place),
-                (keys.at[rows, columns], kv_out.at[:, :DH]),
-                (values.at[rows, columns], kv_out.at[:, DH:]),
+                (keys.at[:, columns], kv_out.at[:, :DH]),
+                (values.at[:, columns], kv_out.at[:, DH:]),
                 (queries, qd_out.at[:tok_dev]),
                 (out_grad, qd_out.at[tok_dev : 2 * tok_dev]),
+                (hidden, held),
             )
         )
     ]
@@ -208,14 +206,12 @@
     if rest > 0:
         qd_out[2 * tok_dev :, tok_dev:] = jnp.zeros((qd_out.shape[0] - 2 * tok_dev, rest), jnp.bfloat16)
     copies[0].wait()
-    turned[...] = held[...].T
-    copies[1].wait()
     high = place[...] // DIGIT
     low = place[...] - high * DIGIT
     pad = jnp.zeros((qd_out.shape[0] - 2 * tok_dev - 2, tok_dev), jnp.float32)
     digits = jnp.concatenate([high.astype(jnp.float32), low.astype(jnp.float32), pad], axis=0)
     qd_out[2 * tok_dev :, :tok_dev] = digits.astype(jnp.bfloat16)
-    for copy in copies[2:]:
+    for copy in copies[1:]:
         copy.wait()
 
 
@@ -223,33 +219,60 @@
     pass
 
 
-def after(x, *events):
+def after(xs, *events):
+    count = len(xs)
     return pl.pallas_call(
         nothing_kernel,
-        out_shape=jax.ShapeDtypeStruct(x.shape, x.dtype),
-        in_specs=[ANY] * (1 + len(events)),
-        out_specs=ANY,
-        input_output_aliases={0: 0},
+        out_shape=tuple(jax.ShapeDtypeStruct(x.shape, x.dtype) for x in xs),
+        in_specs=[ANY] * (count + len(events)),
+        out_specs=(ANY,) * count,
+        input_output_aliases={i: i for i in range(count)},
         compiler_params=pltpu.CompilerParams(vmem_limit_bytes=2**20),
-    )(x, *events)
-
-
-def seen_pairs(ids, owner, planes, half, qd):
+    )(*xs, *events)
+
+
+def halves_kernel(*refs):
+    up, down, (up_half, down_half, sems) = refs[0], refs[1], refs[-3:]
+    half = up_half.shape[0]
+    copies = [
+        pltpu.make_async_copy(up.at[:half], up_half, sems.at[0]),
+        pltpu.make_async_copy(down.at[half:], down_half, sems.at[1]),
+    ]
+    for copy in copies:
+        copy.start()
+    for copy in copies:
+        copy.wait()
+
+
+def halves_after(up, down, *events):
+    half = jax.ShapeDtypeStruct((up.shape[0] // 2, up.shape[1]), up.dtype)
+    return pl.pallas_call(
+        halves_kernel,
+        out_shape=(half, half),
+        in_specs=[ANY] * (2 + len(events)),
+        out_specs=(ANY, ANY),
+        scratch_shapes=[pltpu.SemaphoreType.DMA((2,))],
+        compiler_params=pltpu.CompilerParams(vmem_limit_bytes=2**20),
+    )(up, down, *events)
+
+
+def seen_pairs(ids, owner, planes, tok_dev, qd):
     last = 2 * planes * SIDES - 1
-    tok_dev = 2 * half
-    key_rows = []
-    row = lax.broadcasted_iota(jnp.int32, (half, tok_dev), 0)
-    for j in range(planes):
-        stretch = owner[(ids[0] ^ j) * SIDES + ids[1]]
-        stretch = jnp.where(ids[3] == 0, stretch, last - stretch)
-        key_rows.append(row + stretch * half)
-    key_place = jnp.concatenate(key_rows, axis=0)
+    half = tok_dev // 2
+
+    def place_of(at, block):
+        stretch = owner[block]
+        return jnp.where(at < half, at + stretch * half, at - half + (last - stretch) * half)
+
+    row = lax.broadcasted_iota(jnp.int32, (tok_dev, tok_dev), 0)
+    key_place = jnp.concatenate(
+        [place_of(row, (ids[0] ^ j) * SIDES + ids[1]) for j in range(planes)], axis=0
+    )
     lane = lax.broadcasted_iota(jnp.int32, (1, tok_dev), 1)
     seen = []
     for side in range(SIDES):
-        stretch = owner[ids[0] * SIDES + (ids[1] ^ side)]
-        place = jnp.where(lane < half, lane + stretch * half, lane - half + (last - stretch) * half)
-        digits = qd[side * MEMBERS][2 * tok_dev :, :tok_dev].astype(jnp.float32)
+        place = place_of(lane, ids[0] * SIDES + (ids[1] ^ side))
+        digits = qd[side][2 * tok_dev :, :tok_dev].astype(jnp.float32)
         back = (digits[0:1] * DIGIT + digits[1:2]).astype(jnp.int32)
         seen.append((key_place <= place) & (key_place >= place - back))
     return seen
@@ -260,25 +283,23 @@
 
 
 def stats_kernel(planes, ids, owner, *refs):
-    kv_refs, qd, stats = refs[:planes], refs[planes : planes + SIDES * MEMBERS], refs[-1]
-    half = kv_refs[0].shape[0]
-    tok_dev = 2 * half
+    kv_refs, qd, stats = refs[:planes], refs[planes : planes + SIDES], refs[-1]
+    tok_dev = kv_refs[0].shape[0]
     heads = qd[0].shape[1] // DH
     scale = 1.0 / math.sqrt(DH)
     kv = jnp.concatenate([ref[...] for ref in kv_refs], axis=0)
     k, v = kv[:, :DH], kv[:, DH:]
-    seen = seen_pairs(ids, owner, planes, half, qd)
-    tiles = SIDES * MEMBERS * heads
-    for source in range(SIDES * MEMBERS):
+    seen = seen_pairs(ids, owner, planes, tok_dev, qd)
+    tiles = SIDES * heads
+    for side in range(SIDES):
         for head in range(heads):
-            q = qd[source][:tok_dev, head * DH : (head + 1) * DH]
-            d = qd[source][tok_dev : 2 * tok_dev, head * DH : (head + 1) * DH]
-            mask = seen[source // MEMBERS]
-            scores = jnp.where(mask, scaled_scores(k, q, scale), NEGATIVE)
+            q = qd[side][:tok_dev, head * DH : (head + 1) * DH]
+            d = qd[side][tok_dev : 2 * tok_dev, head * DH : (head + 1) * DH]
+            scores = jnp.where(seen[side], scaled_scores(k, q, scale), NEGATIVE)
             dprobs = lax.dot_general(v, d, CONTRACT_LAST, preferred_element_type=jnp.float32)
             top = jnp.max(scores, axis=0, keepdims=True)
-            weights = jnp.where(mask, jnp.exp(scores - top), 0.0)
-            tile = source * heads + head
+            weights = jnp.where(seen[side], jnp.exp(scores - top), 0.0)
+            tile = side * heads + head
             stats[tile : tile + 1] = top
             stats[tiles + tile : tiles + tile + 1] = jnp.sum(weights, axis=0, keepdims=True)
             stats[2 * tiles + tile : 2 * tiles + tile + 1] = jnp.sum(
@@ -287,29 +308,25 @@
 
 
 def grads_kernel(planes, ids, owner, *refs):
-    sources = SIDES * MEMBERS
     kv_refs, refs = refs[:planes], refs[planes:]
-    qd, refs = refs[:sources], refs[sources:]
-    stats, refs = refs[:sources], refs[sources:]
-    kv_out, slopes_out = refs[:planes], refs[planes]
-    half = kv_refs[0].shape[0]
-    tok_dev = 2 * half
+    qd, refs = refs[:SIDES], refs[SIDES:]
+    stats, (keep, give, slopes_out, acc) = refs[:SIDES], refs[SIDES:]
+    tok_dev = kv_refs[0].shape[0]
+    half = tok_dev // 2
     heads = qd[0].shape[1] // DH
     scale = 1.0 / math.sqrt(DH)
     kv = jnp.concatenate([ref[...] for ref in kv_refs], axis=0)
     k, v = kv[:, :DH], kv[:, DH:]
-    seen = seen_pairs(ids, owner, planes, half, qd)
-    tiles = sources * heads
-    key_acc = jnp.zeros((planes * half, DH), jnp.float32)
-    value_acc = jnp.zeros((planes * half, DH), jnp.float32)
-    for source in range(sources):
+    seen = seen_pairs(ids, owner, planes, tok_dev, qd)
+    tiles = SIDES * heads
+    key_acc = jnp.zeros((planes * tok_dev, DH), jnp.float32)
+    value_acc = jnp.zeros((planes * tok_dev, DH), jnp.float32)
+    for side in range(SIDES):
         q_rows, d_rows, slope_tiles, prob_tiles = [], [], [], []
-        mask = seen[source // MEMBERS]
-        first = source * heads
         parts = [
             [
-                stats[other][kind * tiles + (source ^ other) * heads :][:heads]
-                for other in range(sources)
+                stats[other][kind * tiles + (side ^ other) * heads :][:heads]
+                for other in range(SIDES)
             ]
             for kind in range(3)
         ]
@@ -319,18 +336,18 @@
         lse = top + jnp.log(mass)
         delta = sum(share * part for share, part in zip(shares, parts[2], strict=True)) / mass
         for head in range(heads):
-            q = qd[source][:tok_dev, head * DH : (head + 1) * DH]
-            d = qd[source][tok_dev : 2 * tok_dev, head * DH : (head + 1) * DH]
+            q = qd[side][:tok_dev, head * DH : (head + 1) * DH]
+            d = qd[side][tok_dev : 2 * tok_dev, head * DH : (head + 1) * DH]
             scores = scaled_scores(k, q, scale)
             dprobs = lax.dot_general(v, d, CONTRACT_LAST, preferred_element_type=jnp.float32)
-            probs = jnp.where(mask, jnp.exp(scores - lse[head : head + 1]), 0.0)
+            probs = jnp.where(seen[side], jnp.exp(scores - lse[head : head + 1]), 0.0)
             slopes = (probs * (dprobs - delta[head : head + 1]) * scale).astype(jnp.bfloat16)
             q_rows.append(q)
             d_rows.append(d)
             slope_tiles.append(slopes)
             prob_tiles.append(probs.astype(jnp.bfloat16))
         slope_tile = jnp.concatenate(slope_tiles, axis=1)
-        slopes_out[source] = slope_tile
+        slopes_out[side] = slope_tile
         key_acc += jnp.dot(
             slope_tile,
             jnp.concatenate(q_rows, axis=0),
@@ -341,13 +358,25 @@
             jnp.concatenate(d_rows, axis=0),
             preferred_element_type=jnp.float32,
         )
+    acc[:, :DH] = key_acc
+    acc[:, DH:] = value_acc
     for j in range(planes):
-        kv_out[j][:, :DH] = key_acc[j * half : (j + 1) * half].astype(kv_out[j].dtype)
-        kv_out[j][:, DH:] = value_acc[j * half : (j + 1) * half].astype(kv_out[j].dtype)
+        rows = slice(j * half, (j + 1) * half)
+        own = pl.multiple_of(j * tok_dev + ids[3] * half, half)
+        other = pl.multiple_of(j * tok_dev + (1 - ids[3]) * half, half)
+        keep[rows] = acc[pl.ds(own, half)]
+        give[rows] = acc[pl.ds(other, half)].astype(give.dtype)
+
+
+def members_kernel(keep, got, *outs):
+    half = outs[0].shape[0]
+    for j, out in enumerate(outs):
+        rows = slice(j * half, (j + 1) * half)
+        out[...] = (keep[rows] + got[rows].astype(jnp.float32)).astype(out.dtype)
 
 
 def query_kernel(planes, *refs):
-    kv_refs, slopes, q_out = refs[:planes], refs[planes], refs[planes + 2 :]
+    kv_refs, slopes, q_out = refs[:planes], refs[planes], refs[planes + 3 :]
     k = jnp.concatenate([ref[:, :DH] for ref in kv_refs], axis=0)
     for source, out in enumerate(q_out):
         tok_dev, width = out.shape
@@ -383,18 +412,24 @@
     out[:, width:] += jnp.sum((v * v).reshape(-1, 8, width), axis=0)
 
 
-def project_kernel(planes, steps, ids, squares, turned, *refs):
+def project_kernel(planes, steps, ids, squares, *refs):
     count = planes * SIDES
+    hidden, refs = refs[: count + 1], refs[count + 1 :]
     pieces, (raw, sums, grads, held, sems) = refs[:8], refs[8:]
-    tok_dev = turned.shape[2]
+    tok_dev = hidden[0].shape[0]
     half = tok_dev // 2
     tile = raw.shape[0] // steps
-    copies = [
-        pltpu.make_async_copy(turned.at[:, rows], held.at[:, rows], sems.at[i])
-        for i, rows in enumerate(pl.ds(i * tile, tile) for i in range(steps))
-    ]
-    for copy in copies:
-        copy.start()
+    mine = jnp.where(ids[1] == 0, ids[0], count - 1 - ids[0])
+    copies = []
+    for i in range(steps):
+        columns = pl.ds(i * tile, tile)
+        for r, source in enumerate(hidden):
+            spot = mine + (r if r < count else count // 2)
+            spot = jnp.where(spot >= count, spot - count, spot)
+            first = half if r == count else 0
+            target = held.at[spot, pl.ds(first, source.shape[0]), columns]
+            copies.append(pltpu.make_async_copy(source.at[:, columns], target, sems.at[i, r]))
+            copies[-1].start()
     for index, piece in enumerate(pieces):
         side = ids[1] ^ (index & 1)
         group = ids[2] ^ ((index >> 1) & 1)
@@ -411,10 +446,13 @@
     width = raw.shape[1]
     acc = jnp.zeros((8, width), jnp.float32)
     for i in range(steps):
-        copies[i].wait()
+        for copy in copies[i * (count + 1) : (i + 1) * (count + 1)]:
+            copy.wait()
         rows = slice(i * tile, (i + 1) * tile)
-        block = jnp.concatenate([held[spot, rows] for spot in range(count)], axis=1)
-        out = jnp.dot(block, grads[...], preferred_element_type=jnp.float32)
+        block = held[:, :, rows].reshape(count * tok_dev, tile)
+        out = lax.dot_general(
+            block, grads[...], CONTRACT_FIRST, preferred_element_type=jnp.float32
+        )
         raw[rows] = out
         acc += jnp.sum((out * out).reshape(-1, 8, width), axis=0)
     total = jnp.sum(acc, axis=0, keepdims=True)
@@ -478,34 +516,37 @@
                 pairs.append((i * fs + j, (p * SIDES + s) * fs + g * MEMBERS + m))
         return lax.ppermute(x, ("ctx", "fsdp"), pairs)
 
+    ring = [p * SIDES for p in range(planes)] + [p * SIDES + 1 for p in reversed(range(planes))]
+
+    def around(x, step):
+        pairs = [(ring[i], ring[(i + step) % count]) for i in range(count)]
+        return lax.ppermute(x, "ctx", pairs)
+
+    rows = hidden.shape[1]
+
     far = [
         pltpu.with_memory_space_constraint(x, pltpu.HBM)
         for x in (keys, values, queries, out_grad, positions.reshape(1, tok_dev), hidden)
     ]
-    kv, qd, turned = call(
+    kv, qd, held = call(
         pack_kernel,
         [SMEM] + [ANY] * 6,
         (
-            shape((half, 2 * DH), bf16),
+            shape((tok_dev, 2 * DH), bf16),
             shape((2 * tok_dev + 16, width), bf16),
-            shape(hidden.shape[::-1], bf16),
+            shape(hidden.shape, bf16),
         ),
         scratch_shapes=[
             pltpu.VMEM((1, tok_dev), jnp.int32),
-            pltpu.VMEM(hidden.shape, bf16),
             pltpu.SemaphoreType.DMA((6,)),
         ],
     )(ids, *far)
     qd_side = move(qd, side=1)
     kv_all = [kv] + [move(kv, plane=j) for j in range(1, planes)]
-    qd_member = move(qd, member=1)
-    qd_side = after(qd_side, qd_member, *kv_all)
-    qd_both = move(qd_side, member=1)
-    qd_all = [qd, qd_member, qd_side, qd_both]
-
-    ring = [p * SIDES for p in range(planes)] + [p * SIDES + 1 for p in reversed(range(planes))]
-    turned = lax.all_gather(turned, "ctx", axis_index_groups=[ring])
-    rows = turned.shape[1]
+    qd_all = [qd, qd_side]
+    (held,) = after((held,), qd_side, *kv_all[1:])
+    blocks = {0: held}
+    up, down = around(held, 1), around(held, -1)
 
     columns = 2 * KVG * DH
     steps = 8
@@ -520,58 +561,71 @@
         compiler_params=pltpu.CompilerParams(vmem_limit_bytes=8 * 2**20),
     )(key_weight, value_weight)
 
-    tiles = SIDES * MEMBERS * width // DH
+    tiles = SIDES * width // DH
     stats = call(
         functools.partial(stats_kernel, planes),
-        [SMEM] * 2 + [VMEM] * (planes + 4),
+        [SMEM] * 2 + [VMEM] * (planes + SIDES),
         shape((3 * tiles, tok_dev), f32),
     )(ids, stretch_owner, *kv_all, *qd_all)
-    stats_all = [stats, move(stats, member=1), move(stats, side=1), move(stats, side=1, member=1)]
-    outs = call(
+    stats_side = move(stats, side=1)
+    blocks[count - 1], blocks[1] = after((up, down), stats_side)
+    up, down = around(blocks[count - 1], 1), around(blocks[1], -1)
+    grads_shape = (planes * half, 2 * DH)
+    keep, give, slopes = call(
         functools.partial(grads_kernel, planes),
-        [SMEM] * 2 + [VMEM] * (planes + 8),
-        tuple(shape((half, 2 * DH), bf16 if j else f32) for j in range(planes))
-        + (shape((4, planes * half, tok_dev * width // DH), bf16),),
-    )(ids, stretch_owner, *kv_all, *qd_all, *stats_all)
-    kv_parts, slopes = outs[:planes], outs[planes]
+        [SMEM] * 2 + [VMEM] * (planes + 2 * SIDES),
+        (
+            shape(grads_shape, f32),
+            shape(grads_shape, bf16),
+            shape((SIDES, planes * tok_dev, tok_dev * width // DH), bf16),
+        ),
+        scratch_shapes=[pltpu.VMEM((planes * tok_dev, 2 * DH), f32)],
+    )(ids, stretch_owner, *kv_all, *qd_all, stats, stats_side)
+    kv_parts = call(
+        members_kernel,
+        [VMEM] * 2,
+        tuple(shape((half, 2 * DH), bf16 if j else f32) for j in range(planes)),
+    )(keep, move(give, member=1))
     piece = call(sum_kernel, [VMEM] * planes, shape((half, 2 * DH), bf16))(
         kv_parts[0], *[move(kv_parts[j], plane=j) for j in range(1, planes)]
     )
-    piece_all = call(join_kernel, [VMEM] * planes, shape((planes * half, 2 * DH), bf16))(
-        piece, *[move(piece, plane=j) for j in range(1, planes)]
-    )
-    near = [
-        piece_all,
-        move(piece_all, side=1),
-        move(piece_all, group=1),
-        move(piece_all, side=1, group=1),
-    ]
+    blocks[count - 2], blocks[2] = after((up, down), piece)
+    up, down = around(blocks[count - 2], 1), around(blocks[2], -1)
+    (piece,) = after((piece,), blocks[2])
+    parts = [move(piece, plane=j) for j in range(1, planes)]
+    piece_all = call(join_kernel, [VMEM] * planes, shape(grads_shape, bf16))(piece, *parts)
+    blocks[count - 3], blocks[3] = up, down
+    up, down = halves_after(up, down, piece_all)
+    blocks[4], blocks[count] = around(up, 1), around(down, -1)
+    piece_side = move(piece_all, side=1)
+    (piece_side,) = after((piece_side,), up)
+    near = [piece_all, piece_side, move(piece_all, group=1), move(piece_side, group=1)]
     pieces = near + [move(part, member=1) for part in near]
 
     q_parts = call(
         functools.partial(query_kernel, planes),
-        [VMEM] * (planes + 1) + [ANY],
-        tuple(shape((tok_dev, width), bf16 if j else f32) for j in range(4)),
-    )(*kv_all, slopes, pieces[-1])
-    query_grad = call(sum_kernel, [VMEM] * 4, shape((tok_dev, width), bf16))(
-        q_parts[0],
-        move(q_parts[1], member=1),
-        move(q_parts[2], side=1),
-        move(q_parts[3], side=1, member=1),
-    )
-
-    steps = 4
+        [VMEM] * (planes + 1) + [ANY] * 2,
+        tuple(shape((tok_dev, width), bf16 if j else f32) for j in range(SIDES)),
+    )(*kv_all, slopes, piece, squares)
+    query_grad = call(sum_kernel, [VMEM] * SIDES, shape((tok_dev, width), bf16))(
+        q_parts[0], move(q_parts[1], side=1)
+    )
+
+    steps = 2
+    hidden_all = [
+        pltpu.with_memory_space_constraint(blocks[r], pltpu.HBM) for r in range(count + 1)
+    ]
     raw, sums = call(
         functools.partial(project_kernel, planes, steps),
-        [SMEM, VMEM, ANY] + [VMEM] * len(pieces),
+        [SMEM, VMEM] + [ANY] * (count + 1) + [VMEM] * len(pieces),
         (pltpu.VMEM((rows, columns), f32), shape((8, columns), f32)),
-        mib=24,
+        mib=12,
         scratch_shapes=[
             pltpu.VMEM((total, columns), bf16),
-            pltpu.VMEM(turned.shape, bf16),
-            pltpu.SemaphoreType.DMA((steps,)),
+            pltpu.VMEM((count,) + hidden.shape, bf16),
+            pltpu.SemaphoreType.DMA((steps, count + 1)),
         ],
-    )(ids, squares, pltpu.with_memory_space_constraint(turned, pltpu.HBM), *pieces)
+    )(ids, squares, *hidden_all, *pieces)
     sums_all = [sums, move(sums, member=1), move(sums, group=1), move(sums, group=1, member=1)]
     steps = 8
     key_grad, value_grad = pl.pallas_call(
@@ -581,7 +635,7 @@
         out_specs=(ANY, ANY),
         scratch_shapes=[pltpu.VMEM((rows, columns // 2), f32)] * 2
         + [pltpu.SemaphoreType.DMA((2 * steps,))],
-        compiler_params=pltpu.CompilerParams(vmem_limit_bytes=24 * 2**20),
+        compiler_params=pltpu.CompilerParams(vmem_limit_bytes=8 * 2**20),
     )(*sums_all, pltpu.with_memory_space_constraint(raw, pltpu.VMEM))
     return (query_grad, key_grad, value_grad)
 
@@ -595,7 +649,8 @@
         gathered = hidden.size // fsdp_count * hidden.dtype.itemsize
         planes = ctx_count // SIDES
         small = (
-            gathered <= GATHER_LIMIT
+            ctx_count == 8
+            and gathered <= GATHER_LIMIT
             and planes * SIDES == ctx_count
             and planes & (planes - 1) == 0
             and heads * MEMBERS == HPG

time: 89.9 us -> 82.7 us (0.920)
  between operations: 14.2 us -> 0.93 us
  starting transfers between devices: 26.7 us -> 31.9 us
  waiting for transfers between devices: 31.1 us -> 34.5 us
  Pallas kernels: 16.9 us -> 14.3 us
    ppermute x0 -> x8, starting transfers between devices: none -> 8.28 us  [around(): return lax.ppermute(x, 'ctx', pairs)]
    ppermute x28 -> x23, waiting for transfers between devices: 31.1 us -> 34.4 us  [move(): return lax.ppermute(x, ('ctx', 'fsdp'), pairs)]
    ppermute x28 -> x23, starting transfers between devices: 26.7 us -> 23.7 us  [move(): return lax.ppermute(x, ('ctx', 'fsdp'), pairs)]
    pallas_call x5 -> x11, Pallas kernels: 9.26 us -> 7.56 us  [the longest x1 4.96 us: local_small(): call(functools.partial(project_kernel, planes, steps), [SMEM, VMEM] + [AN...]
  transfers between devices with their start and end apart: 29 -> 31, of which waited for: 14 -> 13; matrix products, arithmetic and copies ran while one was open for 0% -> 0% of each run, Pallas kernels for 13% -> 13%
where the time goes in v4:
time: 82.7 us; the launch traced here: 82.5 us
  waiting for transfers between devices  34.5 us (42%)
  starting transfers between devices  31.9 us (39%)
  Pallas kernels  14.3 us (17%)
  between operations  0.93 us (1%)
    ppermute x23, waiting for transfers between devices, move(): return lax.ppermute(x, ('ctx', 'fsdp'), pairs)  34.4 us
    ppermute x23, starting transfers between devices, move(): return lax.ppermute(x, ('ctx', 'fsdp'), pairs)  23.7 us
    ppermute x8, starting transfers between devices, around(): return lax.ppermute(x, 'ctx', pairs)  8.28 us
    pallas_call x1, Pallas kernels, local_small(): call(functools.partial(project_kernel, planes, steps), [SMEM, VMEM] + [AN...  4.96 us
    pallas_call x1, Pallas kernels, local_small(): pl.pallas_call(functools.partial(scale_kernel, CLIP_RATE * total, steps),...  2.17 us
    pallas_call x1, Pallas kernels, local_small(): call(functools.partial(grads_kernel, planes), [SMEM] * 2 + [VMEM] * (plan...  2.08 us
    pallas_call x1, Pallas kernels, local_small(): call(pack_kernel, [SMEM] + [ANY] * 6, (shape((tok_dev, 2 * DH), bf16), sh...  1.82 us
    pallas_call x1, Pallas kernels, local_small(): call(functools.partial(stats_kernel, planes), [SMEM] * 2 + [VMEM] * (plan...  1.69 us
  transfers between devices with their start and end apart: 31, of which 13 were waited for; matrix products, arithmetic and copies ran while one was open for 0% of the time, Pallas kernels for 13%

profile of v4, /device:TPU:0, one launch (start us, length us, event | category | flops | bytes accessed | tf_op | source)
XLA Modules:
  0.0 82.5 jit_solution(3341932118905893731)
XLA Ops:
  0.8 1.8 %shard_map.112 = (bf16[128,256]{1,0:T(8,128)(2,1)S(1)}, bf16[272,512]{1,0:T(8,128)(2,1)S(1)}, bf16[128,2048]{1,0:T(8,128)(2,1)S(1)}) custom-call(s32[4]{0:T(128)S(1)} %pad_add_fusion.ids, bf16[128,256]{1,0:T(8,128)(2,1)} %keys.1, bf16[128,256]{1,0:T(8,128)(2,1)} %values.1, bf16[128,512]{1,0:T(8,128)(2,1)} %queries.1, bf16[128,512]{1,0:T(8,128)(2,1)} %out_grad.1, ...), custom_call_target="tpu_custom_call" | custom-call | tf_op jit(solution)/shard_map/pallas_call | solution.py:531
  2.6 3.0 %collective-permute-start.3 = (bf16[272,512]{1,0:T(8,128)(2,1)S(1)}, bf16[272,512]{1,0:T(8,128)(2,1)S(1)}, u32[]{:S(2)}, u32[]{:S(2)}) collective-permute-start(bf16[272,512]{1,0:T(8,128)(2,1)S(1)} %get-tuple-element.26.refs_4_), channel_id=1, source_target_pairs={{0,4},{1,5},{2,6},{3,7},{4,0},{5,1},{6,2},{7,3},{8,12},{9,13},{10,... | collective-permute-start | bytes 835592 | tf_op jit(solution)/shard_map/ppermute | solution.py:517
  5.6 3.6 %collective-permute-start.2 = (bf16[128,256]{1,0:T(8,128)(2,1)S(1)}, bf16[128,256]{1,0:T(8,128)(2,1)S(1)}, u32[]{:S(2)}, u32[]{:S(2)}) collective-permute-start(bf16[128,256]{1,0:T(8,128)(2,1)S(1)} %get-tuple-element.25.refs_0_), channel_id=1, source_target_pairs={{0,24},{1,25},{2,26},{3,27},{4,28},{5,29},{6,30},{7,31},{8,16},{9,... | collective-permute-start | bytes 196616 | tf_op jit(solution)/shard_map/ppermute | solution.py:517
  10.0 2.5 %collective-permute-done.2.refs_3_.refs_4_ = bf16[128,256]{1,0:T(8,128)(2,1)S(1)} collective-permute-done((bf16[128,256]{1,0:T(8,128)(2,1)S(1)}, bf16[128,256]{1,0:T(8,128)(2,1)S(1)}, u32[]{:S(2)}, u32[]{:S(2)}) %collective-permute-start.2) | collective-permute-done | bytes 65568 | tf_op jit(solution)/shard_map/ppermute | solution.py:517
  12.4 2.1 %collective-permute-done.1.refs_2_.refs_3_ = bf16[128,256]{1,0:T(8,128)(2,1)S(1)} collective-permute-done((bf16[128,256]{1,0:T(8,128)(2,1)S(1)}, bf16[128,256]{1,0:T(8,128)(2,1)S(1)}, u32[]{:S(2)}, u32[]{:S(2)}) %collective-permute-start.1) | collective-permute-done | bytes 65568 | tf_op jit(solution)/shard_map/ppermute | solution.py:517
  15.1 1.6 %collective-permute-start.9 = (bf16[128,2048]{1,0:T(8,128)(2,1)S(1)}, bf16[128,2048]{1,0:T(8,128)(2,1)S(1)}, u32[]{:S(2)}, u32[]{:S(2)}) collective-permute-start(bf16[128,2048]{1,0:T(8,128)(2,1)S(1)} %shard_map.117.refs_0_), channel_id=1, source_target_pairs={{0,8},{8,16},{16,24},{24,28},{28,20},{20,12},{12,4},{4,0},{1,9},{9... | collective-permute-start | bytes 1572872 | tf_op jit(solution)/shard_map/ppermute | solution.py:523
  16.7 1.7 %shard_map.113.refs_6_ = f32[24,128]{1,0:T(8,128)S(1)} custom-call(s32[4]{0:T(128)S(1)} %pad_add_fusion.ids, s32[8]{0:T(128)S(1)} %copy-done.9, bf16[128,256]{1,0:T(8,128)(2,1)S(1)} %get-tuple-element.25.refs_0_, bf16[128,256]{1,0:T(8,128)(2,1)S(1)} %collective-permute-done.refs_1_.refs_2_, bf16[128,256]{1,0:T(8,128)(2,1)S(1)} %collective-permute-done.1.refs_2_.refs_3_, ...), custom_call_target="tpu_custom_call" | custom-call | tf_op jit(solution)/shard_map/pallas_call | solution.py:565
  18.9 9.5 %collective-permute-done.4.refs_7_.refs_2_ = f32[24,128]{1,0:T(8,128)S(1)} collective-permute-done((f32[24,128]{1,0:T(8,128)S(1)}, f32[24,128]{1,0:T(8,128)S(1)}, u32[]{:S(2)}, u32[]{:S(2)}) %collective-permute-start.4) | collective-permute-done | bytes 12320 | tf_op jit(solution)/shard_map/ppermute | solution.py:517
  30.5 2.1 %shard_map.114 = (f32[256,256]{1,0:T(8,128)S(1)}, bf16[256,256]{1,0:T(8,128)(2,1)S(1)}, bf16[2,512,512]{2,1,0:T(8,128)(2,1)S(1)}) custom-call(s32[4]{0:T(128)S(1)} %pad_add_fusion.ids, s32[8]{0:T(128)S(1)} %copy-done.9, bf16[128,256]{1,0:T(8,128)(2,1)S(1)} %get-tuple-element.25.refs_0_, bf16[128,256]{1,0:T(8,128)(2,1)S(1)} %collective-permute-done.refs_1_.refs_2_, ...), custom_call_target="tpu_custom_call" | custom-call | tf_op jit(solution)/shard_map/pallas_call | solution.py:574
  32.7 1.3 %collective-permute-done.5.got = bf16[256,256]{1,0:T(8,128)(2,1)S(1)} collective-permute-done((bf16[256,256]{1,0:T(8,128)(2,1)S(1)}, bf16[256,256]{1,0:T(8,128)(2,1)S(1)}, u32[]{:S(2)}, u32[]{:S(2)}) %collective-permute-start.5) | collective-permute-done | bytes 131104 | tf_op jit(solution)/shard_map/ppermute | solution.py:517
  34.1 1.2 %collective-permute-start.6 = (bf16[64,256]{1,0:T(8,128)(2,1)S(1)}, bf16[64,256]{1,0:T(8,128)(2,1)S(1)}, u32[]{:S(2)}, u32[]{:S(2)}) collective-permute-start(bf16[64,256]{1,0:T(8,128)(2,1)S(1)} %get-tuple-element.31), channel_id=1, source_target_pairs={{0,8},{1,9},{2,10},{3,11},{4,12},{5,13},{6,14},{7,15},{8,0},{9,1},... | collective-permute-start | bytes 98312 | tf_op jit(solution)/shard_map/ppermute | solution.py:517
  36.1 2.4 %collective-permute-start.8 = (bf16[64,256]{1,0:T(8,128)(2,1)S(1)}, bf16[64,256]{1,0:T(8,128)(2,1)S(1)}, u32[]{:S(2)}, u32[]{:S(2)}) collective-permute-start(bf16[64,256]{1,0:T(8,128)(2,1)S(1)} %get-tuple-element.33), channel_id=1, source_target_pairs={{0,24},{1,25},{2,26},{3,27},{4,28},{5,29},{6,30},{7,31},{8,16},{9,... | collective-permute-start | bytes 98312 | tf_op jit(solution)/shard_map/ppermute | solution.py:517
  38.5 4.7 %collective-permute-done.6.refs_1_ = bf16[64,256]{1,0:T(8,128)(2,1)S(1)} collective-permute-done((bf16[64,256]{1,0:T(8,128)(2,1)S(1)}, bf16[64,256]{1,0:T(8,128)(2,1)S(1)}, u32[]{:S(2)}, u32[]{:S(2)}) %collective-permute-start.6) | collective-permute-done | bytes 32800 | tf_op jit(solution)/shard_map/ppermute | solution.py:517
  45.8 2.0 %collective-permute-start.18 = (bf16[64,256]{1,0:T(8,128)(2,1)S(1)}, bf16[64,256]{1,0:T(8,128)(2,1)S(1)}, u32[]{:S(2)}, u32[]{:S(2)}) collective-permute-start(bf16[64,256]{1,0:T(8,128)(2,1)S(1)} %shard_map.120.refs_5_.refs_0_), channel_id=1, source_target_pairs={{0,24},{1,25},{2,26},{3,27},{4,28},{5,29},{6,30},{7,31},{8,16},{9,... | collective-permute-start | bytes 98312 | tf_op jit(solution)/shard_map/ppermute | solution.py:517
  48.2 2.0 %collective-permute-start.16 = (bf16[64,256]{1,0:T(8,128)(2,1)S(1)}, bf16[64,256]{1,0:T(8,128)(2,1)S(1)}, u32[]{:S(2)}, u32[]{:S(2)}) collective-permute-start(bf16[64,256]{1,0:T(8,128)(2,1)S(1)} %shard_map.120.refs_5_.refs_0_), channel_id=1, source_target_pairs={{0,8},{1,9},{2,10},{3,11},{4,12},{5,13},{6,14},{7,15},{8,0},{9,1},... | collective-permute-start | bytes 98312 | tf_op jit(solution)/shard_map/ppermute | solution.py:517
  50.2 8.0 %collective-permute-done.18.refs_3_ = bf16[64,256]{1,0:T(8,128)(2,1)S(1)} collective-permute-done((bf16[64,256]{1,0:T(8,128)(2,1)S(1)}, bf16[64,256]{1,0:T(8,128)(2,1)S(1)}, u32[]{:S(2)}, u32[]{:S(2)}) %collective-permute-start.18) | collective-permute-done | bytes 32800 | tf_op jit(solution)/shard_map/ppermute | solution.py:517
  58.3 1.6 %collective-permute-start.22 = (bf16[256,256]{1,0:T(8,128)(2,1)S(1)}, bf16[256,256]{1,0:T(8,128)(2,1)S(1)}, u32[]{:S(2)}, u32[]{:S(2)}) collective-permute-start(bf16[256,256]{1,0:T(8,128)(2,1)S(1)} %shard_map.124.refs_2_.refs_9_), channel_id=1, source_target_pairs={{0,2},{1,3},{2,0},{3,1},{4,6},{5,7},{6,4},{7,5},{8,10},{9,11},{10,... | collective-permute-start | bytes 393224 | tf_op jit(solution)/shard_map/ppermute | solution.py:517
  60.0 2.0 %collective-permute-start.20 = (bf16[64,2048]{1,0:T(8,128)(2,1)S(1)}, bf16[64,2048]{1,0:T(8,128)(2,1)S(1)}, u32[]{:S(2)}, u32[]{:S(2)}) collective-permute-start(bf16[64,2048]{1,0:T(8,128)(2,1)S(1)} %get-tuple-element.42), channel_id=1, source_target_pairs={{0,4},{8,0},{16,8},{24,16},{28,24},{20,28},{12,20},{4,12},{1,5},{9... | collective-permute-start | bytes 786440 | tf_op jit(solution)/shard_map/ppermute | solution.py:523
  63.2 1.5 %collective-permute-start.23 = (bf16[256,256]{1,0:T(8,128)(2,1)S(1)}, bf16[256,256]{1,0:T(8,128)(2,1)S(1)}, u32[]{:S(2)}, u32[]{:S(2)}) collective-permute-start(bf16[256,256]{1,0:T(8,128)(2,1)S(1)} %shard_map.126.refs_10_), channel_id=1, source_target_pairs={{0,2},{1,3},{2,0},{3,1},{4,6},{5,7},{6,4},{7,5},{8,10},{9,11},{10,... | collective-permute-start | bytes 393224 | tf_op jit(solution)/shard_map/ppermute | solution.py:517
  65.3 2.9 %collective-permute-done.23.refs_12_ = bf16[256,256]{1,0:T(8,128)(2,1)S(1)} collective-permute-done((bf16[256,256]{1,0:T(8,128)(2,1)S(1)}, bf16[256,256]{1,0:T(8,128)(2,1)S(1)}, u32[]{:S(2)}, u32[]{:S(2)}) %collective-permute-start.23) | collective-permute-done | bytes 131104 | tf_op jit(solution)/shard_map/ppermute | solution.py:517
  69.1 1.2 %collective-permute-start.13 = (bf16[128,512]{1,0:T(8,128)(2,1)S(1)}, bf16[128,512]{1,0:T(8,128)(2,1)S(1)}, u32[]{:S(2)}, u32[]{:S(2)}) collective-permute-start(bf16[128,512]{1,0:T(8,128)(2,1)S(1)} %get-tuple-element.39), channel_id=1, source_target_pairs={{0,4},{1,5},{2,6},{3,7},{4,0},{5,1},{6,2},{7,3},{8,12},{9,13},{10,... | collective-permute-start | bytes 393224 | tf_op jit(solution)/shard_map/ppermute | solution.py:517
  71.1 5.0 %shard_map.127 = (f32[2048,512]{1,0:T(8,128)S(1)}, f32[8,512]{1,0:T(8,128)S(1)}) custom-call(s32[4]{0:T(128)S(1)} %pad_add_fusion.ids, f32[8,512]{1,0:T(8,128)S(1)} %shard_map.121.refs_6_.squares, bf16[128,2048]{1,0:T(8,128)(2,1)} %copy-done.1, bf16[128,2048]{1,0:T(8,128)(2,1)} %copy-done.5, bf16[128,2048]{1,0:T(8,128)(2,1)} %copy-done, ...), custom_call_target="tpu_custom_call" | custom-call | tf_op jit(solution)/shard_map/pallas_call | solution.py:618
  76.6 1.4 %collective-permute-start.29 = (f32[8,512]{1,0:T(8,128)S(1)}, f32[8,512]{1,0:T(8,128)S(1)}, u32[]{:S(2)}, u32[]{:S(2)}) collective-permute-start(f32[8,512]{1,0:T(8,128)S(1)} %get-tuple-element.43.sums), channel_id=1, source_target_pairs={{0,2},{1,3},{2,0},{3,1},{4,6},{5,7},{6,4},{7,5},{8,10},{9,11},{10,... | collective-permute-start | bytes 49160 | tf_op jit(solution)/shard_map/ppermute | solution.py:517
  80.3 2.2 %shard_map.128 = (f32[2048,256]{1,0:T(8,128)}, f32[2048,256]{1,0:T(8,128)}) custom-call(f32[8,512]{1,0:T(8,128)S(1)} %get-tuple-element.43.sums, f32[8,512]{1,0:T(8,128)S(1)} %collective-permute-done.28.sums_1, f32[8,512]{1,0:T(8,128)S(1)} %collective-permute-done.29.sums_2, f32[8,512]{1,0:T(8,128)S(1)} %collective-permute-done.30.sums_3, ...), custom_call_target="tpu_custom_call" | custom-call | tf_op jit(solution)/shard_map/pallas_call | solution.py:631
  (80 shorter events, 14.5 us)
Async XLA Ops:
  2.6 12.0 %collective-permute-start.3 = (bf16[272,512]{1,0:T(8,128)(2,1)S(1)}, bf16[272,512]{1,0:T(8,128)(2,1)S(1)}, u32[]{:S(2)}, u32[]{:S(2)}) collective-permute-start(bf16[272,512]{1,0:T(8,128)(2,1)S(1)} %get-tuple-element.26.refs_4_), channel_id=1, source_target_pairs={{0,4},{1,5},{2,6},{3,7},{4,0},{5,1},{6,2},{7,3},{8,12},{9,13},{10,... | collective-permute-start | bytes 835592 | tf_op jit(solution)/shard_map/ppermute | solution.py:517
  5.6 6.9 %collective-permute-start.2 = (bf16[128,256]{1,0:T(8,128)(2,1)S(1)}, bf16[128,256]{1,0:T(8,128)(2,1)S(1)}, u32[]{:S(2)}, u32[]{:S(2)}) collective-permute-start(bf16[128,256]{1,0:T(8,128)(2,1)S(1)} %get-tuple-element.25.refs_0_), channel_id=1, source_target_pairs={{0,24},{1,25},{2,26},{3,27},{4,28},{5,29},{6,30},{7,31},{8,16},{9,... | collective-permute-start | bytes 196616 | tf_op jit(solution)/shard_map/ppermute | solution.py:517
  9.2 5.4 %collective-permute-start.1 = (bf16[128,256]{1,0:T(8,128)(2,1)S(1)}, bf16[128,256]{1,0:T(8,128)(2,1)S(1)}, u32[]{:S(2)}, u32[]{:S(2)}) collective-permute-start(bf16[128,256]{1,0:T(8,128)(2,1)S(1)} %get-tuple-element.25.refs_0_), channel_id=1, source_target_pairs={{0,16},{1,17},{2,18},{3,19},{4,20},{5,21},{6,22},{7,23},{8,24},{9,... | collective-permute-start | bytes 196616 | tf_op jit(solution)/shard_map/ppermute | solution.py:517
  9.2 5.4 %collective-permute-start = (bf16[128,256]{1,0:T(8,128)(2,1)S(1)}, bf16[128,256]{1,0:T(8,128)(2,1)S(1)}, u32[]{:S(2)}, u32[]{:S(2)}) collective-permute-start(bf16[128,256]{1,0:T(8,128)(2,1)S(1)} %get-tuple-element.25.refs_0_), channel_id=1, source_target_pairs={{0,8},{1,9},{2,10},{3,11},{4,12},{5,13},{6,14},{7,15},{8,0},{9,1},... | collective-permute-start | bytes 196616 | tf_op jit(solution)/shard_map/ppermute | solution.py:517
  14.6 13.8 %collective-permute-start.10 = (bf16[128,2048]{1,0:T(8,128)(2,1)S(1)}, bf16[128,2048]{1,0:T(8,128)(2,1)S(1)}, u32[]{:S(2)}, u32[]{:S(2)}) collective-permute-start(bf16[128,2048]{1,0:T(8,128)(2,1)S(1)} %shard_map.117.refs_0_), channel_id=1, source_target_pairs={{0,4},{8,0},{16,8},{24,16},{28,24},{20,28},{12,20},{4,12},{1,5},{9... | collective-permute-start | bytes 1572872 | tf_op jit(solution)/shard_map/ppermute | solution.py:523
  15.1 13.3 %collective-permute-start.9 = (bf16[128,2048]{1,0:T(8,128)(2,1)S(1)}, bf16[128,2048]{1,0:T(8,128)(2,1)S(1)}, u32[]{:S(2)}, u32[]{:S(2)}) collective-permute-start(bf16[128,2048]{1,0:T(8,128)(2,1)S(1)} %shard_map.117.refs_0_), channel_id=1, source_target_pairs={{0,8},{8,16},{16,24},{24,28},{28,20},{20,12},{12,4},{4,0},{1,9},{9... | collective-permute-start | bytes 1572872 | tf_op jit(solution)/shard_map/ppermute | solution.py:523
  18.4 10.1 %collective-permute-start.4 = (f32[24,128]{1,0:T(8,128)S(1)}, f32[24,128]{1,0:T(8,128)S(1)}, u32[]{:S(2)}, u32[]{:S(2)}) collective-permute-start(f32[24,128]{1,0:T(8,128)S(1)} %shard_map.113.refs_6_), channel_id=1, source_target_pairs={{0,4},{1,5},{2,6},{3,7},{4,0},{5,1},{6,2},{7,3},{8,12},{9,13},{10,... | collective-permute-start | bytes 36872 | tf_op jit(solution)/shard_map/ppermute | solution.py:517
  28.4 15.2 %collective-permute-start.11 = (bf16[128,2048]{1,0:T(8,128)(2,1)S(1)}, bf16[128,2048]{1,0:T(8,128)(2,1)S(1)}, u32[]{:S(2)}, u32[]{:S(2)}) collective-permute-start(bf16[128,2048]{1,0:T(8,128)(2,1)S(1)} %get-tuple-element.35.refs_7_), channel_id=1, source_target_pairs={{0,8},{8,16},{16,24},{24,28},{28,20},{20,12},{12,4},{4,0},{1,9},{9... | collective-permute-start | bytes 1572872 | tf_op jit(solution)/shard_map/ppermute | solution.py:523
  29.7 14.0 %collective-permute-start.12 = (bf16[128,2048]{1,0:T(8,128)(2,1)S(1)}, bf16[128,2048]{1,0:T(8,128)(2,1)S(1)}, u32[]{:S(2)}, u32[]{:S(2)}) collective-permute-start(bf16[128,2048]{1,0:T(8,128)(2,1)S(1)} %get-tuple-element.36.refs_1_), channel_id=1, source_target_pairs={{0,4},{8,0},{16,8},{24,16},{28,24},{20,28},{12,20},{4,12},{1,5},{9... | collective-permute-start | bytes 1572872 | tf_op jit(solution)/shard_map/ppermute | solution.py:523
  34.1 9.1 %collective-permute-start.6 = (bf16[64,256]{1,0:T(8,128)(2,1)S(1)}, bf16[64,256]{1,0:T(8,128)(2,1)S(1)}, u32[]{:S(2)}, u32[]{:S(2)}) collective-permute-start(bf16[64,256]{1,0:T(8,128)(2,1)S(1)} %get-tuple-element.31), channel_id=1, source_target_pairs={{0,8},{1,9},{2,10},{3,11},{4,12},{5,13},{6,14},{7,15},{8,0},{9,1},... | collective-permute-start | bytes 98312 | tf_op jit(solution)/shard_map/ppermute | solution.py:517
  35.3 8.4 %collective-permute-start.7 = (bf16[64,256]{1,0:T(8,128)(2,1)S(1)}, bf16[64,256]{1,0:T(8,128)(2,1)S(1)}, u32[]{:S(2)}, u32[]{:S(2)}) collective-permute-start(bf16[64,256]{1,0:T(8,128)(2,1)S(1)} %get-tuple-element.32), channel_id=1, source_target_pairs={{0,16},{1,17},{2,18},{3,19},{4,20},{5,21},{6,22},{7,23},{8,24},{9,... | collective-permute-start | bytes 98312 | tf_op jit(solution)/shard_map/ppermute | solution.py:517
  36.1 7.5 %collective-permute-start.8 = (bf16[64,256]{1,0:T(8,128)(2,1)S(1)}, bf16[64,256]{1,0:T(8,128)(2,1)S(1)}, u32[]{:S(2)}, u32[]{:S(2)}) collective-permute-start(bf16[64,256]{1,0:T(8,128)(2,1)S(1)} %get-tuple-element.33), channel_id=1, source_target_pairs={{0,24},{1,25},{2,26},{3,27},{4,28},{5,29},{6,30},{7,31},{8,16},{9,... | collective-permute-start | bytes 98312 | tf_op jit(solution)/shard_map/ppermute | solution.py:517
  43.7 16.1 %collective-permute-start.15 = (bf16[128,2048]{1,0:T(8,128)(2,1)S(1)}, bf16[128,2048]{1,0:T(8,128)(2,1)S(1)}, u32[]{:S(2)}, u32[]{:S(2)}) collective-permute-start(bf16[128,2048]{1,0:T(8,128)(2,1)S(1)} %get-tuple-element.40.refs_6_), channel_id=1, source_target_pairs={{0,8},{8,16},{16,24},{24,28},{28,20},{20,12},{12,4},{4,0},{1,9},{9... | collective-permute-start | bytes 1572872 | tf_op jit(solution)/shard_map/ppermute | solution.py:523
  44.7 15.2 %collective-permute-start.14 = (bf16[128,2048]{1,0:T(8,128)(2,1)S(1)}, bf16[128,2048]{1,0:T(8,128)(2,1)S(1)}, u32[]{:S(2)}, u32[]{:S(2)}) collective-permute-start(bf16[128,2048]{1,0:T(8,128)(2,1)S(1)} %get-tuple-element.37.refs_1_.refs_2_), channel_id=1, source_target_pairs={{0,4},{8,0},{16,8},{24,16},{28,24},{20,28},{12,20},{4,12},{1,5},{9... | collective-permute-start | bytes 1572872 | tf_op jit(solution)/shard_map/ppermute | solution.py:523
  45.8 12.4 %collective-permute-start.18 = (bf16[64,256]{1,0:T(8,128)(2,1)S(1)}, bf16[64,256]{1,0:T(8,128)(2,1)S(1)}, u32[]{:S(2)}, u32[]{:S(2)}) collective-permute-start(bf16[64,256]{1,0:T(8,128)(2,1)S(1)} %shard_map.120.refs_5_.refs_0_), channel_id=1, source_target_pairs={{0,24},{1,25},{2,26},{3,27},{4,28},{5,29},{6,30},{7,31},{8,16},{9,... | collective-permute-start | bytes 98312 | tf_op jit(solution)/shard_map/ppermute | solution.py:517
  47.8 10.4 %collective-permute-start.17 = (bf16[64,256]{1,0:T(8,128)(2,1)S(1)}, bf16[64,256]{1,0:T(8,128)(2,1)S(1)}, u32[]{:S(2)}, u32[]{:S(2)}) collective-permute-start(bf16[64,256]{1,0:T(8,128)(2,1)S(1)} %shard_map.120.refs_5_.refs_0_), channel_id=1, source_target_pairs={{0,16},{1,17},{2,18},{3,19},{4,20},{5,21},{6,22},{7,23},{8,24},{9,... | collective-permute-start | bytes 98312 | tf_op jit(solution)/shard_map/ppermute | solution.py:517
  48.2 10.0 %collective-permute-start.16 = (bf16[64,256]{1,0:T(8,128)(2,1)S(1)}, bf16[64,256]{1,0:T(8,128)(2,1)S(1)}, u32[]{:S(2)}, u32[]{:S(2)}) collective-permute-start(bf16[64,256]{1,0:T(8,128)(2,1)S(1)} %shard_map.120.refs_5_.refs_0_), channel_id=1, source_target_pairs={{0,8},{1,9},{2,10},{3,11},{4,12},{5,13},{6,14},{7,15},{8,0},{9,1},... | collective-permute-start | bytes 98312 | tf_op jit(solution)/shard_map/ppermute | solution.py:517
  58.2 5.0 %collective-permute-start.21 = (bf16[256,256]{1,0:T(8,128)(2,1)S(1)}, bf16[256,256]{1,0:T(8,128)(2,1)S(1)}, u32[]{:S(2)}, u32[]{:S(2)}) collective-permute-start(bf16[256,256]{1,0:T(8,128)(2,1)S(1)} %shard_map.124.refs_2_.refs_9_), channel_id=1, source_target_pairs={{0,4},{1,5},{2,6},{3,7},{4,0},{5,1},{6,2},{7,3},{8,12},{9,13},{10,... | collective-permute-start | bytes 393224 | tf_op jit(solution)/shard_map/ppermute | solution.py:517
  58.3 6.5 %collective-permute-start.22 = (bf16[256,256]{1,0:T(8,128)(2,1)S(1)}, bf16[256,256]{1,0:T(8,128)(2,1)S(1)}, u32[]{:S(2)}, u32[]{:S(2)}) collective-permute-start(bf16[256,256]{1,0:T(8,128)(2,1)S(1)} %shard_map.124.refs_2_.refs_9_), channel_id=1, source_target_pairs={{0,2},{1,3},{2,0},{3,1},{4,6},{5,7},{6,4},{7,5},{8,10},{9,11},{10,... | collective-permute-start | bytes 393224 | tf_op jit(solution)/shard_map/ppermute | solution.py:517
  60.0 10.3 %collective-permute-start.20 = (bf16[64,2048]{1,0:T(8,128)(2,1)S(1)}, bf16[64,2048]{1,0:T(8,128)(2,1)S(1)}, u32[]{:S(2)}, u32[]{:S(2)}) collective-permute-start(bf16[64,2048]{1,0:T(8,128)(2,1)S(1)} %get-tuple-element.42), channel_id=1, source_target_pairs={{0,4},{8,0},{16,8},{24,16},{28,24},{20,28},{12,20},{4,12},{1,5},{9... | collective-permute-start | bytes 786440 | tf_op jit(solution)/shard_map/ppermute | solution.py:523
  62.0 8.4 %collective-permute-start.19 = (bf16[64,2048]{1,0:T(8,128)(2,1)S(1)}, bf16[64,2048]{1,0:T(8,128)(2,1)S(1)}, u32[]{:S(2)}, u32[]{:S(2)}) collective-permute-start(bf16[64,2048]{1,0:T(8,128)(2,1)S(1)} %get-tuple-element.41.refs_1_), channel_id=1, source_target_pairs={{0,8},{8,16},{16,24},{24,28},{28,20},{20,12},{12,4},{4,0},{1,9},{9... | collective-permute-start | bytes 786440 | tf_op jit(solution)/shard_map/ppermute | solution.py:523
  63.2 5.0 %collective-permute-start.23 = (bf16[256,256]{1,0:T(8,128)(2,1)S(1)}, bf16[256,256]{1,0:T(8,128)(2,1)S(1)}, u32[]{:S(2)}, u32[]{:S(2)}) collective-permute-start(bf16[256,256]{1,0:T(8,128)(2,1)S(1)} %shard_map.126.refs_10_), channel_id=1, source_target_pairs={{0,2},{1,3},{2,0},{3,1},{4,6},{5,7},{6,4},{7,5},{8,10},{9,11},{10,... | collective-permute-start | bytes 393224 | tf_op jit(solution)/shard_map/ppermute | solution.py:517
  64.8 5.5 %collective-permute-start.25 = (bf16[256,256]{1,0:T(8,128)(2,1)S(1)}, bf16[256,256]{1,0:T(8,128)(2,1)S(1)}, u32[]{:S(2)}, u32[]{:S(2)}) collective-permute-start(bf16[256,256]{1,0:T(8,128)(2,1)S(1)} %shard_map.126.refs_10_), channel_id=1, source_target_pairs={{0,1},{1,0},{2,3},{3,2},{4,5},{5,4},{6,7},{7,6},{8,9},{9,8},{10,11... | collective-permute-start | bytes 393224 | tf_op jit(solution)/shard_map/ppermute | solution.py:517
  69.1 8.9 %collective-permute-start.13 = (bf16[128,512]{1,0:T(8,128)(2,1)S(1)}, bf16[128,512]{1,0:T(8,128)(2,1)S(1)}, u32[]{:S(2)}, u32[]{:S(2)}) collective-permute-start(bf16[128,512]{1,0:T(8,128)(2,1)S(1)} %get-tuple-element.39), channel_id=1, source_target_pairs={{0,4},{1,5},{2,6},{3,7},{4,0},{5,1},{6,2},{7,3},{8,12},{9,13},{10,... | collective-permute-start | bytes 393224 | tf_op jit(solution)/shard_map/ppermute | solution.py:517
  (19 other events, 268.2 us)

commit v5 on v4

--- a/solution.py
+++ b/solution.py
@@ -386,7 +386,7 @@
             out[:, head * DH : (head + 1) * DH] = part.astype(out.dtype)
 
 
-def join_kernel(*refs):
+def join_kernel(event, *refs):
     rows = refs[0].shape[0]
     for i, ref in enumerate(refs[:-1]):
         refs[-1][i * rows : (i + 1) * rows] = ref[...]
@@ -415,21 +415,16 @@
 def project_kernel(planes, steps, ids, squares, *refs):
     count = planes * SIDES
     hidden, refs = refs[: count + 1], refs[count + 1 :]
-    pieces, (raw, sums, grads, held, sems) = refs[:8], refs[8:]
+    pieces, (raw, sums, grads, held) = refs[:8], refs[8:]
     tok_dev = hidden[0].shape[0]
     half = tok_dev // 2
     tile = raw.shape[0] // steps
     mine = jnp.where(ids[1] == 0, ids[0], count - 1 - ids[0])
-    copies = []
-    for i in range(steps):
-        columns = pl.ds(i * tile, tile)
-        for r, source in enumerate(hidden):
-            spot = mine + (r if r < count else count // 2)
-            spot = jnp.where(spot >= count, spot - count, spot)
-            first = half if r == count else 0
-            target = held.at[spot, pl.ds(first, source.shape[0]), columns]
-            copies.append(pltpu.make_async_copy(source.at[:, columns], target, sems.at[i, r]))
-            copies[-1].start()
+    for r, block in enumerate(hidden):
+        spot = mine + (r if r < count else count // 2)
+        spot = jnp.where(spot >= count, spot - count, spot)
+        first = half if r == count else 0
+        held[spot, first : first + block.shape[0]] = block[...]
     for index, piece in enumerate(pieces):
         side = ids[1] ^ (index & 1)
         group = ids[2] ^ ((index >> 1) & 1)
@@ -446,8 +441,6 @@
     width = raw.shape[1]
     acc = jnp.zeros((8, width), jnp.float32)
     for i in range(steps):
-        for copy in copies[i * (count + 1) : (i + 1) * (count + 1)]:
-            copy.wait()
         rows = slice(i * tile, (i + 1) * tile)
         block = held[:, :, rows].reshape(count * tok_dev, tile)
         out = lax.dot_general(
@@ -591,9 +584,15 @@
     )
     blocks[count - 2], blocks[2] = after((up, down), piece)
     up, down = around(blocks[count - 2], 1), around(blocks[2], -1)
-    (piece,) = after((piece,), blocks[2])
     parts = [move(piece, plane=j) for j in range(1, planes)]
-    piece_all = call(join_kernel, [VMEM] * planes, shape(grads_shape, bf16))(piece, *parts)
+    q_parts = call(
+        functools.partial(query_kernel, planes),
+        [VMEM] * (planes + 1) + [ANY] * 2,
+        tuple(shape((tok_dev, width), bf16 if j else f32) for j in range(SIDES)),
+    )(*kv_all, slopes, piece, squares)
+    piece_all = call(join_kernel, [ANY] + [VMEM] * planes, shape(grads_shape, bf16))(
+        q_parts[1], piece, *parts
+    )
     blocks[count - 3], blocks[3] = up, down
     up, down = halves_after(up, down, piece_all)
     blocks[4], blocks[count] = around(up, 1), around(down, -1)
@@ -602,30 +601,21 @@
     near = [piece_all, piece_side, move(piece_all, group=1), move(piece_side, group=1)]
     pieces = near + [move(part, member=1) for part in near]
 
-    q_parts = call(
-        functools.partial(query_kernel, planes),
-        [VMEM] * (planes + 1) + [ANY] * 2,
-        tuple(shape((tok_dev, width), bf16 if j else f32) for j in range(SIDES)),
-    )(*kv_all, slopes, piece, squares)
     query_grad = call(sum_kernel, [VMEM] * SIDES, shape((tok_dev, width), bf16))(
         q_parts[0], move(q_parts[1], side=1)
     )
 
     steps = 2
-    hidden_all = [
-        pltpu.with_memory_space_constraint(blocks[r], pltpu.HBM) for r in range(count + 1)
-    ]
     raw, sums = call(
         functools.partial(project_kernel, planes, steps),
-        [SMEM, VMEM] + [ANY] * (count + 1) + [VMEM] * len(pieces),
+        [SMEM] + [VMEM] * (count + 2 + len(pieces)),
         (pltpu.VMEM((rows, columns), f32), shape((8, columns), f32)),
         mib=12,
         scratch_shapes=[
             pltpu.VMEM((total, columns), bf16),
             pltpu.VMEM((count,) + hidden.shape, bf16),
-            pltpu.SemaphoreType.DMA((steps, count + 1)),
         ],
-    )(ids, squares, *hidden_all, *pieces)
+    )(ids, squares, *[blocks[r] for r in range(count + 1)], *pieces)
     sums_all = [sums, move(sums, member=1), move(sums, group=1), move(sums, group=1, member=1)]
     steps = 8
     key_grad, value_grad = pl.pallas_call(

time: 82.7 us -> 80.2 us (0.970)
  Pallas kernels: 14.3 us -> 12.8 us
    pallas_call x2, Pallas kernels: 4.97 us -> 3.4 us  [the longest x1 3.39 us: local_small(): call(functools.partial(project_kernel, planes, steps), [SMEM] + [VMEM] *...]
    ppermute x23, waiting for transfers between devices: 34.4 us -> 33 us  [move(): return lax.ppermute(x, ('ctx', 'fsdp'), pairs)]
    ppermute x8, waiting for transfers between devices: 0.12 us -> 1.06 us  [around(): return lax.ppermute(x, 'ctx', pairs)]
  transfers between devices with their start and end apart: 31 -> 31, of which waited for: 13 -> 14; matrix products, arithmetic and copies ran while one was open for 0% -> 0% of each run, Pallas kernels for 13% -> 11%
where the time goes in v5:
time: 80.2 us; the launch traced here: 80 us
  waiting for transfers between devices  34.1 us (43%)
  starting transfers between devices  32.2 us (40%)
  Pallas kernels  12.8 us (16%)
  between operations  0.81 us (1%)
    ppermute x23, waiting for transfers between devices, move(): return lax.ppermute(x, ('ctx', 'fsdp'), pairs)  33 us
    ppermute x23, starting transfers between devices, move(): return lax.ppermute(x, ('ctx', 'fsdp'), pairs)  23.9 us
    ppermute x8, starting transfers between devices, around(): return lax.ppermute(x, 'ctx', pairs)  8.31 us
    pallas_call x1, Pallas kernels, local_small(): call(functools.partial(project_kernel, planes, steps), [SMEM] + [VMEM] *...  3.39 us
    pallas_call x1, Pallas kernels, local_small(): pl.pallas_call(functools.partial(scale_kernel, CLIP_RATE * total, steps),...  2.17 us
    pallas_call x1, Pallas kernels, local_small(): call(functools.partial(grads_kernel, planes), [SMEM] * 2 + [VMEM] * (plan...  2.08 us
    pallas_call x1, Pallas kernels, local_small(): call(pack_kernel, [SMEM] + [ANY] * 6, (shape((tok_dev, 2 * DH), bf16), sh...  1.82 us
    pallas_call x1, Pallas kernels, local_small(): call(functools.partial(stats_kernel, planes), [SMEM] * 2 + [VMEM] * (plan...  1.72 us
  transfers between devices with their start and end apart: 31, of which 14 were waited for; matrix products, arithmetic and copies ran while one was open for 0% of the time, Pallas kernels for 11%

profile of v5, /device:TPU:0, one launch (start us, length us, event | category | flops | bytes accessed | tf_op | source)
XLA Modules:
  0.0 80.0 jit_solution(16769622857947106845)
XLA Ops:
  0.8 1.8 %shard_map.112 = (bf16[128,256]{1,0:T(8,128)(2,1)S(1)}, bf16[272,512]{1,0:T(8,128)(2,1)S(1)}, bf16[128,2048]{1,0:T(8,128)(2,1)S(1)}) custom-call(s32[4]{0:T(128)S(1)} %pad_add_fusion.ids, bf16[128,256]{1,0:T(8,128)(2,1)} %keys.1, bf16[128,256]{1,0:T(8,128)(2,1)} %values.1, bf16[128,512]{1,0:T(8,128)(2,1)} %queries.1, bf16[128,512]{1,0:T(8,128)(2,1)} %out_grad.1, ...), custom_call_target="tpu_custom_call" | custom-call | tf_op jit(solution)/shard_map/pallas_call | solution.py:524
  2.6 3.0 %collective-permute-start.3 = (bf16[272,512]{1,0:T(8,128)(2,1)S(1)}, bf16[272,512]{1,0:T(8,128)(2,1)S(1)}, u32[]{:S(2)}, u32[]{:S(2)}) collective-permute-start(bf16[272,512]{1,0:T(8,128)(2,1)S(1)} %get-tuple-element.26.refs_4_), channel_id=1, source_target_pairs={{0,4},{1,5},{2,6},{3,7},{4,0},{5,1},{6,2},{7,3},{8,12},{9,13},{10,... | collective-permute-start | bytes 835592 | tf_op jit(solution)/shard_map/ppermute | solution.py:510
  5.6 3.6 %collective-permute-start.2 = (bf16[128,256]{1,0:T(8,128)(2,1)S(1)}, bf16[128,256]{1,0:T(8,128)(2,1)S(1)}, u32[]{:S(2)}, u32[]{:S(2)}) collective-permute-start(bf16[128,256]{1,0:T(8,128)(2,1)S(1)} %get-tuple-element.25.refs_0_), channel_id=1, source_target_pairs={{0,24},{1,25},{2,26},{3,27},{4,28},{5,29},{6,30},{7,31},{8,16},{9,... | collective-permute-start | bytes 196616 | tf_op jit(solution)/shard_map/ppermute | solution.py:510
  10.0 2.5 %collective-permute-done.2.refs_3_.refs_4_ = bf16[128,256]{1,0:T(8,128)(2,1)S(1)} collective-permute-done((bf16[128,256]{1,0:T(8,128)(2,1)S(1)}, bf16[128,256]{1,0:T(8,128)(2,1)S(1)}, u32[]{:S(2)}, u32[]{:S(2)}) %collective-permute-start.2) | collective-permute-done | bytes 65568 | tf_op jit(solution)/shard_map/ppermute | solution.py:510
  12.4 2.1 %collective-permute-done.1.refs_2_.refs_3_ = bf16[128,256]{1,0:T(8,128)(2,1)S(1)} collective-permute-done((bf16[128,256]{1,0:T(8,128)(2,1)S(1)}, bf16[128,256]{1,0:T(8,128)(2,1)S(1)}, u32[]{:S(2)}, u32[]{:S(2)}) %collective-permute-start.1) | collective-permute-done | bytes 65568 | tf_op jit(solution)/shard_map/ppermute | solution.py:510
  15.1 1.6 %collective-permute-start.10 = (bf16[128,2048]{1,0:T(8,128)(2,1)S(1)}, bf16[128,2048]{1,0:T(8,128)(2,1)S(1)}, u32[]{:S(2)}, u32[]{:S(2)}) collective-permute-start(bf16[128,2048]{1,0:T(8,128)(2,1)S(1)} %shard_map.120.refs_0_), channel_id=1, source_target_pairs={{0,8},{8,16},{16,24},{24,28},{28,20},{20,12},{12,4},{4,0},{1,9},{9... | collective-permute-start | bytes 1572872 | tf_op jit(solution)/shard_map/ppermute | solution.py:516
  16.7 1.7 %shard_map.113.refs_6_ = f32[24,128]{1,0:T(8,128)S(1)} custom-call(s32[4]{0:T(128)S(1)} %pad_add_fusion.ids, s32[8]{0:T(128)S(1)} %copy-done.2, bf16[128,256]{1,0:T(8,128)(2,1)S(1)} %get-tuple-element.25.refs_0_, bf16[128,256]{1,0:T(8,128)(2,1)S(1)} %collective-permute-done.refs_1_.refs_2_, bf16[128,256]{1,0:T(8,128)(2,1)S(1)} %collective-permute-done.1.refs_2_.refs_3_, ...), custom_call_target="tpu_custom_call" | custom-call | tf_op jit(solution)/shard_map/pallas_call | solution.py:558
  18.9 9.5 %collective-permute-done.4.refs_7_.refs_2_ = f32[24,128]{1,0:T(8,128)S(1)} collective-permute-done((f32[24,128]{1,0:T(8,128)S(1)}, f32[24,128]{1,0:T(8,128)S(1)}, u32[]{:S(2)}, u32[]{:S(2)}) %collective-permute-start.4) | collective-permute-done | bytes 12320 | tf_op jit(solution)/shard_map/ppermute | solution.py:510
  28.8 1.7 %collective-permute-start.12 = (bf16[128,2048]{1,0:T(8,128)(2,1)S(1)}, bf16[128,2048]{1,0:T(8,128)(2,1)S(1)}, u32[]{:S(2)}, u32[]{:S(2)}) collective-permute-start(bf16[128,2048]{1,0:T(8,128)(2,1)S(1)} %get-tuple-element.38.refs_7_), channel_id=1, source_target_pairs={{0,8},{8,16},{16,24},{24,28},{28,20},{20,12},{12,4},{4,0},{1,9},{9... | collective-permute-start | bytes 1572872 | tf_op jit(solution)/shard_map/ppermute | solution.py:516
  30.5 2.1 %shard_map.114 = (f32[256,256]{1,0:T(8,128)S(1)}, bf16[256,256]{1,0:T(8,128)(2,1)S(1)}, bf16[2,512,512]{2,1,0:T(8,128)(2,1)S(1)}) custom-call(s32[4]{0:T(128)S(1)} %pad_add_fusion.ids, s32[8]{0:T(128)S(1)} %copy-done.2, bf16[128,256]{1,0:T(8,128)(2,1)S(1)} %get-tuple-element.25.refs_0_, bf16[128,256]{1,0:T(8,128)(2,1)S(1)} %collective-permute-done.refs_1_.refs_2_, ...), custom_call_target="tpu_custom_call" | custom-call | tf_op jit(solution)/shard_map/pallas_call | solution.py:567
  32.7 1.3 %collective-permute-done.5.got = bf16[256,256]{1,0:T(8,128)(2,1)S(1)} collective-permute-done((bf16[256,256]{1,0:T(8,128)(2,1)S(1)}, bf16[256,256]{1,0:T(8,128)(2,1)S(1)}, u32[]{:S(2)}, u32[]{:S(2)}) %collective-permute-start.5) | collective-permute-done | bytes 131104 | tf_op jit(solution)/shard_map/ppermute | solution.py:510
  36.0 2.5 %collective-permute-start.8 = (bf16[64,256]{1,0:T(8,128)(2,1)S(1)}, bf16[64,256]{1,0:T(8,128)(2,1)S(1)}, u32[]{:S(2)}, u32[]{:S(2)}) collective-permute-start(bf16[64,256]{1,0:T(8,128)(2,1)S(1)} %get-tuple-element.33), channel_id=1, source_target_pairs={{0,24},{1,25},{2,26},{3,27},{4,28},{5,29},{6,30},{7,31},{8,16},{9,... | collective-permute-start | bytes 98312 | tf_op jit(solution)/shard_map/ppermute | solution.py:510
  38.5 3.5 %collective-permute-done.6.refs_1_ = bf16[64,256]{1,0:T(8,128)(2,1)S(1)} collective-permute-done((bf16[64,256]{1,0:T(8,128)(2,1)S(1)}, bf16[64,256]{1,0:T(8,128)(2,1)S(1)}, u32[]{:S(2)}, u32[]{:S(2)}) %collective-permute-start.6) | collective-permute-done | bytes 32800 | tf_op jit(solution)/shard_map/ppermute | solution.py:510
  42.0 1.6 %collective-permute-done.7.refs_2_ = bf16[64,256]{1,0:T(8,128)(2,1)S(1)} collective-permute-done((bf16[64,256]{1,0:T(8,128)(2,1)S(1)}, bf16[64,256]{1,0:T(8,128)(2,1)S(1)}, u32[]{:S(2)}, u32[]{:S(2)}) %collective-permute-start.7) | collective-permute-done | bytes 32800 | tf_op jit(solution)/shard_map/ppermute | solution.py:510
  44.4 1.4 %collective-permute-start.15 = (bf16[128,2048]{1,0:T(8,128)(2,1)S(1)}, bf16[128,2048]{1,0:T(8,128)(2,1)S(1)}, u32[]{:S(2)}, u32[]{:S(2)}) collective-permute-start(bf16[128,2048]{1,0:T(8,128)(2,1)S(1)} %get-tuple-element.40.refs_6_), channel_id=1, source_target_pairs={{0,8},{8,16},{16,24},{24,28},{28,20},{20,12},{12,4},{4,0},{1,9},{9... | collective-permute-start | bytes 1572872 | tf_op jit(solution)/shard_map/ppermute | solution.py:516
  45.8 2.8 %collective-permute-start.18 = (bf16[64,256]{1,0:T(8,128)(2,1)S(1)}, bf16[64,256]{1,0:T(8,128)(2,1)S(1)}, u32[]{:S(2)}, u32[]{:S(2)}) collective-permute-start(bf16[64,256]{1,0:T(8,128)(2,1)S(1)} %shard_map.116.refs_5_.refs_2_.refs_0_), channel_id=1, source_target_pairs={{0,24},{1,25},{2,26},{3,27},{4,28},{5,29},{6,30},{7,31},{8,16},{9,... | collective-permute-start | bytes 98312 | tf_op jit(solution)/shard_map/ppermute | solution.py:510
  48.6 1.5 %collective-permute-start.16 = (bf16[64,256]{1,0:T(8,128)(2,1)S(1)}, bf16[64,256]{1,0:T(8,128)(2,1)S(1)}, u32[]{:S(2)}, u32[]{:S(2)}) collective-permute-start(bf16[64,256]{1,0:T(8,128)(2,1)S(1)} %shard_map.116.refs_5_.refs_2_.refs_0_), channel_id=1, source_target_pairs={{0,8},{1,9},{2,10},{3,11},{4,12},{5,13},{6,14},{7,15},{8,0},{9,1},... | collective-permute-start | bytes 98312 | tf_op jit(solution)/shard_map/ppermute | solution.py:510
  50.9 5.8 %collective-permute-done.18.refs_3_ = bf16[64,256]{1,0:T(8,128)(2,1)S(1)} collective-permute-done((bf16[64,256]{1,0:T(8,128)(2,1)S(1)}, bf16[64,256]{1,0:T(8,128)(2,1)S(1)}, u32[]{:S(2)}, u32[]{:S(2)}) %collective-permute-start.18) | collective-permute-done | bytes 32800 | tf_op jit(solution)/shard_map/ppermute | solution.py:510
  58.5 1.5 %collective-permute-start.22 = (bf16[256,256]{1,0:T(8,128)(2,1)S(1)}, bf16[256,256]{1,0:T(8,128)(2,1)S(1)}, u32[]{:S(2)}, u32[]{:S(2)}) collective-permute-start(bf16[256,256]{1,0:T(8,128)(2,1)S(1)} %shard_map.123.refs_2_.refs_9_), channel_id=1, source_target_pairs={{0,2},{1,3},{2,0},{3,1},{4,6},{5,7},{6,4},{7,5},{8,10},{9,11},{10,... | collective-permute-start | bytes 393224 | tf_op jit(solution)/shard_map/ppermute | solution.py:510
  60.1 1.6 %collective-permute-start.20 = (bf16[64,2048]{1,0:T(8,128)(2,1)S(1)}, bf16[64,2048]{1,0:T(8,128)(2,1)S(1)}, u32[]{:S(2)}, u32[]{:S(2)}) collective-permute-start(bf16[64,2048]{1,0:T(8,128)(2,1)S(1)} %get-tuple-element.42), channel_id=1, source_target_pairs={{0,4},{8,0},{16,8},{24,16},{28,24},{20,28},{12,20},{4,12},{1,5},{9... | collective-permute-start | bytes 786440 | tf_op jit(solution)/shard_map/ppermute | solution.py:516
  63.0 1.5 %collective-permute-start.23 = (bf16[256,256]{1,0:T(8,128)(2,1)S(1)}, bf16[256,256]{1,0:T(8,128)(2,1)S(1)}, u32[]{:S(2)}, u32[]{:S(2)}) collective-permute-start(bf16[256,256]{1,0:T(8,128)(2,1)S(1)} %shard_map.125.refs_10_), channel_id=1, source_target_pairs={{0,2},{1,3},{2,0},{3,1},{4,6},{5,7},{6,4},{7,5},{8,10},{9,11},{10,... | collective-permute-start | bytes 393224 | tf_op jit(solution)/shard_map/ppermute | solution.py:510
  65.1 2.9 %collective-permute-done.23.refs_12_ = bf16[256,256]{1,0:T(8,128)(2,1)S(1)} collective-permute-done((bf16[256,256]{1,0:T(8,128)(2,1)S(1)}, bf16[256,256]{1,0:T(8,128)(2,1)S(1)}, u32[]{:S(2)}, u32[]{:S(2)}) %collective-permute-start.23) | collective-permute-done | bytes 131104 | tf_op jit(solution)/shard_map/ppermute | solution.py:510
  70.2 3.4 %shard_map.126 = (f32[2048,512]{1,0:T(8,128)S(1)}, f32[8,512]{1,0:T(8,128)S(1)}) custom-call(s32[4]{0:T(128)S(1)} %pad_add_fusion.ids, f32[8,512]{1,0:T(8,128)S(1)} %shard_map.117.refs_6_.squares, bf16[128,2048]{1,0:T(8,128)(2,1)S(1)} %shard_map.120.refs_0_, bf16[128,2048]{1,0:T(8,128)(2,1)S(1)} %get-tuple-element.37.refs_1_, ...), custom_call_target="tpu_custom_call" | custom-call | tf_op jit(solution)/shard_map/pallas_call | solution.py:609
  77.8 2.2 %shard_map.127 = (f32[2048,256]{1,0:T(8,128)}, f32[2048,256]{1,0:T(8,128)}) custom-call(f32[8,512]{1,0:T(8,128)S(1)} %get-tuple-element.43.sums, f32[8,512]{1,0:T(8,128)S(1)} %collective-permute-done.28.sums_1, f32[8,512]{1,0:T(8,128)S(1)} %collective-permute-done.29.sums_2, f32[8,512]{1,0:T(8,128)S(1)} %collective-permute-done.30.sums_3, ...), custom_call_target="tpu_custom_call" | custom-call | tf_op jit(solution)/shard_map/pallas_call | solution.py:621
  (61 shorter events, 15.9 us)
Async XLA Ops:
  2.6 12.0 %collective-permute-start.3 = (bf16[272,512]{1,0:T(8,128)(2,1)S(1)}, bf16[272,512]{1,0:T(8,128)(2,1)S(1)}, u32[]{:S(2)}, u32[]{:S(2)}) collective-permute-start(bf16[272,512]{1,0:T(8,128)(2,1)S(1)} %get-tuple-element.26.refs_4_), channel_id=1, source_target_pairs={{0,4},{1,5},{2,6},{3,7},{4,0},{5,1},{6,2},{7,3},{8,12},{9,13},{10,... | collective-permute-start | bytes 835592 | tf_op jit(solution)/shard_map/ppermute | solution.py:510
  5.6 6.9 %collective-permute-start.2 = (bf16[128,256]{1,0:T(8,128)(2,1)S(1)}, bf16[128,256]{1,0:T(8,128)(2,1)S(1)}, u32[]{:S(2)}, u32[]{:S(2)}) collective-permute-start(bf16[128,256]{1,0:T(8,128)(2,1)S(1)} %get-tuple-element.25.refs_0_), channel_id=1, source_target_pairs={{0,24},{1,25},{2,26},{3,27},{4,28},{5,29},{6,30},{7,31},{8,16},{9,... | collective-permute-start | bytes 196616 | tf_op jit(solution)/shard_map/ppermute | solution.py:510
  9.2 5.4 %collective-permute-start.1 = (bf16[128,256]{1,0:T(8,128)(2,1)S(1)}, bf16[128,256]{1,0:T(8,128)(2,1)S(1)}, u32[]{:S(2)}, u32[]{:S(2)}) collective-permute-start(bf16[128,256]{1,0:T(8,128)(2,1)S(1)} %get-tuple-element.25.refs_0_), channel_id=1, source_target_pairs={{0,16},{1,17},{2,18},{3,19},{4,20},{5,21},{6,22},{7,23},{8,24},{9,... | collective-permute-start | bytes 196616 | tf_op jit(solution)/shard_map/ppermute | solution.py:510
  9.2 5.4 %collective-permute-start = (bf16[128,256]{1,0:T(8,128)(2,1)S(1)}, bf16[128,256]{1,0:T(8,128)(2,1)S(1)}, u32[]{:S(2)}, u32[]{:S(2)}) collective-permute-start(bf16[128,256]{1,0:T(8,128)(2,1)S(1)} %get-tuple-element.25.refs_0_), channel_id=1, source_target_pairs={{0,8},{1,9},{2,10},{3,11},{4,12},{5,13},{6,14},{7,15},{8,0},{9,1},... | collective-permute-start | bytes 196616 | tf_op jit(solution)/shard_map/ppermute | solution.py:510
  14.6 13.8 %collective-permute-start.11 = (bf16[128,2048]{1,0:T(8,128)(2,1)S(1)}, bf16[128,2048]{1,0:T(8,128)(2,1)S(1)}, u32[]{:S(2)}, u32[]{:S(2)}) collective-permute-start(bf16[128,2048]{1,0:T(8,128)(2,1)S(1)} %shard_map.120.refs_0_), channel_id=1, source_target_pairs={{0,4},{8,0},{16,8},{24,16},{28,24},{20,28},{12,20},{4,12},{1,5},{9... | collective-permute-start | bytes 1572872 | tf_op jit(solution)/shard_map/ppermute | solution.py:516
  15.1 13.3 %collective-permute-start.10 = (bf16[128,2048]{1,0:T(8,128)(2,1)S(1)}, bf16[128,2048]{1,0:T(8,128)(2,1)S(1)}, u32[]{:S(2)}, u32[]{:S(2)}) collective-permute-start(bf16[128,2048]{1,0:T(8,128)(2,1)S(1)} %shard_map.120.refs_0_), channel_id=1, source_target_pairs={{0,8},{8,16},{16,24},{24,28},{28,20},{20,12},{12,4},{4,0},{1,9},{9... | collective-permute-start | bytes 1572872 | tf_op jit(solution)/shard_map/ppermute | solution.py:516
  18.4 10.0 %collective-permute-start.4 = (f32[24,128]{1,0:T(8,128)S(1)}, f32[24,128]{1,0:T(8,128)S(1)}, u32[]{:S(2)}, u32[]{:S(2)}) collective-permute-start(f32[24,128]{1,0:T(8,128)S(1)} %shard_map.113.refs_6_), channel_id=1, source_target_pairs={{0,4},{1,5},{2,6},{3,7},{4,0},{5,1},{6,2},{7,3},{8,12},{9,13},{10,... | collective-permute-start | bytes 36872 | tf_op jit(solution)/shard_map/ppermute | solution.py:510
  28.4 15.2 %collective-permute-start.13 = (bf16[128,2048]{1,0:T(8,128)(2,1)S(1)}, bf16[128,2048]{1,0:T(8,128)(2,1)S(1)}, u32[]{:S(2)}, u32[]{:S(2)}) collective-permute-start(bf16[128,2048]{1,0:T(8,128)(2,1)S(1)} %get-tuple-element.37.refs_1_), channel_id=1, source_target_pairs={{0,4},{8,0},{16,8},{24,16},{28,24},{20,28},{12,20},{4,12},{1,5},{9... | collective-permute-start | bytes 1572872 | tf_op jit(solution)/shard_map/ppermute | solution.py:516
  28.8 14.9 %collective-permute-start.12 = (bf16[128,2048]{1,0:T(8,128)(2,1)S(1)}, bf16[128,2048]{1,0:T(8,128)(2,1)S(1)}, u32[]{:S(2)}, u32[]{:S(2)}) collective-permute-start(bf16[128,2048]{1,0:T(8,128)(2,1)S(1)} %get-tuple-element.38.refs_7_), channel_id=1, source_target_pairs={{0,8},{8,16},{16,24},{24,28},{28,20},{20,12},{12,4},{4,0},{1,9},{9... | collective-permute-start | bytes 1572872 | tf_op jit(solution)/shard_map/ppermute | solution.py:516
  34.0 8.0 %collective-permute-start.6 = (bf16[64,256]{1,0:T(8,128)(2,1)S(1)}, bf16[64,256]{1,0:T(8,128)(2,1)S(1)}, u32[]{:S(2)}, u32[]{:S(2)}) collective-permute-start(bf16[64,256]{1,0:T(8,128)(2,1)S(1)} %get-tuple-element.31), channel_id=1, source_target_pairs={{0,8},{1,9},{2,10},{3,11},{4,12},{5,13},{6,14},{7,15},{8,0},{9,1},... | collective-permute-start | bytes 98312 | tf_op jit(solution)/shard_map/ppermute | solution.py:510
  35.3 8.3 %collective-permute-start.7 = (bf16[64,256]{1,0:T(8,128)(2,1)S(1)}, bf16[64,256]{1,0:T(8,128)(2,1)S(1)}, u32[]{:S(2)}, u32[]{:S(2)}) collective-permute-start(bf16[64,256]{1,0:T(8,128)(2,1)S(1)} %get-tuple-element.32), channel_id=1, source_target_pairs={{0,16},{1,17},{2,18},{3,19},{4,20},{5,21},{6,22},{7,23},{8,24},{9,... | collective-permute-start | bytes 98312 | tf_op jit(solution)/shard_map/ppermute | solution.py:510
  36.0 7.6 %collective-permute-start.8 = (bf16[64,256]{1,0:T(8,128)(2,1)S(1)}, bf16[64,256]{1,0:T(8,128)(2,1)S(1)}, u32[]{:S(2)}, u32[]{:S(2)}) collective-permute-start(bf16[64,256]{1,0:T(8,128)(2,1)S(1)} %get-tuple-element.33), channel_id=1, source_target_pairs={{0,24},{1,25},{2,26},{3,27},{4,28},{5,29},{6,30},{7,31},{8,16},{9,... | collective-permute-start | bytes 98312 | tf_op jit(solution)/shard_map/ppermute | solution.py:510
  43.7 16.4 %collective-permute-start.14 = (bf16[128,2048]{1,0:T(8,128)(2,1)S(1)}, bf16[128,2048]{1,0:T(8,128)(2,1)S(1)}, u32[]{:S(2)}, u32[]{:S(2)}) collective-permute-start(bf16[128,2048]{1,0:T(8,128)(2,1)S(1)} %get-tuple-element.39.refs_2_), channel_id=1, source_target_pairs={{0,4},{8,0},{16,8},{24,16},{28,24},{20,28},{12,20},{4,12},{1,5},{9... | collective-permute-start | bytes 1572872 | tf_op jit(solution)/shard_map/ppermute | solution.py:516
  44.4 15.7 %collective-permute-start.15 = (bf16[128,2048]{1,0:T(8,128)(2,1)S(1)}, bf16[128,2048]{1,0:T(8,128)(2,1)S(1)}, u32[]{:S(2)}, u32[]{:S(2)}) collective-permute-start(bf16[128,2048]{1,0:T(8,128)(2,1)S(1)} %get-tuple-element.40.refs_6_), channel_id=1, source_target_pairs={{0,8},{8,16},{16,24},{24,28},{28,20},{20,12},{12,4},{4,0},{1,9},{9... | collective-permute-start | bytes 1572872 | tf_op jit(solution)/shard_map/ppermute | solution.py:516
  45.8 11.0 %collective-permute-start.18 = (bf16[64,256]{1,0:T(8,128)(2,1)S(1)}, bf16[64,256]{1,0:T(8,128)(2,1)S(1)}, u32[]{:S(2)}, u32[]{:S(2)}) collective-permute-start(bf16[64,256]{1,0:T(8,128)(2,1)S(1)} %shard_map.116.refs_5_.refs_2_.refs_0_), channel_id=1, source_target_pairs={{0,24},{1,25},{2,26},{3,27},{4,28},{5,29},{6,30},{7,31},{8,16},{9,... | collective-permute-start | bytes 98312 | tf_op jit(solution)/shard_map/ppermute | solution.py:510
  48.6 9.4 %collective-permute-start.17 = (bf16[64,256]{1,0:T(8,128)(2,1)S(1)}, bf16[64,256]{1,0:T(8,128)(2,1)S(1)}, u32[]{:S(2)}, u32[]{:S(2)}) collective-permute-start(bf16[64,256]{1,0:T(8,128)(2,1)S(1)} %shard_map.116.refs_5_.refs_2_.refs_0_), channel_id=1, source_target_pairs={{0,16},{1,17},{2,18},{3,19},{4,20},{5,21},{6,22},{7,23},{8,24},{9,... | collective-permute-start | bytes 98312 | tf_op jit(solution)/shard_map/ppermute | solution.py:510
  48.6 9.4 %collective-permute-start.16 = (bf16[64,256]{1,0:T(8,128)(2,1)S(1)}, bf16[64,256]{1,0:T(8,128)(2,1)S(1)}, u32[]{:S(2)}, u32[]{:S(2)}) collective-permute-start(bf16[64,256]{1,0:T(8,128)(2,1)S(1)} %shard_map.116.refs_5_.refs_2_.refs_0_), channel_id=1, source_target_pairs={{0,8},{1,9},{2,10},{3,11},{4,12},{5,13},{6,14},{7,15},{8,0},{9,1},... | collective-permute-start | bytes 98312 | tf_op jit(solution)/shard_map/ppermute | solution.py:510
  58.0 5.0 %collective-permute-start.21 = (bf16[256,256]{1,0:T(8,128)(2,1)S(1)}, bf16[256,256]{1,0:T(8,128)(2,1)S(1)}, u32[]{:S(2)}, u32[]{:S(2)}) collective-permute-start(bf16[256,256]{1,0:T(8,128)(2,1)S(1)} %shard_map.123.refs_2_.refs_9_), channel_id=1, source_target_pairs={{0,4},{1,5},{2,6},{3,7},{4,0},{5,1},{6,2},{7,3},{8,12},{9,13},{10,... | collective-permute-start | bytes 393224 | tf_op jit(solution)/shard_map/ppermute | solution.py:510
  58.5 6.1 %collective-permute-start.22 = (bf16[256,256]{1,0:T(8,128)(2,1)S(1)}, bf16[256,256]{1,0:T(8,128)(2,1)S(1)}, u32[]{:S(2)}, u32[]{:S(2)}) collective-permute-start(bf16[256,256]{1,0:T(8,128)(2,1)S(1)} %shard_map.123.refs_2_.refs_9_), channel_id=1, source_target_pairs={{0,2},{1,3},{2,0},{3,1},{4,6},{5,7},{6,4},{7,5},{8,10},{9,11},{10,... | collective-permute-start | bytes 393224 | tf_op jit(solution)/shard_map/ppermute | solution.py:510
  60.1 9.0 %collective-permute-start.20 = (bf16[64,2048]{1,0:T(8,128)(2,1)S(1)}, bf16[64,2048]{1,0:T(8,128)(2,1)S(1)}, u32[]{:S(2)}, u32[]{:S(2)}) collective-permute-start(bf16[64,2048]{1,0:T(8,128)(2,1)S(1)} %get-tuple-element.42), channel_id=1, source_target_pairs={{0,4},{8,0},{16,8},{24,16},{28,24},{20,28},{12,20},{4,12},{1,5},{9... | collective-permute-start | bytes 786440 | tf_op jit(solution)/shard_map/ppermute | solution.py:516
  61.7 8.4 %collective-permute-start.19 = (bf16[64,2048]{1,0:T(8,128)(2,1)S(1)}, bf16[64,2048]{1,0:T(8,128)(2,1)S(1)}, u32[]{:S(2)}, u32[]{:S(2)}) collective-permute-start(bf16[64,2048]{1,0:T(8,128)(2,1)S(1)} %get-tuple-element.41.refs_1_), channel_id=1, source_target_pairs={{0,8},{8,16},{16,24},{24,28},{28,20},{20,12},{12,4},{4,0},{1,9},{9... | collective-permute-start | bytes 786440 | tf_op jit(solution)/shard_map/ppermute | solution.py:516
  63.0 5.0 %collective-permute-start.23 = (bf16[256,256]{1,0:T(8,128)(2,1)S(1)}, bf16[256,256]{1,0:T(8,128)(2,1)S(1)}, u32[]{:S(2)}, u32[]{:S(2)}) collective-permute-start(bf16[256,256]{1,0:T(8,128)(2,1)S(1)} %shard_map.125.refs_10_), channel_id=1, source_target_pairs={{0,2},{1,3},{2,0},{3,1},{4,6},{5,7},{6,4},{7,5},{8,10},{9,11},{10,... | collective-permute-start | bytes 393224 | tf_op jit(solution)/shard_map/ppermute | solution.py:510
  64.6 4.6 %collective-permute-start.25 = (bf16[256,256]{1,0:T(8,128)(2,1)S(1)}, bf16[256,256]{1,0:T(8,128)(2,1)S(1)}, u32[]{:S(2)}, u32[]{:S(2)}) collective-permute-start(bf16[256,256]{1,0:T(8,128)(2,1)S(1)} %shard_map.125.refs_10_), channel_id=1, source_target_pairs={{0,1},{1,0},{2,3},{3,2},{4,5},{5,4},{6,7},{7,6},{8,9},{9,8},{10,11... | collective-permute-start | bytes 393224 | tf_op jit(solution)/shard_map/ppermute | solution.py:510
  68.0 7.5 %collective-permute-start.9 = (bf16[128,512]{1,0:T(8,128)(2,1)S(1)}, bf16[128,512]{1,0:T(8,128)(2,1)S(1)}, u32[]{:S(2)}, u32[]{:S(2)}) collective-permute-start(bf16[128,512]{1,0:T(8,128)(2,1)S(1)} %get-tuple-element.35.event), channel_id=1, source_target_pairs={{0,4},{1,5},{2,6},{3,7},{4,0},{5,1},{6,2},{7,3},{8,12},{9,13},{10,... | collective-permute-start | bytes 393224 | tf_op jit(solution)/shard_map/ppermute | solution.py:510
  (10 other events, 108.9 us)

commit v6 on v5

--- a/solution.py
+++ b/solution.py
@@ -386,7 +386,7 @@
             out[:, head * DH : (head + 1) * DH] = part.astype(out.dtype)
 
 
-def join_kernel(event, *refs):
+def join_kernel(event, other_event, *refs):
     rows = refs[0].shape[0]
     for i, ref in enumerate(refs[:-1]):
         refs[-1][i * rows : (i + 1) * rows] = ref[...]
@@ -412,19 +412,29 @@
     out[:, width:] += jnp.sum((v * v).reshape(-1, 8, width), axis=0)
 
 
+def spot_of(ids, planes, distance):
+    count = planes * SIDES
+    spot = jnp.where(ids[1] == 0, ids[0], count - 1 - ids[0]) + distance
+    return jnp.where(spot >= count, spot - count, spot)
+
+
+def order_kernel(planes, distances, ids, *refs):
+    for r, block in zip(distances, refs[:-1], strict=True):
+        refs[-1][spot_of(ids, planes, r)] = block[...]
+
+
 def project_kernel(planes, steps, ids, squares, *refs):
     count = planes * SIDES
-    hidden, refs = refs[: count + 1], refs[count + 1 :]
-    pieces, (raw, sums, grads, held) = refs[:8], refs[8:]
-    tok_dev = hidden[0].shape[0]
+    before, beyond, first, second, refs = *refs[1:5], refs[5:]
+    pieces, (raw, sums, held, grads) = refs[:8], refs[8:]
+    tok_dev = held.shape[1]
     half = tok_dev // 2
     tile = raw.shape[0] // steps
-    mine = jnp.where(ids[1] == 0, ids[0], count - 1 - ids[0])
-    for r, block in enumerate(hidden):
-        spot = mine + (r if r < count else count // 2)
-        spot = jnp.where(spot >= count, spot - count, spot)
-        first = half if r == count else 0
-        held[spot, first : first + block.shape[0]] = block[...]
+    spot = spot_of(ids, planes, count // 2)
+    held[spot, :half] = first[...]
+    held[spot, half:] = second[...]
+    held[spot_of(ids, planes, count // 2 - 1)] = before[...]
+    held[spot_of(ids, planes, count // 2 + 1)] = beyond[...]
     for index, piece in enumerate(pieces):
         side = ids[1] ^ (index & 1)
         group = ids[2] ^ ((index >> 1) & 1)
@@ -590,8 +600,14 @@
         [VMEM] * (planes + 1) + [ANY] * 2,
         tuple(shape((tok_dev, width), bf16 if j else f32) for j in range(SIDES)),
     )(*kv_all, slopes, piece, squares)
-    piece_all = call(join_kernel, [ANY] + [VMEM] * planes, shape(grads_shape, bf16))(
-        q_parts[1], piece, *parts
+    early = tuple(range(count // 2 - 1)) + tuple(range(count // 2 + 2, count))
+    ordered = call(
+        functools.partial(order_kernel, planes, early),
+        [SMEM] + [VMEM] * len(early),
+        pltpu.VMEM((count,) + hidden.shape, bf16),
+    )(ids, *[blocks[r] for r in early])
+    piece_all = call(join_kernel, [ANY] * 2 + [VMEM] * planes, shape(grads_shape, bf16))(
+        q_parts[1], ordered, piece, *parts
     )
     blocks[count - 3], blocks[3] = up, down
     up, down = halves_after(up, down, piece_all)
@@ -606,16 +622,27 @@
     )
 
     steps = 2
-    raw, sums = call(
+    raw, sums, _ = call(
         functools.partial(project_kernel, planes, steps),
-        [SMEM] + [VMEM] * (count + 2 + len(pieces)),
-        (pltpu.VMEM((rows, columns), f32), shape((8, columns), f32)),
+        [SMEM] + [VMEM] * (6 + len(pieces)),
+        (
+            pltpu.VMEM((rows, columns), f32),
+            shape((8, columns), f32),
+            pltpu.VMEM(ordered.shape, bf16),
+        ),
         mib=12,
-        scratch_shapes=[
-            pltpu.VMEM((total, columns), bf16),
-            pltpu.VMEM((count,) + hidden.shape, bf16),
-        ],
-    )(ids, squares, *[blocks[r] for r in range(count + 1)], *pieces)
+        scratch_shapes=[pltpu.VMEM((total, columns), bf16)],
+        input_output_aliases={2: 2},
+    )(
+        ids,
+        squares,
+        pltpu.with_memory_space_constraint(ordered, pltpu.VMEM),
+        blocks[count // 2 - 1],
+        blocks[count // 2 + 1],
+        blocks[count // 2],
+        blocks[count],
+        *pieces,
+    )
     sums_all = [sums, move(sums, member=1), move(sums, group=1), move(sums, group=1, member=1)]
     steps = 8
     key_grad, value_grad = pl.pallas_call(

time: 80.2 us -> 80 us (level)
  waiting for transfers between devices: 34.1 us -> 32.8 us
    ppermute x23, waiting for transfers between devices: 33 us -> 31.8 us  [move(): return lax.ppermute(x, ('ctx', 'fsdp'), pairs)]
  transfers between devices with their start and end apart: 31 -> 31, of which waited for: 14 -> 14; matrix products, arithmetic and copies ran while one was open for 0% -> 0% of each run, Pallas kernels for 11% -> 12%
where the time goes in v6:
time: 80 us; the launch traced here: 79.9 us
  waiting for transfers between devices  32.8 us (41%)
  starting transfers between devices  32.2 us (40%)
  Pallas kernels  13.3 us (17%)
  between operations  0.82 us (1%)
    ppermute x23, waiting for transfers between devices, move(): return lax.ppermute(x, ('ctx', 'fsdp'), pairs)  31.8 us
    ppermute x23, starting transfers between devices, move(): return lax.ppermute(x, ('ctx', 'fsdp'), pairs)  23.9 us
    ppermute x8, starting transfers between devices, around(): return lax.ppermute(x, 'ctx', pairs)  8.26 us
    pallas_call x1, Pallas kernels, local_small(): call(functools.partial(project_kernel, planes, steps), [SMEM] + [VMEM] *...  3.21 us
    pallas_call x1, Pallas kernels, local_small(): pl.pallas_call(functools.partial(scale_kernel, CLIP_RATE * total, steps),...  2.17 us
    pallas_call x1, Pallas kernels, local_small(): call(functools.partial(grads_kernel, planes), [SMEM] * 2 + [VMEM] * (plan...  2.08 us
    pallas_call x1, Pallas kernels, local_small(): call(pack_kernel, [SMEM] + [ANY] * 6, (shape((tok_dev, 2 * DH), bf16), sh...  1.82 us
    pallas_call x1, Pallas kernels, local_small(): call(functools.partial(stats_kernel, planes), [SMEM] * 2 + [VMEM] * (plan...  1.69 us
  transfers between devices with their start and end apart: 31, of which 14 were waited for; matrix products, arithmetic and copies ran while one was open for 0% of the time, Pallas kernels for 12%

profile of v6, /device:TPU:0, one launch (start us, length us, event | category | flops | bytes accessed | tf_op | source)
XLA Modules:
  0.0 79.9 jit_solution(5556712572459949737)
XLA Ops:
  0.8 1.8 %shard_map.112 = (bf16[128,256]{1,0:T(8,128)(2,1)S(1)}, bf16[272,512]{1,0:T(8,128)(2,1)S(1)}, bf16[128,2048]{1,0:T(8,128)(2,1)S(1)}) custom-call(s32[4]{0:T(128)S(1)} %pad_add_fusion.ids, bf16[128,256]{1,0:T(8,128)(2,1)} %keys.1, bf16[128,256]{1,0:T(8,128)(2,1)} %values.1, bf16[128,512]{1,0:T(8,128)(2,1)} %queries.1, bf16[128,512]{1,0:T(8,128)(2,1)} %out_grad.1, ...), custom_call_target="tpu_custom_call" | custom-call | tf_op jit(solution)/shard_map/pallas_call | solution.py:534
  2.6 3.0 %collective-permute-start.3 = (bf16[272,512]{1,0:T(8,128)(2,1)S(1)}, bf16[272,512]{1,0:T(8,128)(2,1)S(1)}, u32[]{:S(2)}, u32[]{:S(2)}) collective-permute-start(bf16[272,512]{1,0:T(8,128)(2,1)S(1)} %get-tuple-element.26.refs_4_), channel_id=1, source_target_pairs={{0,4},{1,5},{2,6},{3,7},{4,0},{5,1},{6,2},{7,3},{8,12},{9,13},{10,... | collective-permute-start | bytes 835592 | tf_op jit(solution)/shard_map/ppermute | solution.py:520
  5.6 3.6 %collective-permute-start.2 = (bf16[128,256]{1,0:T(8,128)(2,1)S(1)}, bf16[128,256]{1,0:T(8,128)(2,1)S(1)}, u32[]{:S(2)}, u32[]{:S(2)}) collective-permute-start(bf16[128,256]{1,0:T(8,128)(2,1)S(1)} %get-tuple-element.25.refs_0_), channel_id=1, source_target_pairs={{0,24},{1,25},{2,26},{3,27},{4,28},{5,29},{6,30},{7,31},{8,16},{9,... | collective-permute-start | bytes 196616 | tf_op jit(solution)/shard_map/ppermute | solution.py:520
  10.0 2.5 %collective-permute-done.2.refs_3_.refs_4_ = bf16[128,256]{1,0:T(8,128)(2,1)S(1)} collective-permute-done((bf16[128,256]{1,0:T(8,128)(2,1)S(1)}, bf16[128,256]{1,0:T(8,128)(2,1)S(1)}, u32[]{:S(2)}, u32[]{:S(2)}) %collective-permute-start.2) | collective-permute-done | bytes 65568 | tf_op jit(solution)/shard_map/ppermute | solution.py:520
  12.5 2.1 %collective-permute-done.1.refs_2_.refs_3_ = bf16[128,256]{1,0:T(8,128)(2,1)S(1)} collective-permute-done((bf16[128,256]{1,0:T(8,128)(2,1)S(1)}, bf16[128,256]{1,0:T(8,128)(2,1)S(1)}, u32[]{:S(2)}, u32[]{:S(2)}) %collective-permute-start.1) | collective-permute-done | bytes 65568 | tf_op jit(solution)/shard_map/ppermute | solution.py:520
  15.1 1.5 %collective-permute-start.10 = (bf16[128,2048]{1,0:T(8,128)(2,1)S(1)}, bf16[128,2048]{1,0:T(8,128)(2,1)S(1)}, u32[]{:S(2)}, u32[]{:S(2)}) collective-permute-start(bf16[128,2048]{1,0:T(8,128)(2,1)S(1)} %shard_map.120.refs_0_), channel_id=1, source_target_pairs={{0,8},{8,16},{16,24},{24,28},{28,20},{20,12},{12,4},{4,0},{1,9},{9... | collective-permute-start | bytes 1572872 | tf_op jit(solution)/shard_map/ppermute | solution.py:526
  17.3 1.7 %shard_map.113.refs_6_ = f32[24,128]{1,0:T(8,128)S(1)} custom-call(s32[4]{0:T(128)S(1)} %pad_add_fusion.ids, s32[8]{0:T(128)S(1)} %copy-done.2, bf16[128,256]{1,0:T(8,128)(2,1)S(1)} %get-tuple-element.25.refs_0_, bf16[128,256]{1,0:T(8,128)(2,1)S(1)} %collective-permute-done.refs_1_.refs_2_, bf16[128,256]{1,0:T(8,128)(2,1)S(1)} %collective-permute-done.1.refs_2_.refs_3_, ...), custom_call_target="tpu_custom_call" | custom-call | tf_op jit(solution)/shard_map/pallas_call | solution.py:568
  19.6 8.9 %collective-permute-done.4.refs_7_.refs_2_ = f32[24,128]{1,0:T(8,128)S(1)} collective-permute-done((f32[24,128]{1,0:T(8,128)S(1)}, f32[24,128]{1,0:T(8,128)S(1)}, u32[]{:S(2)}, u32[]{:S(2)}) %collective-permute-start.4) | collective-permute-done | bytes 12320 | tf_op jit(solution)/shard_map/ppermute | solution.py:520
  28.8 1.7 %collective-permute-start.12 = (bf16[128,2048]{1,0:T(8,128)(2,1)S(1)}, bf16[128,2048]{1,0:T(8,128)(2,1)S(1)}, u32[]{:S(2)}, u32[]{:S(2)}) collective-permute-start(bf16[128,2048]{1,0:T(8,128)(2,1)S(1)} %get-tuple-element.38.refs_4_), channel_id=1, source_target_pairs={{0,8},{8,16},{16,24},{24,28},{28,20},{20,12},{12,4},{4,0},{1,9},{9... | collective-permute-start | bytes 1572872 | tf_op jit(solution)/shard_map/ppermute | solution.py:526
  30.5 2.1 %shard_map.114 = (f32[256,256]{1,0:T(8,128)S(1)}, bf16[256,256]{1,0:T(8,128)(2,1)S(1)}, bf16[2,512,512]{2,1,0:T(8,128)(2,1)S(1)}) custom-call(s32[4]{0:T(128)S(1)} %pad_add_fusion.ids, s32[8]{0:T(128)S(1)} %copy-done.2, bf16[128,256]{1,0:T(8,128)(2,1)S(1)} %get-tuple-element.25.refs_0_, bf16[128,256]{1,0:T(8,128)(2,1)S(1)} %collective-permute-done.refs_1_.refs_2_, ...), custom_call_target="tpu_custom_call" | custom-call | tf_op jit(solution)/shard_map/pallas_call | solution.py:577
  32.7 1.3 %collective-permute-done.5.got = bf16[256,256]{1,0:T(8,128)(2,1)S(1)} collective-permute-done((bf16[256,256]{1,0:T(8,128)(2,1)S(1)}, bf16[256,256]{1,0:T(8,128)(2,1)S(1)}, u32[]{:S(2)}, u32[]{:S(2)}) %collective-permute-start.5) | collective-permute-done | bytes 131104 | tf_op jit(solution)/shard_map/ppermute | solution.py:520
  35.9 2.5 %collective-permute-start.8 = (bf16[64,256]{1,0:T(8,128)(2,1)S(1)}, bf16[64,256]{1,0:T(8,128)(2,1)S(1)}, u32[]{:S(2)}, u32[]{:S(2)}) collective-permute-start(bf16[64,256]{1,0:T(8,128)(2,1)S(1)} %get-tuple-element.33), channel_id=1, source_target_pairs={{0,24},{1,25},{2,26},{3,27},{4,28},{5,29},{6,30},{7,31},{8,16},{9,... | collective-permute-start | bytes 98312 | tf_op jit(solution)/shard_map/ppermute | solution.py:520
  38.5 3.5 %collective-permute-done.6.refs_1_ = bf16[64,256]{1,0:T(8,128)(2,1)S(1)} collective-permute-done((bf16[64,256]{1,0:T(8,128)(2,1)S(1)}, bf16[64,256]{1,0:T(8,128)(2,1)S(1)}, u32[]{:S(2)}, u32[]{:S(2)}) %collective-permute-start.6) | collective-permute-done | bytes 32800 | tf_op jit(solution)/shard_map/ppermute | solution.py:520
  42.0 1.7 %collective-permute-done.7.refs_2_ = bf16[64,256]{1,0:T(8,128)(2,1)S(1)} collective-permute-done((bf16[64,256]{1,0:T(8,128)(2,1)S(1)}, bf16[64,256]{1,0:T(8,128)(2,1)S(1)}, u32[]{:S(2)}, u32[]{:S(2)}) %collective-permute-start.7) | collective-permute-done | bytes 32800 | tf_op jit(solution)/shard_map/ppermute | solution.py:520
  44.4 1.5 %collective-permute-start.15 = (bf16[128,2048]{1,0:T(8,128)(2,1)S(1)}, bf16[128,2048]{1,0:T(8,128)(2,1)S(1)}, u32[]{:S(2)}, u32[]{:S(2)}) collective-permute-start(bf16[128,2048]{1,0:T(8,128)(2,1)S(1)} %get-tuple-element.40.refs_3_), channel_id=1, source_target_pairs={{0,8},{8,16},{16,24},{24,28},{28,20},{20,12},{12,4},{4,0},{1,9},{9... | collective-permute-start | bytes 1572872 | tf_op jit(solution)/shard_map/ppermute | solution.py:526
  45.8 2.7 %collective-permute-start.18 = (bf16[64,256]{1,0:T(8,128)(2,1)S(1)}, bf16[64,256]{1,0:T(8,128)(2,1)S(1)}, u32[]{:S(2)}, u32[]{:S(2)}) collective-permute-start(bf16[64,256]{1,0:T(8,128)(2,1)S(1)} %shard_map.116.refs_5_.refs_2_.refs_0_), channel_id=1, source_target_pairs={{0,24},{1,25},{2,26},{3,27},{4,28},{5,29},{6,30},{7,31},{8,16},{9,... | collective-permute-start | bytes 98312 | tf_op jit(solution)/shard_map/ppermute | solution.py:520
  48.6 1.7 %collective-permute-start.16 = (bf16[64,256]{1,0:T(8,128)(2,1)S(1)}, bf16[64,256]{1,0:T(8,128)(2,1)S(1)}, u32[]{:S(2)}, u32[]{:S(2)}) collective-permute-start(bf16[64,256]{1,0:T(8,128)(2,1)S(1)} %shard_map.116.refs_5_.refs_2_.refs_0_), channel_id=1, source_target_pairs={{0,8},{1,9},{2,10},{3,11},{4,12},{5,13},{6,14},{7,15},{8,0},{9,1},... | collective-permute-start | bytes 98312 | tf_op jit(solution)/shard_map/ppermute | solution.py:520
  51.8 5.0 %collective-permute-done.18.refs_3_ = bf16[64,256]{1,0:T(8,128)(2,1)S(1)} collective-permute-done((bf16[64,256]{1,0:T(8,128)(2,1)S(1)}, bf16[64,256]{1,0:T(8,128)(2,1)S(1)}, u32[]{:S(2)}, u32[]{:S(2)}) %collective-permute-start.18) | collective-permute-done | bytes 32800 | tf_op jit(solution)/shard_map/ppermute | solution.py:520
  58.5 1.5 %collective-permute-start.22 = (bf16[256,256]{1,0:T(8,128)(2,1)S(1)}, bf16[256,256]{1,0:T(8,128)(2,1)S(1)}, u32[]{:S(2)}, u32[]{:S(2)}) collective-permute-start(bf16[256,256]{1,0:T(8,128)(2,1)S(1)} %shard_map.124.refs_2_.refs_5_), channel_id=1, source_target_pairs={{0,2},{1,3},{2,0},{3,1},{4,6},{5,7},{6,4},{7,5},{8,10},{9,11},{10,... | collective-permute-start | bytes 393224 | tf_op jit(solution)/shard_map/ppermute | solution.py:520
  60.1 1.7 %collective-permute-start.20 = (bf16[64,2048]{1,0:T(8,128)(2,1)S(1)}, bf16[64,2048]{1,0:T(8,128)(2,1)S(1)}, u32[]{:S(2)}, u32[]{:S(2)}) collective-permute-start(bf16[64,2048]{1,0:T(8,128)(2,1)S(1)} %get-tuple-element.42), channel_id=1, source_target_pairs={{0,4},{8,0},{16,8},{24,16},{28,24},{20,28},{12,20},{4,12},{1,5},{9... | collective-permute-start | bytes 786440 | tf_op jit(solution)/shard_map/ppermute | solution.py:526
  63.0 1.5 %collective-permute-start.23 = (bf16[256,256]{1,0:T(8,128)(2,1)S(1)}, bf16[256,256]{1,0:T(8,128)(2,1)S(1)}, u32[]{:S(2)}, u32[]{:S(2)}) collective-permute-start(bf16[256,256]{1,0:T(8,128)(2,1)S(1)} %shard_map.126.refs_6_), channel_id=1, source_target_pairs={{0,2},{1,3},{2,0},{3,1},{4,6},{5,7},{6,4},{7,5},{8,10},{9,11},{10,... | collective-permute-start | bytes 393224 | tf_op jit(solution)/shard_map/ppermute | solution.py:520
  65.1 2.9 %collective-permute-done.23.refs_8_ = bf16[256,256]{1,0:T(8,128)(2,1)S(1)} collective-permute-done((bf16[256,256]{1,0:T(8,128)(2,1)S(1)}, bf16[256,256]{1,0:T(8,128)(2,1)S(1)}, u32[]{:S(2)}, u32[]{:S(2)}) %collective-permute-start.23) | collective-permute-done | bytes 131104 | tf_op jit(solution)/shard_map/ppermute | solution.py:520
  70.2 3.2 %shard_map.127 = (f32[2048,512]{1,0:T(8,128)S(1)}, f32[8,512]{1,0:T(8,128)S(1)}, bf16[8,128,2048]{2,1,0:T(8,128)(2,1)S(1)}) custom-call(s32[4]{0:T(128)S(1)} %pad_add_fusion.ids, f32[8,512]{1,0:T(8,128)S(1)} %shard_map.117.refs_6_.squares, bf16[8,128,2048]{2,1,0:T(8,128)(2,1)S(1)} %shard_map.123.other_event.refs_0_, ...), custom_call_target="tpu_custom_call", output_to_operand_aliasing={{2}: (2, {})} | custom-call | tf_op jit(solution)/shard_map/pallas_call | solution.py:625
  77.7 2.2 %shard_map.128 = (f32[2048,256]{1,0:T(8,128)}, f32[2048,256]{1,0:T(8,128)}) custom-call(f32[8,512]{1,0:T(8,128)S(1)} %get-tuple-element.43.sums, f32[8,512]{1,0:T(8,128)S(1)} %collective-permute-done.28.sums_1, f32[8,512]{1,0:T(8,128)S(1)} %collective-permute-done.29.sums_2, f32[8,512]{1,0:T(8,128)S(1)} %collective-permute-done.30.sums_3, ...), custom_call_target="tpu_custom_call" | custom-call | tf_op jit(solution)/shard_map/pallas_call | solution.py:648
  (62 shorter events, 17.2 us)
Async XLA Ops:
  2.6 12.0 %collective-permute-start.3 = (bf16[272,512]{1,0:T(8,128)(2,1)S(1)}, bf16[272,512]{1,0:T(8,128)(2,1)S(1)}, u32[]{:S(2)}, u32[]{:S(2)}) collective-permute-start(bf16[272,512]{1,0:T(8,128)(2,1)S(1)} %get-tuple-element.26.refs_4_), channel_id=1, source_target_pairs={{0,4},{1,5},{2,6},{3,7},{4,0},{5,1},{6,2},{7,3},{8,12},{9,13},{10,... | collective-permute-start | bytes 835592 | tf_op jit(solution)/shard_map/ppermute | solution.py:520
  5.6 6.9 %collective-permute-start.2 = (bf16[128,256]{1,0:T(8,128)(2,1)S(1)}, bf16[128,256]{1,0:T(8,128)(2,1)S(1)}, u32[]{:S(2)}, u32[]{:S(2)}) collective-permute-start(bf16[128,256]{1,0:T(8,128)(2,1)S(1)} %get-tuple-element.25.refs_0_), channel_id=1, source_target_pairs={{0,24},{1,25},{2,26},{3,27},{4,28},{5,29},{6,30},{7,31},{8,16},{9,... | collective-permute-start | bytes 196616 | tf_op jit(solution)/shard_map/ppermute | solution.py:520
  9.2 5.4 %collective-permute-start.1 = (bf16[128,256]{1,0:T(8,128)(2,1)S(1)}, bf16[128,256]{1,0:T(8,128)(2,1)S(1)}, u32[]{:S(2)}, u32[]{:S(2)}) collective-permute-start(bf16[128,256]{1,0:T(8,128)(2,1)S(1)} %get-tuple-element.25.refs_0_), channel_id=1, source_target_pairs={{0,16},{1,17},{2,18},{3,19},{4,20},{5,21},{6,22},{7,23},{8,24},{9,... | collective-permute-start | bytes 196616 | tf_op jit(solution)/shard_map/ppermute | solution.py:520
  9.2 5.4 %collective-permute-start = (bf16[128,256]{1,0:T(8,128)(2,1)S(1)}, bf16[128,256]{1,0:T(8,128)(2,1)S(1)}, u32[]{:S(2)}, u32[]{:S(2)}) collective-permute-start(bf16[128,256]{1,0:T(8,128)(2,1)S(1)} %get-tuple-element.25.refs_0_), channel_id=1, source_target_pairs={{0,8},{1,9},{2,10},{3,11},{4,12},{5,13},{6,14},{7,15},{8,0},{9,1},... | collective-permute-start | bytes 196616 | tf_op jit(solution)/shard_map/ppermute | solution.py:520
  14.6 13.8 %collective-permute-start.11 = (bf16[128,2048]{1,0:T(8,128)(2,1)S(1)}, bf16[128,2048]{1,0:T(8,128)(2,1)S(1)}, u32[]{:S(2)}, u32[]{:S(2)}) collective-permute-start(bf16[128,2048]{1,0:T(8,128)(2,1)S(1)} %shard_map.120.refs_0_), channel_id=1, source_target_pairs={{0,4},{8,0},{16,8},{24,16},{28,24},{20,28},{12,20},{4,12},{1,5},{9... | collective-permute-start | bytes 1572872 | tf_op jit(solution)/shard_map/ppermute | solution.py:526
  15.1 13.3 %collective-permute-start.10 = (bf16[128,2048]{1,0:T(8,128)(2,1)S(1)}, bf16[128,2048]{1,0:T(8,128)(2,1)S(1)}, u32[]{:S(2)}, u32[]{:S(2)}) collective-permute-start(bf16[128,2048]{1,0:T(8,128)(2,1)S(1)} %shard_map.120.refs_0_), channel_id=1, source_target_pairs={{0,8},{8,16},{16,24},{24,28},{28,20},{20,12},{12,4},{4,0},{1,9},{9... | collective-permute-start | bytes 1572872 | tf_op jit(solution)/shard_map/ppermute | solution.py:526
  19.0 9.4 %collective-permute-start.4 = (f32[24,128]{1,0:T(8,128)S(1)}, f32[24,128]{1,0:T(8,128)S(1)}, u32[]{:S(2)}, u32[]{:S(2)}) collective-permute-start(f32[24,128]{1,0:T(8,128)S(1)} %shard_map.113.refs_6_), channel_id=1, source_target_pairs={{0,4},{1,5},{2,6},{3,7},{4,0},{5,1},{6,2},{7,3},{8,12},{9,13},{10,... | collective-permute-start | bytes 36872 | tf_op jit(solution)/shard_map/ppermute | solution.py:520
  28.4 15.3 %collective-permute-start.13 = (bf16[128,2048]{1,0:T(8,128)(2,1)S(1)}, bf16[128,2048]{1,0:T(8,128)(2,1)S(1)}, u32[]{:S(2)}, u32[]{:S(2)}) collective-permute-start(bf16[128,2048]{1,0:T(8,128)(2,1)S(1)} %get-tuple-element.37.refs_1_), channel_id=1, source_target_pairs={{0,4},{8,0},{16,8},{24,16},{28,24},{20,28},{12,20},{4,12},{1,5},{9... | collective-permute-start | bytes 1572872 | tf_op jit(solution)/shard_map/ppermute | solution.py:526
  28.8 15.0 %collective-permute-start.12 = (bf16[128,2048]{1,0:T(8,128)(2,1)S(1)}, bf16[128,2048]{1,0:T(8,128)(2,1)S(1)}, u32[]{:S(2)}, u32[]{:S(2)}) collective-permute-start(bf16[128,2048]{1,0:T(8,128)(2,1)S(1)} %get-tuple-element.38.refs_4_), channel_id=1, source_target_pairs={{0,8},{8,16},{16,24},{24,28},{28,20},{20,12},{12,4},{4,0},{1,9},{9... | collective-permute-start | bytes 1572872 | tf_op jit(solution)/shard_map/ppermute | solution.py:526
  34.0 8.0 %collective-permute-start.6 = (bf16[64,256]{1,0:T(8,128)(2,1)S(1)}, bf16[64,256]{1,0:T(8,128)(2,1)S(1)}, u32[]{:S(2)}, u32[]{:S(2)}) collective-permute-start(bf16[64,256]{1,0:T(8,128)(2,1)S(1)} %get-tuple-element.31), channel_id=1, source_target_pairs={{0,8},{1,9},{2,10},{3,11},{4,12},{5,13},{6,14},{7,15},{8,0},{9,1},... | collective-permute-start | bytes 98312 | tf_op jit(solution)/shard_map/ppermute | solution.py:520
  35.3 8.4 %collective-permute-start.7 = (bf16[64,256]{1,0:T(8,128)(2,1)S(1)}, bf16[64,256]{1,0:T(8,128)(2,1)S(1)}, u32[]{:S(2)}, u32[]{:S(2)}) collective-permute-start(bf16[64,256]{1,0:T(8,128)(2,1)S(1)} %get-tuple-element.32), channel_id=1, source_target_pairs={{0,16},{1,17},{2,18},{3,19},{4,20},{5,21},{6,22},{7,23},{8,24},{9,... | collective-permute-start | bytes 98312 | tf_op jit(solution)/shard_map/ppermute | solution.py:520
  35.9 7.8 %collective-permute-start.8 = (bf16[64,256]{1,0:T(8,128)(2,1)S(1)}, bf16[64,256]{1,0:T(8,128)(2,1)S(1)}, u32[]{:S(2)}, u32[]{:S(2)}) collective-permute-start(bf16[64,256]{1,0:T(8,128)(2,1)S(1)} %get-tuple-element.33), channel_id=1, source_target_pairs={{0,24},{1,25},{2,26},{3,27},{4,28},{5,29},{6,30},{7,31},{8,16},{9,... | collective-permute-start | bytes 98312 | tf_op jit(solution)/shard_map/ppermute | solution.py:520
  43.8 16.3 %collective-permute-start.14 = (bf16[128,2048]{1,0:T(8,128)(2,1)S(1)}, bf16[128,2048]{1,0:T(8,128)(2,1)S(1)}, u32[]{:S(2)}, u32[]{:S(2)}) collective-permute-start(bf16[128,2048]{1,0:T(8,128)(2,1)S(1)} %get-tuple-element.39.refs_2_), channel_id=1, source_target_pairs={{0,4},{8,0},{16,8},{24,16},{28,24},{20,28},{12,20},{4,12},{1,5},{9... | collective-permute-start | bytes 1572872 | tf_op jit(solution)/shard_map/ppermute | solution.py:526
  44.4 15.6 %collective-permute-start.15 = (bf16[128,2048]{1,0:T(8,128)(2,1)S(1)}, bf16[128,2048]{1,0:T(8,128)(2,1)S(1)}, u32[]{:S(2)}, u32[]{:S(2)}) collective-permute-start(bf16[128,2048]{1,0:T(8,128)(2,1)S(1)} %get-tuple-element.40.refs_3_), channel_id=1, source_target_pairs={{0,8},{8,16},{16,24},{24,28},{28,20},{20,12},{12,4},{4,0},{1,9},{9... | collective-permute-start | bytes 1572872 | tf_op jit(solution)/shard_map/ppermute | solution.py:526
  45.8 10.9 %collective-permute-start.18 = (bf16[64,256]{1,0:T(8,128)(2,1)S(1)}, bf16[64,256]{1,0:T(8,128)(2,1)S(1)}, u32[]{:S(2)}, u32[]{:S(2)}) collective-permute-start(bf16[64,256]{1,0:T(8,128)(2,1)S(1)} %shard_map.116.refs_5_.refs_2_.refs_0_), channel_id=1, source_target_pairs={{0,24},{1,25},{2,26},{3,27},{4,28},{5,29},{6,30},{7,31},{8,16},{9,... | collective-permute-start | bytes 98312 | tf_op jit(solution)/shard_map/ppermute | solution.py:520
  48.6 9.4 %collective-permute-start.17 = (bf16[64,256]{1,0:T(8,128)(2,1)S(1)}, bf16[64,256]{1,0:T(8,128)(2,1)S(1)}, u32[]{:S(2)}, u32[]{:S(2)}) collective-permute-start(bf16[64,256]{1,0:T(8,128)(2,1)S(1)} %shard_map.116.refs_5_.refs_2_.refs_0_), channel_id=1, source_target_pairs={{0,16},{1,17},{2,18},{3,19},{4,20},{5,21},{6,22},{7,23},{8,24},{9,... | collective-permute-start | bytes 98312 | tf_op jit(solution)/shard_map/ppermute | solution.py:520
  48.6 9.4 %collective-permute-start.16 = (bf16[64,256]{1,0:T(8,128)(2,1)S(1)}, bf16[64,256]{1,0:T(8,128)(2,1)S(1)}, u32[]{:S(2)}, u32[]{:S(2)}) collective-permute-start(bf16[64,256]{1,0:T(8,128)(2,1)S(1)} %shard_map.116.refs_5_.refs_2_.refs_0_), channel_id=1, source_target_pairs={{0,8},{1,9},{2,10},{3,11},{4,12},{5,13},{6,14},{7,15},{8,0},{9,1},... | collective-permute-start | bytes 98312 | tf_op jit(solution)/shard_map/ppermute | solution.py:520
  58.0 5.0 %collective-permute-start.21 = (bf16[256,256]{1,0:T(8,128)(2,1)S(1)}, bf16[256,256]{1,0:T(8,128)(2,1)S(1)}, u32[]{:S(2)}, u32[]{:S(2)}) collective-permute-start(bf16[256,256]{1,0:T(8,128)(2,1)S(1)} %shard_map.124.refs_2_.refs_5_), channel_id=1, source_target_pairs={{0,4},{1,5},{2,6},{3,7},{4,0},{5,1},{6,2},{7,3},{8,12},{9,13},{10,... | collective-permute-start | bytes 393224 | tf_op jit(solution)/shard_map/ppermute | solution.py:520
  58.5 6.1 %collective-permute-start.22 = (bf16[256,256]{1,0:T(8,128)(2,1)S(1)}, bf16[256,256]{1,0:T(8,128)(2,1)S(1)}, u32[]{:S(2)}, u32[]{:S(2)}) collective-permute-start(bf16[256,256]{1,0:T(8,128)(2,1)S(1)} %shard_map.124.refs_2_.refs_5_), channel_id=1, source_target_pairs={{0,2},{1,3},{2,0},{3,1},{4,6},{5,7},{6,4},{7,5},{8,10},{9,11},{10,... | collective-permute-start | bytes 393224 | tf_op jit(solution)/shard_map/ppermute | solution.py:520
  60.0 4.6 %collective-permute-start.24 = (bf16[256,256]{1,0:T(8,128)(2,1)S(1)}, bf16[256,256]{1,0:T(8,128)(2,1)S(1)}, u32[]{:S(2)}, u32[]{:S(2)}) collective-permute-start(bf16[256,256]{1,0:T(8,128)(2,1)S(1)} %shard_map.124.refs_2_.refs_5_), channel_id=1, source_target_pairs={{0,1},{1,0},{2,3},{3,2},{4,5},{5,4},{6,7},{7,6},{8,9},{9,8},{10,11... | collective-permute-start | bytes 393224 | tf_op jit(solution)/shard_map/ppermute | solution.py:520
  60.1 9.1 %collective-permute-start.20 = (bf16[64,2048]{1,0:T(8,128)(2,1)S(1)}, bf16[64,2048]{1,0:T(8,128)(2,1)S(1)}, u32[]{:S(2)}, u32[]{:S(2)}) collective-permute-start(bf16[64,2048]{1,0:T(8,128)(2,1)S(1)} %get-tuple-element.42), channel_id=1, source_target_pairs={{0,4},{8,0},{16,8},{24,16},{28,24},{20,28},{12,20},{4,12},{1,5},{9... | collective-permute-start | bytes 786440 | tf_op jit(solution)/shard_map/ppermute | solution.py:526
  61.8 8.4 %collective-permute-start.19 = (bf16[64,2048]{1,0:T(8,128)(2,1)S(1)}, bf16[64,2048]{1,0:T(8,128)(2,1)S(1)}, u32[]{:S(2)}, u32[]{:S(2)}) collective-permute-start(bf16[64,2048]{1,0:T(8,128)(2,1)S(1)} %get-tuple-element.41.refs_1_), channel_id=1, source_target_pairs={{0,8},{8,16},{16,24},{24,28},{28,20},{20,12},{12,4},{4,0},{1,9},{9... | collective-permute-start | bytes 786440 | tf_op jit(solution)/shard_map/ppermute | solution.py:526
  63.0 5.0 %collective-permute-start.23 = (bf16[256,256]{1,0:T(8,128)(2,1)S(1)}, bf16[256,256]{1,0:T(8,128)(2,1)S(1)}, u32[]{:S(2)}, u32[]{:S(2)}) collective-permute-start(bf16[256,256]{1,0:T(8,128)(2,1)S(1)} %shard_map.126.refs_6_), channel_id=1, source_target_pairs={{0,2},{1,3},{2,0},{3,1},{4,6},{5,7},{6,4},{7,5},{8,10},{9,11},{10,... | collective-permute-start | bytes 393224 | tf_op jit(solution)/shard_map/ppermute | solution.py:520
  68.0 7.3 %collective-permute-start.9 = (bf16[128,512]{1,0:T(8,128)(2,1)S(1)}, bf16[128,512]{1,0:T(8,128)(2,1)S(1)}, u32[]{:S(2)}, u32[]{:S(2)}) collective-permute-start(bf16[128,512]{1,0:T(8,128)(2,1)S(1)} %get-tuple-element.35.event), channel_id=1, source_target_pairs={{0,4},{1,5},{2,6},{3,7},{4,0},{5,1},{6,2},{7,3},{8,12},{9,13},{10,... | collective-permute-start | bytes 393224 | tf_op jit(solution)/shard_map/ppermute | solution.py:520
  (10 other events, 121.6 us)

commit v7 on v6

--- a/solution.py
+++ b/solution.py
@@ -183,7 +183,7 @@
 
 
 def pack_kernel(
-    ids, keys, values, queries, out_grad, positions, hidden, kv_out, qd_out, held, place, sems
+    ids, keys, values, queries, out_grad, positions, kv_out, qd_out, place, sems
 ):
     tok_dev = queries.shape[0]
     columns = pl.ds(pl.multiple_of(ids[2] * DH, DH), DH)
@@ -196,7 +196,6 @@
                 (values.at[:, columns], kv_out.at[:, DH:]),
                 (queries, qd_out.at[:tok_dev]),
                 (out_grad, qd_out.at[tok_dev : 2 * tok_dev]),
-                (hidden, held),
             )
         )
     ]
@@ -386,6 +385,10 @@
             out[:, head * DH : (head + 1) * DH] = part.astype(out.dtype)
 
 
+def copy_kernel(event, source, out):
+    out[...] = source[...]
+
+
 def join_kernel(event, other_event, *refs):
     rows = refs[0].shape[0]
     for i, ref in enumerate(refs[:-1]):
@@ -529,24 +532,24 @@
 
     far = [
         pltpu.with_memory_space_constraint(x, pltpu.HBM)
-        for x in (keys, values, queries, out_grad, positions.reshape(1, tok_dev), hidden)
+        for x in (keys, values, queries, out_grad, positions.reshape(1, tok_dev))
     ]
-    kv, qd, held = call(
+    kv, qd = call(
         pack_kernel,
-        [SMEM] + [ANY] * 6,
+        [SMEM] + [ANY] * 5,
         (
             shape((tok_dev, 2 * DH), bf16),
             shape((2 * tok_dev + 16, width), bf16),
-            shape(hidden.shape, bf16),
         ),
         scratch_shapes=[
             pltpu.VMEM((1, tok_dev), jnp.int32),
-            pltpu.SemaphoreType.DMA((6,)),
+            pltpu.SemaphoreType.DMA((5,)),
         ],
     )(ids, *far)
     qd_side = move(qd, side=1)
     kv_all = [kv] + [move(kv, plane=j) for j in range(1, planes)]
     qd_all = [qd, qd_side]
+    held = call(copy_kernel, [ANY, VMEM], shape(hidden.shape, bf16))(qd, hidden)
     (held,) = after((held,), qd_side, *kv_all[1:])
     blocks = {0: held}
     up, down = around(held, 1), around(held, -1)

time: 80 us -> 79.8 us (level)
  waiting for transfers between devices: 32.8 us -> 31.7 us
  local copies, waits for them, and re-layouts: 0.66 us -> 1.71 us
    ppermute x23, waiting for transfers between devices: 31.8 us -> 30.6 us  [move(): return lax.ppermute(x, ('ctx', 'fsdp'), pairs)]
    unnamed x6 -> x10, local copies, waits for them, and re-layouts: 0.66 us -> 1.71 us
    pallas_call x1 -> x2, Pallas kernels: 1.82 us -> 1.64 us  [the longest x1 1.61 us: local_small(): call(pack_kernel, [SMEM] + [ANY] * 5, (shape((tok_dev, 2 * DH), bf16), sh...]
where the time goes in v7:
time: 79.8 us; the launch traced here: 79.6 us
  starting transfers between devices  32.2 us (40%)
  waiting for transfers between devices  31.7 us (40%)
  Pallas kernels  13.2 us (17%)
  local copies, waits for them, and re-layouts  1.71 us (2%)
  between operations  0.82 us (1%)
    ppermute x23, waiting for transfers between devices, move(): return lax.ppermute(x, ('ctx', 'fsdp'), pairs)  30.6 us
    ppermute x23, starting transfers between devices, move(): return lax.ppermute(x, ('ctx', 'fsdp'), pairs)  23.9 us
    ppermute x8, starting transfers between devices, around(): return lax.ppermute(x, 'ctx', pairs)  8.26 us
    pallas_call x1, Pallas kernels, local_small(): call(functools.partial(project_kernel, planes, steps), [SMEM] + [VMEM] *...  3.22 us
    pallas_call x1, Pallas kernels, local_small(): pl.pallas_call(functools.partial(scale_kernel, CLIP_RATE * total, steps),...  2.17 us
    pallas_call x1, Pallas kernels, local_small(): call(functools.partial(grads_kernel, planes), [SMEM] * 2 + [VMEM] * (plan...  2.1 us
    pallas_call x1, Pallas kernels, local_small(): call(functools.partial(stats_kernel, planes), [SMEM] * 2 + [VMEM] * (plan...  1.72 us
    unnamed x10, local copies, waits for them, and re-layouts  1.71 us
  transfers between devices with their start and end apart: 31, of which 14 were waited for; matrix products, arithmetic and copies ran while one was open for 0% of the time, Pallas kernels for 12%

profile of v7, /device:TPU:0, one launch (start us, length us, event | category | flops | bytes accessed | tf_op | source)
XLA Modules:
  0.0 79.6 jit_solution(12134042841163392074)
XLA Ops:
  0.8 1.6 %shard_map.112 = (bf16[128,256]{1,0:T(8,128)(2,1)S(1)}, bf16[272,512]{1,0:T(8,128)(2,1)S(1)}) custom-call(s32[4]{0:T(128)S(1)} %pad_add_fusion.ids, bf16[128,256]{1,0:T(8,128)(2,1)} %keys.1, bf16[128,256]{1,0:T(8,128)(2,1)} %values.1, bf16[128,512]{1,0:T(8,128)(2,1)} %queries.1, bf16[128,512]{1,0:T(8,128)(2,1)} %out_grad.1, s32[1,128]{1,0:T(1,128)} %bitcast.5), custom_call_target="tpu_custom_call" | custom-call | tf_op jit(solution)/shard_map/pallas_call | solution.py:537
  2.4 3.0 %collective-permute-start.3 = (bf16[272,512]{1,0:T(8,128)(2,1)S(1)}, bf16[272,512]{1,0:T(8,128)(2,1)S(1)}, u32[]{:S(2)}, u32[]{:S(2)}) collective-permute-start(bf16[272,512]{1,0:T(8,128)(2,1)S(1)} %get-tuple-element.25.refs_4_.event), channel_id=1, source_target_pairs={{0,4},{1,5},{2,6},{3,7},{4,0},{5,1},{6,2},{7,3},{8,12},{9,13},{10,... | collective-permute-start | bytes 835592 | tf_op jit(solution)/shard_map/ppermute | solution.py:523
  5.4 3.6 %collective-permute-start.2 = (bf16[128,256]{1,0:T(8,128)(2,1)S(1)}, bf16[128,256]{1,0:T(8,128)(2,1)S(1)}, u32[]{:S(2)}, u32[]{:S(2)}) collective-permute-start(bf16[128,256]{1,0:T(8,128)(2,1)S(1)} %get-tuple-element.24.refs_0_), channel_id=1, source_target_pairs={{0,24},{1,25},{2,26},{3,27},{4,28},{5,29},{6,30},{7,31},{8,16},{9,... | collective-permute-start | bytes 196616 | tf_op jit(solution)/shard_map/ppermute | solution.py:523
  10.9 1.4 %collective-permute-done.2.refs_3_.refs_4_ = bf16[128,256]{1,0:T(8,128)(2,1)S(1)} collective-permute-done((bf16[128,256]{1,0:T(8,128)(2,1)S(1)}, bf16[128,256]{1,0:T(8,128)(2,1)S(1)}, u32[]{:S(2)}, u32[]{:S(2)}) %collective-permute-start.2) | collective-permute-done | bytes 65568 | tf_op jit(solution)/shard_map/ppermute | solution.py:523
  12.2 2.1 %collective-permute-done.1.refs_2_.refs_3_ = bf16[128,256]{1,0:T(8,128)(2,1)S(1)} collective-permute-done((bf16[128,256]{1,0:T(8,128)(2,1)S(1)}, bf16[128,256]{1,0:T(8,128)(2,1)S(1)}, u32[]{:S(2)}, u32[]{:S(2)}) %collective-permute-start.1) | collective-permute-done | bytes 65568 | tf_op jit(solution)/shard_map/ppermute | solution.py:523
  14.9 1.5 %collective-permute-start.10 = (bf16[128,2048]{1,0:T(8,128)(2,1)S(1)}, bf16[128,2048]{1,0:T(8,128)(2,1)S(1)}, u32[]{:S(2)}, u32[]{:S(2)}) collective-permute-start(bf16[128,2048]{1,0:T(8,128)(2,1)S(1)} %shard_map.121.refs_0_), channel_id=1, source_target_pairs={{0,8},{8,16},{16,24},{24,28},{28,20},{20,12},{12,4},{4,0},{1,9},{9... | collective-permute-start | bytes 1572872 | tf_op jit(solution)/shard_map/ppermute | solution.py:529
  17.1 1.7 %shard_map.113.refs_6_ = f32[24,128]{1,0:T(8,128)S(1)} custom-call(s32[4]{0:T(128)S(1)} %pad_add_fusion.ids, s32[8]{0:T(128)S(1)} %copy-done.3, bf16[128,256]{1,0:T(8,128)(2,1)S(1)} %get-tuple-element.24.refs_0_, bf16[128,256]{1,0:T(8,128)(2,1)S(1)} %collective-permute-done.refs_1_.refs_2_, bf16[128,256]{1,0:T(8,128)(2,1)S(1)} %collective-permute-done.1.refs_2_.refs_3_, ...), custom_call_target="tpu_custom_call" | custom-call | tf_op jit(solution)/shard_map/pallas_call | solution.py:571
  19.4 8.8 %collective-permute-done.4.refs_7_.refs_2_ = f32[24,128]{1,0:T(8,128)S(1)} collective-permute-done((f32[24,128]{1,0:T(8,128)S(1)}, f32[24,128]{1,0:T(8,128)S(1)}, u32[]{:S(2)}, u32[]{:S(2)}) %collective-permute-start.4) | collective-permute-done | bytes 12320 | tf_op jit(solution)/shard_map/ppermute | solution.py:523
  28.5 1.7 %collective-permute-start.12 = (bf16[128,2048]{1,0:T(8,128)(2,1)S(1)}, bf16[128,2048]{1,0:T(8,128)(2,1)S(1)}, u32[]{:S(2)}, u32[]{:S(2)}) collective-permute-start(bf16[128,2048]{1,0:T(8,128)(2,1)S(1)} %get-tuple-element.36.refs_4_), channel_id=1, source_target_pairs={{0,8},{8,16},{16,24},{24,28},{28,20},{20,12},{12,4},{4,0},{1,9},{9... | collective-permute-start | bytes 1572872 | tf_op jit(solution)/shard_map/ppermute | solution.py:529
  30.3 2.1 %shard_map.114 = (f32[256,256]{1,0:T(8,128)S(1)}, bf16[256,256]{1,0:T(8,128)(2,1)S(1)}, bf16[2,512,512]{2,1,0:T(8,128)(2,1)S(1)}) custom-call(s32[4]{0:T(128)S(1)} %pad_add_fusion.ids, s32[8]{0:T(128)S(1)} %copy-done.4, bf16[128,256]{1,0:T(8,128)(2,1)S(1)} %get-tuple-element.24.refs_0_, bf16[128,256]{1,0:T(8,128)(2,1)S(1)} %collective-permute-done.refs_1_.refs_2_, ...), custom_call_target="tpu_custom_call" | custom-call | tf_op jit(solution)/shard_map/pallas_call | solution.py:580
  32.5 1.3 %collective-permute-done.5.got = bf16[256,256]{1,0:T(8,128)(2,1)S(1)} collective-permute-done((bf16[256,256]{1,0:T(8,128)(2,1)S(1)}, bf16[256,256]{1,0:T(8,128)(2,1)S(1)}, u32[]{:S(2)}, u32[]{:S(2)}) %collective-permute-start.5) | collective-permute-done | bytes 131104 | tf_op jit(solution)/shard_map/ppermute | solution.py:523
  35.7 2.5 %collective-permute-start.8 = (bf16[64,256]{1,0:T(8,128)(2,1)S(1)}, bf16[64,256]{1,0:T(8,128)(2,1)S(1)}, u32[]{:S(2)}, u32[]{:S(2)}) collective-permute-start(bf16[64,256]{1,0:T(8,128)(2,1)S(1)} %get-tuple-element.32), channel_id=1, source_target_pairs={{0,24},{1,25},{2,26},{3,27},{4,28},{5,29},{6,30},{7,31},{8,16},{9,... | collective-permute-start | bytes 98312 | tf_op jit(solution)/shard_map/ppermute | solution.py:523
  38.3 3.5 %collective-permute-done.6.refs_1_ = bf16[64,256]{1,0:T(8,128)(2,1)S(1)} collective-permute-done((bf16[64,256]{1,0:T(8,128)(2,1)S(1)}, bf16[64,256]{1,0:T(8,128)(2,1)S(1)}, u32[]{:S(2)}, u32[]{:S(2)}) %collective-permute-start.6) | collective-permute-done | bytes 32800 | tf_op jit(solution)/shard_map/ppermute | solution.py:523
  41.8 1.7 %collective-permute-done.7.refs_2_ = bf16[64,256]{1,0:T(8,128)(2,1)S(1)} collective-permute-done((bf16[64,256]{1,0:T(8,128)(2,1)S(1)}, bf16[64,256]{1,0:T(8,128)(2,1)S(1)}, u32[]{:S(2)}, u32[]{:S(2)}) %collective-permute-start.7) | collective-permute-done | bytes 32800 | tf_op jit(solution)/shard_map/ppermute | solution.py:523
  44.2 1.5 %collective-permute-start.15 = (bf16[128,2048]{1,0:T(8,128)(2,1)S(1)}, bf16[128,2048]{1,0:T(8,128)(2,1)S(1)}, u32[]{:S(2)}, u32[]{:S(2)}) collective-permute-start(bf16[128,2048]{1,0:T(8,128)(2,1)S(1)} %get-tuple-element.38.refs_3_), channel_id=1, source_target_pairs={{0,8},{8,16},{16,24},{24,28},{28,20},{20,12},{12,4},{4,0},{1,9},{9... | collective-permute-start | bytes 1572872 | tf_op jit(solution)/shard_map/ppermute | solution.py:529
  45.6 2.7 %collective-permute-start.18 = (bf16[64,256]{1,0:T(8,128)(2,1)S(1)}, bf16[64,256]{1,0:T(8,128)(2,1)S(1)}, u32[]{:S(2)}, u32[]{:S(2)}) collective-permute-start(bf16[64,256]{1,0:T(8,128)(2,1)S(1)} %shard_map.116.refs_5_.refs_2_.refs_0_), channel_id=1, source_target_pairs={{0,24},{1,25},{2,26},{3,27},{4,28},{5,29},{6,30},{7,31},{8,16},{9,... | collective-permute-start | bytes 98312 | tf_op jit(solution)/shard_map/ppermute | solution.py:523
  48.4 1.7 %collective-permute-start.16 = (bf16[64,256]{1,0:T(8,128)(2,1)S(1)}, bf16[64,256]{1,0:T(8,128)(2,1)S(1)}, u32[]{:S(2)}, u32[]{:S(2)}) collective-permute-start(bf16[64,256]{1,0:T(8,128)(2,1)S(1)} %shard_map.116.refs_5_.refs_2_.refs_0_), channel_id=1, source_target_pairs={{0,8},{1,9},{2,10},{3,11},{4,12},{5,13},{6,14},{7,15},{8,0},{9,1},... | collective-permute-start | bytes 98312 | tf_op jit(solution)/shard_map/ppermute | solution.py:523
  51.5 5.0 %collective-permute-done.18.refs_3_ = bf16[64,256]{1,0:T(8,128)(2,1)S(1)} collective-permute-done((bf16[64,256]{1,0:T(8,128)(2,1)S(1)}, bf16[64,256]{1,0:T(8,128)(2,1)S(1)}, u32[]{:S(2)}, u32[]{:S(2)}) %collective-permute-start.18) | collective-permute-done | bytes 32800 | tf_op jit(solution)/shard_map/ppermute | solution.py:523
  58.3 1.5 %collective-permute-start.22 = (bf16[256,256]{1,0:T(8,128)(2,1)S(1)}, bf16[256,256]{1,0:T(8,128)(2,1)S(1)}, u32[]{:S(2)}, u32[]{:S(2)}) collective-permute-start(bf16[256,256]{1,0:T(8,128)(2,1)S(1)} %shard_map.125.refs_2_.refs_5_), channel_id=1, source_target_pairs={{0,2},{1,3},{2,0},{3,1},{4,6},{5,7},{6,4},{7,5},{8,10},{9,11},{10,... | collective-permute-start | bytes 393224 | tf_op jit(solution)/shard_map/ppermute | solution.py:523
  59.9 1.7 %collective-permute-start.20 = (bf16[64,2048]{1,0:T(8,128)(2,1)S(1)}, bf16[64,2048]{1,0:T(8,128)(2,1)S(1)}, u32[]{:S(2)}, u32[]{:S(2)}) collective-permute-start(bf16[64,2048]{1,0:T(8,128)(2,1)S(1)} %get-tuple-element.40), channel_id=1, source_target_pairs={{0,4},{8,0},{16,8},{24,16},{28,24},{20,28},{12,20},{4,12},{1,5},{9... | collective-permute-start | bytes 786440 | tf_op jit(solution)/shard_map/ppermute | solution.py:529
  62.8 1.5 %collective-permute-start.23 = (bf16[256,256]{1,0:T(8,128)(2,1)S(1)}, bf16[256,256]{1,0:T(8,128)(2,1)S(1)}, u32[]{:S(2)}, u32[]{:S(2)}) collective-permute-start(bf16[256,256]{1,0:T(8,128)(2,1)S(1)} %shard_map.127.refs_6_), channel_id=1, source_target_pairs={{0,2},{1,3},{2,0},{3,1},{4,6},{5,7},{6,4},{7,5},{8,10},{9,11},{10,... | collective-permute-start | bytes 393224 | tf_op jit(solution)/shard_map/ppermute | solution.py:523
  64.9 2.9 %collective-permute-done.23.refs_8_ = bf16[256,256]{1,0:T(8,128)(2,1)S(1)} collective-permute-done((bf16[256,256]{1,0:T(8,128)(2,1)S(1)}, bf16[256,256]{1,0:T(8,128)(2,1)S(1)}, u32[]{:S(2)}, u32[]{:S(2)}) %collective-permute-start.23) | collective-permute-done | bytes 131104 | tf_op jit(solution)/shard_map/ppermute | solution.py:523
  70.0 3.2 %shard_map.128 = (f32[2048,512]{1,0:T(8,128)S(1)}, f32[8,512]{1,0:T(8,128)S(1)}, bf16[8,128,2048]{2,1,0:T(8,128)(2,1)S(1)}) custom-call(s32[4]{0:T(128)S(1)} %pad_add_fusion.ids, f32[8,512]{1,0:T(8,128)S(1)} %shard_map.117.refs_6_.squares, bf16[8,128,2048]{2,1,0:T(8,128)(2,1)S(1)} %shard_map.124.other_event.refs_0_, ...), custom_call_target="tpu_custom_call", output_to_operand_aliasing={{2}: (2, {})} | custom-call | tf_op jit(solution)/shard_map/pallas_call | solution.py:628
  77.5 2.2 %shard_map.129 = (f32[2048,256]{1,0:T(8,128)}, f32[2048,256]{1,0:T(8,128)}) custom-call(f32[8,512]{1,0:T(8,128)S(1)} %get-tuple-element.41.sums, f32[8,512]{1,0:T(8,128)S(1)} %collective-permute-done.28.sums_1, f32[8,512]{1,0:T(8,128)S(1)} %collective-permute-done.29.sums_2, f32[8,512]{1,0:T(8,128)S(1)} %collective-permute-done.30.sums_3, ...), custom_call_target="tpu_custom_call" | custom-call | tf_op jit(solution)/shard_map/pallas_call | solution.py:651
  (67 shorter events, 18.3 us)
Async XLA Ops:
  2.4 12.0 %collective-permute-start.3 = (bf16[272,512]{1,0:T(8,128)(2,1)S(1)}, bf16[272,512]{1,0:T(8,128)(2,1)S(1)}, u32[]{:S(2)}, u32[]{:S(2)}) collective-permute-start(bf16[272,512]{1,0:T(8,128)(2,1)S(1)} %get-tuple-element.25.refs_4_.event), channel_id=1, source_target_pairs={{0,4},{1,5},{2,6},{3,7},{4,0},{5,1},{6,2},{7,3},{8,12},{9,13},{10,... | collective-permute-start | bytes 835592 | tf_op jit(solution)/shard_map/ppermute | solution.py:523
  5.4 6.9 %collective-permute-start.2 = (bf16[128,256]{1,0:T(8,128)(2,1)S(1)}, bf16[128,256]{1,0:T(8,128)(2,1)S(1)}, u32[]{:S(2)}, u32[]{:S(2)}) collective-permute-start(bf16[128,256]{1,0:T(8,128)(2,1)S(1)} %get-tuple-element.24.refs_0_), channel_id=1, source_target_pairs={{0,24},{1,25},{2,26},{3,27},{4,28},{5,29},{6,30},{7,31},{8,16},{9,... | collective-permute-start | bytes 196616 | tf_op jit(solution)/shard_map/ppermute | solution.py:523
  9.0 5.4 %collective-permute-start.1 = (bf16[128,256]{1,0:T(8,128)(2,1)S(1)}, bf16[128,256]{1,0:T(8,128)(2,1)S(1)}, u32[]{:S(2)}, u32[]{:S(2)}) collective-permute-start(bf16[128,256]{1,0:T(8,128)(2,1)S(1)} %get-tuple-element.24.refs_0_), channel_id=1, source_target_pairs={{0,16},{1,17},{2,18},{3,19},{4,20},{5,21},{6,22},{7,23},{8,24},{9,... | collective-permute-start | bytes 196616 | tf_op jit(solution)/shard_map/ppermute | solution.py:523
  9.0 5.4 %collective-permute-start = (bf16[128,256]{1,0:T(8,128)(2,1)S(1)}, bf16[128,256]{1,0:T(8,128)(2,1)S(1)}, u32[]{:S(2)}, u32[]{:S(2)}) collective-permute-start(bf16[128,256]{1,0:T(8,128)(2,1)S(1)} %get-tuple-element.24.refs_0_), channel_id=1, source_target_pairs={{0,8},{1,9},{2,10},{3,11},{4,12},{5,13},{6,14},{7,15},{8,0},{9,1},... | collective-permute-start | bytes 196616 | tf_op jit(solution)/shard_map/ppermute | solution.py:523
  14.4 13.8 %collective-permute-start.11 = (bf16[128,2048]{1,0:T(8,128)(2,1)S(1)}, bf16[128,2048]{1,0:T(8,128)(2,1)S(1)}, u32[]{:S(2)}, u32[]{:S(2)}) collective-permute-start(bf16[128,2048]{1,0:T(8,128)(2,1)S(1)} %shard_map.121.refs_0_), channel_id=1, source_target_pairs={{0,4},{8,0},{16,8},{24,16},{28,24},{20,28},{12,20},{4,12},{1,5},{9... | collective-permute-start | bytes 1572872 | tf_op jit(solution)/shard_map/ppermute | solution.py:529
  14.9 13.3 %collective-permute-start.10 = (bf16[128,2048]{1,0:T(8,128)(2,1)S(1)}, bf16[128,2048]{1,0:T(8,128)(2,1)S(1)}, u32[]{:S(2)}, u32[]{:S(2)}) collective-permute-start(bf16[128,2048]{1,0:T(8,128)(2,1)S(1)} %shard_map.121.refs_0_), channel_id=1, source_target_pairs={{0,8},{8,16},{16,24},{24,28},{28,20},{20,12},{12,4},{4,0},{1,9},{9... | collective-permute-start | bytes 1572872 | tf_op jit(solution)/shard_map/ppermute | solution.py:529
  18.8 9.4 %collective-permute-start.4 = (f32[24,128]{1,0:T(8,128)S(1)}, f32[24,128]{1,0:T(8,128)S(1)}, u32[]{:S(2)}, u32[]{:S(2)}) collective-permute-start(f32[24,128]{1,0:T(8,128)S(1)} %shard_map.113.refs_6_), channel_id=1, source_target_pairs={{0,4},{1,5},{2,6},{3,7},{4,0},{5,1},{6,2},{7,3},{8,12},{9,13},{10,... | collective-permute-start | bytes 36872 | tf_op jit(solution)/shard_map/ppermute | solution.py:523
  28.2 15.3 %collective-permute-start.13 = (bf16[128,2048]{1,0:T(8,128)(2,1)S(1)}, bf16[128,2048]{1,0:T(8,128)(2,1)S(1)}, u32[]{:S(2)}, u32[]{:S(2)}) collective-permute-start(bf16[128,2048]{1,0:T(8,128)(2,1)S(1)} %get-tuple-element.35.refs_1_), channel_id=1, source_target_pairs={{0,4},{8,0},{16,8},{24,16},{28,24},{20,28},{12,20},{4,12},{1,5},{9... | collective-permute-start | bytes 1572872 | tf_op jit(solution)/shard_map/ppermute | solution.py:529
  28.5 15.0 %collective-permute-start.12 = (bf16[128,2048]{1,0:T(8,128)(2,1)S(1)}, bf16[128,2048]{1,0:T(8,128)(2,1)S(1)}, u32[]{:S(2)}, u32[]{:S(2)}) collective-permute-start(bf16[128,2048]{1,0:T(8,128)(2,1)S(1)} %get-tuple-element.36.refs_4_), channel_id=1, source_target_pairs={{0,8},{8,16},{16,24},{24,28},{28,20},{20,12},{12,4},{4,0},{1,9},{9... | collective-permute-start | bytes 1572872 | tf_op jit(solution)/shard_map/ppermute | solution.py:529
  33.8 7.9 %collective-permute-start.6 = (bf16[64,256]{1,0:T(8,128)(2,1)S(1)}, bf16[64,256]{1,0:T(8,128)(2,1)S(1)}, u32[]{:S(2)}, u32[]{:S(2)}) collective-permute-start(bf16[64,256]{1,0:T(8,128)(2,1)S(1)} %get-tuple-element.30), channel_id=1, source_target_pairs={{0,8},{1,9},{2,10},{3,11},{4,12},{5,13},{6,14},{7,15},{8,0},{9,1},... | collective-permute-start | bytes 98312 | tf_op jit(solution)/shard_map/ppermute | solution.py:523
  35.1 8.4 %collective-permute-start.7 = (bf16[64,256]{1,0:T(8,128)(2,1)S(1)}, bf16[64,256]{1,0:T(8,128)(2,1)S(1)}, u32[]{:S(2)}, u32[]{:S(2)}) collective-permute-start(bf16[64,256]{1,0:T(8,128)(2,1)S(1)} %get-tuple-element.31), channel_id=1, source_target_pairs={{0,16},{1,17},{2,18},{3,19},{4,20},{5,21},{6,22},{7,23},{8,24},{9,... | collective-permute-start | bytes 98312 | tf_op jit(solution)/shard_map/ppermute | solution.py:523
  35.7 7.8 %collective-permute-start.8 = (bf16[64,256]{1,0:T(8,128)(2,1)S(1)}, bf16[64,256]{1,0:T(8,128)(2,1)S(1)}, u32[]{:S(2)}, u32[]{:S(2)}) collective-permute-start(bf16[64,256]{1,0:T(8,128)(2,1)S(1)} %get-tuple-element.32), channel_id=1, source_target_pairs={{0,24},{1,25},{2,26},{3,27},{4,28},{5,29},{6,30},{7,31},{8,16},{9,... | collective-permute-start | bytes 98312 | tf_op jit(solution)/shard_map/ppermute | solution.py:523
  43.6 16.3 %collective-permute-start.14 = (bf16[128,2048]{1,0:T(8,128)(2,1)S(1)}, bf16[128,2048]{1,0:T(8,128)(2,1)S(1)}, u32[]{:S(2)}, u32[]{:S(2)}) collective-permute-start(bf16[128,2048]{1,0:T(8,128)(2,1)S(1)} %get-tuple-element.37.refs_2_), channel_id=1, source_target_pairs={{0,4},{8,0},{16,8},{24,16},{28,24},{20,28},{12,20},{4,12},{1,5},{9... | collective-permute-start | bytes 1572872 | tf_op jit(solution)/shard_map/ppermute | solution.py:529
  44.2 15.6 %collective-permute-start.15 = (bf16[128,2048]{1,0:T(8,128)(2,1)S(1)}, bf16[128,2048]{1,0:T(8,128)(2,1)S(1)}, u32[]{:S(2)}, u32[]{:S(2)}) collective-permute-start(bf16[128,2048]{1,0:T(8,128)(2,1)S(1)} %get-tuple-element.38.refs_3_), channel_id=1, source_target_pairs={{0,8},{8,16},{16,24},{24,28},{28,20},{20,12},{12,4},{4,0},{1,9},{9... | collective-permute-start | bytes 1572872 | tf_op jit(solution)/shard_map/ppermute | solution.py:529
  45.6 10.9 %collective-permute-start.18 = (bf16[64,256]{1,0:T(8,128)(2,1)S(1)}, bf16[64,256]{1,0:T(8,128)(2,1)S(1)}, u32[]{:S(2)}, u32[]{:S(2)}) collective-permute-start(bf16[64,256]{1,0:T(8,128)(2,1)S(1)} %shard_map.116.refs_5_.refs_2_.refs_0_), channel_id=1, source_target_pairs={{0,24},{1,25},{2,26},{3,27},{4,28},{5,29},{6,30},{7,31},{8,16},{9,... | collective-permute-start | bytes 98312 | tf_op jit(solution)/shard_map/ppermute | solution.py:523
  48.4 9.4 %collective-permute-start.17 = (bf16[64,256]{1,0:T(8,128)(2,1)S(1)}, bf16[64,256]{1,0:T(8,128)(2,1)S(1)}, u32[]{:S(2)}, u32[]{:S(2)}) collective-permute-start(bf16[64,256]{1,0:T(8,128)(2,1)S(1)} %shard_map.116.refs_5_.refs_2_.refs_0_), channel_id=1, source_target_pairs={{0,16},{1,17},{2,18},{3,19},{4,20},{5,21},{6,22},{7,23},{8,24},{9,... | collective-permute-start | bytes 98312 | tf_op jit(solution)/shard_map/ppermute | solution.py:523
  48.4 9.4 %collective-permute-start.16 = (bf16[64,256]{1,0:T(8,128)(2,1)S(1)}, bf16[64,256]{1,0:T(8,128)(2,1)S(1)}, u32[]{:S(2)}, u32[]{:S(2)}) collective-permute-start(bf16[64,256]{1,0:T(8,128)(2,1)S(1)} %shard_map.116.refs_5_.refs_2_.refs_0_), channel_id=1, source_target_pairs={{0,8},{1,9},{2,10},{3,11},{4,12},{5,13},{6,14},{7,15},{8,0},{9,1},... | collective-permute-start | bytes 98312 | tf_op jit(solution)/shard_map/ppermute | solution.py:523
  57.8 5.0 %collective-permute-start.21 = (bf16[256,256]{1,0:T(8,128)(2,1)S(1)}, bf16[256,256]{1,0:T(8,128)(2,1)S(1)}, u32[]{:S(2)}, u32[]{:S(2)}) collective-permute-start(bf16[256,256]{1,0:T(8,128)(2,1)S(1)} %shard_map.125.refs_2_.refs_5_), channel_id=1, source_target_pairs={{0,4},{1,5},{2,6},{3,7},{4,0},{5,1},{6,2},{7,3},{8,12},{9,13},{10,... | collective-permute-start | bytes 393224 | tf_op jit(solution)/shard_map/ppermute | solution.py:523
  58.3 6.1 %collective-permute-start.22 = (bf16[256,256]{1,0:T(8,128)(2,1)S(1)}, bf16[256,256]{1,0:T(8,128)(2,1)S(1)}, u32[]{:S(2)}, u32[]{:S(2)}) collective-permute-start(bf16[256,256]{1,0:T(8,128)(2,1)S(1)} %shard_map.125.refs_2_.refs_5_), channel_id=1, source_target_pairs={{0,2},{1,3},{2,0},{3,1},{4,6},{5,7},{6,4},{7,5},{8,10},{9,11},{10,... | collective-permute-start | bytes 393224 | tf_op jit(solution)/shard_map/ppermute | solution.py:523
  59.9 9.0 %collective-permute-start.20 = (bf16[64,2048]{1,0:T(8,128)(2,1)S(1)}, bf16[64,2048]{1,0:T(8,128)(2,1)S(1)}, u32[]{:S(2)}, u32[]{:S(2)}) collective-permute-start(bf16[64,2048]{1,0:T(8,128)(2,1)S(1)} %get-tuple-element.40), channel_id=1, source_target_pairs={{0,4},{8,0},{16,8},{24,16},{28,24},{20,28},{12,20},{4,12},{1,5},{9... | collective-permute-start | bytes 786440 | tf_op jit(solution)/shard_map/ppermute | solution.py:529
  61.5 8.4 %collective-permute-start.19 = (bf16[64,2048]{1,0:T(8,128)(2,1)S(1)}, bf16[64,2048]{1,0:T(8,128)(2,1)S(1)}, u32[]{:S(2)}, u32[]{:S(2)}) collective-permute-start(bf16[64,2048]{1,0:T(8,128)(2,1)S(1)} %get-tuple-element.39.refs_1_), channel_id=1, source_target_pairs={{0,8},{8,16},{16,24},{24,28},{28,20},{20,12},{12,4},{4,0},{1,9},{9... | collective-permute-start | bytes 786440 | tf_op jit(solution)/shard_map/ppermute | solution.py:529
  62.8 5.0 %collective-permute-start.23 = (bf16[256,256]{1,0:T(8,128)(2,1)S(1)}, bf16[256,256]{1,0:T(8,128)(2,1)S(1)}, u32[]{:S(2)}, u32[]{:S(2)}) collective-permute-start(bf16[256,256]{1,0:T(8,128)(2,1)S(1)} %shard_map.127.refs_6_), channel_id=1, source_target_pairs={{0,2},{1,3},{2,0},{3,1},{4,6},{5,7},{6,4},{7,5},{8,10},{9,11},{10,... | collective-permute-start | bytes 393224 | tf_op jit(solution)/shard_map/ppermute | solution.py:523
  64.4 4.6 %collective-permute-start.25 = (bf16[256,256]{1,0:T(8,128)(2,1)S(1)}, bf16[256,256]{1,0:T(8,128)(2,1)S(1)}, u32[]{:S(2)}, u32[]{:S(2)}) collective-permute-start(bf16[256,256]{1,0:T(8,128)(2,1)S(1)} %shard_map.127.refs_6_), channel_id=1, source_target_pairs={{0,1},{1,0},{2,3},{3,2},{4,5},{5,4},{6,7},{7,6},{8,9},{9,8},{10,11... | collective-permute-start | bytes 393224 | tf_op jit(solution)/shard_map/ppermute | solution.py:523
  67.8 7.3 %collective-permute-start.9 = (bf16[128,512]{1,0:T(8,128)(2,1)S(1)}, bf16[128,512]{1,0:T(8,128)(2,1)S(1)}, u32[]{:S(2)}, u32[]{:S(2)}) collective-permute-start(bf16[128,512]{1,0:T(8,128)(2,1)S(1)} %get-tuple-element.34.event), channel_id=1, source_target_pairs={{0,4},{1,5},{2,6},{3,7},{4,0},{5,1},{6,2},{7,3},{8,12},{9,13},{10,... | collective-permute-start | bytes 393224 | tf_op jit(solution)/shard_map/ppermute | solution.py:523
  (12 other events, 141.7 us)
